TPU v7x, 512 devices: a whole 4x8x8 slice. The times are simulated.
512 devices in a mesh: row: 4 (over z_lo), col: 16 (over z_hi, x, core), par: 8 (over y).
Axes of the slice: x: 4, y: 8, z: 8 (z_hi: 2, z_lo: 4; z = z_hi * 4 + z_lo), core: 2. Of those that a mesh axis runs over, the one named last changes fastest.
Arguments:
- log_derivs: float32 [8192, 4096], P(('row', 'col'), 'par'), may hold values from -0.09375 to 0.09375
- sample_vector: float32 [8192], P(('row', 'col')), may hold values from -6 to 6
Outputs:
- gram_tiles: float32 [2048, 4, 8192], P(('col', 'par'), None, 'row')
- projected: float32 [4096], P('par')
All inputs are finite; a program needn't handle non-finite values.
Results may differ from a plain program's by a relative error of at most 0.0001.
Values sent between devices are 32-bit elements; how exact they have to be, the bound alone decides.
No kernel may reach another device: no remote copies, remote signals or barrier semaphores. Data moves between devices by JAX's collectives and lax.ppermute only.
A program may use at most 64 MiB of HBM per device.

v0:
```python
import jax
import jax.numpy as jnp
from jax import lax
from jax.sharding import PartitionSpec as P


def body(log_derivs, sample_vector):
    local = log_derivs.shape[0]
    params = log_derivs.shape[1]
    row_count = lax.axis_size("row")
    gathered = lax.all_gather(log_derivs, "row", axis=0, tiled=True)
    col_side = gathered.reshape(row_count, local, params)
    row_side = lax.all_gather(log_derivs, "col", axis=0, tiled=True)
    partial_value = jnp.dot(
        sample_vector,
        log_derivs,
        precision=lax.Precision.HIGHEST,
        preferred_element_type=jnp.float32,
    )
    projected = lax.psum(partial_value, ("row", "col"))
    share = local // lax.axis_size("par")
    summed = lax.psum(
        jnp.einsum(
            "aip,sp->ias",
            col_side,
            row_side,
            precision=lax.Precision.HIGHEST,
            preferred_element_type=jnp.float32,
        ),
        "par",
    )
    gram_tiles = lax.dynamic_slice_in_dim(summed, lax.axis_index("par") * share, share, 0)
    return (gram_tiles, projected)


def solution(mesh):
    in_specs = (P(("row", "col"), "par"), P(("row", "col")))
    out_specs = (P(("col", "par"), None, "row"), P("par"))
    return jax.shard_map(body, mesh=mesh, in_specs=in_specs, out_specs=out_specs, check_vma=False)
```

profile of v0, /device:TPU:7, one launch (start us, length us, event | category | flops | bytes accessed | tf_op | source)
XLA Modules:
  0.0 330.7 jit_solution(4911320246977652936)
XLA Ops:
  7.2 0.0 copy-start
  7.2 0.0 all-gather.5.cloned.1.call-start
  7.2 0.7 all-gather.5.cloned.1.call-update
  7.9 0.0 all-gather.3.cloned.1.call-start
  8.0 0.7 all-gather.3.cloned.1.call-update
  8.7 0.0 all-reduce.2.cloned.1.call-start
  8.7 42.4 %all-gather.5.cloned.1.call-done = f32[512,512]{1,0:T(8,128)} async-done(((f32[128,512]{1,0:T(8,128)}), f32[512,512]{1,0:T(8,128)}) %all-gather.5.cloned.1.call-update) | async-done | bytes 1048592 | tf_op jit(solution)/shard_map/all_gather | solution.py:11
  51.1 85.7 %all-gather.3.cloned.1.call-done = f32[2048,512]{1,0:T(8,128)} async-done(((f32[128,512]{1,0:T(8,128)}), f32[2048,512]{1,0:T(8,128)}) %all-gather.3.cloned.1.call-update) | async-done | bytes 4194320 | tf_op jit(solution)/shard_map/all_gather | solution.py:13
  136.9 10.1 %fusion.2 = f32[128,4,2048]{0,2,1:T(8,128)} fusion(f32[4,128,512]{2,1,0:T(8,128)} %bitcast.14, f32[2048,512]{1,0:T(8,128)} %all-gather.3.cloned.1.call-done), kind=kOutput, calls=%fused_computation.2 | convolution fusion | flops 6442450944 | bytes 9437184 | tf_op jit(solution)/shard_map/aip,sp->ias/dot_general | solution.py:23
  146.9 0.0 copy-start.1
  147.0 0.0 all-reduce.2.cloned.1.call-update
  147.0 0.0 copy-done
  147.0 0.9 copy-done.1
  147.9 0.2 fusion.5
  148.1 167.2 %psum.15 = f32[512]{0:T(512)} all-reduce(f32[512]{0:T(512)S(1)} %bitcast.15), channel_id=1, replica_groups=mesh['row'=4,'col'=16,'par'=8] {'row','col'}, use_global_device_ids=true, to_apply=%region_1.0 | all-reduce | flops 512 | bytes 4096 | tf_op jit(solution)/shard_map/psum | solution.py:20
  315.4 0.0 all-reduce.2.cloned.1.call-done
  315.4 5.3 %constant_dynamic-slice_fusion = f32[16,4,2048]{0,2,1:T(8,128)} fusion(f32[128,4,2048]{0,2,1:T(8,128)} %all-reduce.2.cloned.1.call-done, s32[]{:T(128)S(6)} %select_n.3), kind=kLoop, calls=%fused_computation.5 | loop fusion | bytes 1048580 | tf_op jit(solution)/shard_map/dynamic_slice | solution.py:32
  320.6 3.5 %copy.4 = f32[16,4,2048]{2,1,0:T(4,128)} copy(f32[16,4,2048]{0,2,1:T(8,128)} %constant_dynamic-slice_fusion) | data formatting | bytes 1048576
Async XLA Ops:
  7.2 139.8 %copy-start = (f32[128]{0:T(128)S(1)}, f32[128]{0:T(128)}, u32[]{:S(2)}) copy-start(f32[128]{0:T(128)} %param.3) | copy-start | bytes 1540
  7.2 43.9 %all-gather.5.cloned.1.call-start = ((), (), s32[]{:S(2)}) async-start(), calls=%async_computation.1 | async-start | bytes 1310720 | tf_op jit(solution)/shard_map/all_gather | solution.py:11
  7.9 128.9 %all-gather.3.cloned.1.call-start = ((), (), s32[]{:S(2)}) async-start(), calls=%async_computation | async-start | bytes 4456448 | tf_op jit(solution)/shard_map/all_gather | solution.py:13
  8.7 306.7 %all-reduce.2.cloned.1.call-start = ((), (), s32[]{:S(2)}) async-start(), calls=%async_computation.2 | async-start | bytes 8388608 | tf_op jit(solution)/shard_map/psum | solution.py:22
  146.9 0.9 copy-start.1
Sparse Core Ops, SparseCore 0:
  10.1 40.9 all-gather.4
  54.4 82.3 all-gather.2
  147.1 109.6 all-reduce.1
where the time goes:
time: 331 us
  blocking collectives  167 us (50%)
  waiting for transfers between devices  130 us (39%)
  between operations  13.8 us (4%)
  matrix products  10.3 us (3%)
  local copies, waits for them, and re-layouts  9.73 us (3%)
    psum x1, blocking collectives, body(): projected = lax.psum(partial_value, ('row', 'col'))  167 us
    all_gather x1, waiting for transfers between devices, body(): row_side = lax.all_gather(log_derivs, 'col', axis=0, tiled=True)  85.7 us
    all_gather x1, waiting for transfers between devices, body(): gathered = lax.all_gather(log_derivs, 'row', axis=0, tiled=True)  42.4 us
    dot_general x1, matrix products, body(): jnp.einsum('aip,sp->ias', col_side, row_side, precision=lax.Precision.HIG...  10.1 us
  transfers between devices with their start and end apart: 3, of which 2 were waited for; matrix products, arithmetic and copies ran while one was open for 0% of the time, Pallas kernels for 0%

commit v1 on v0

v1 whole, which is shorter than its diff:
```python
import jax
import jax.numpy as jnp
from jax import lax
from jax.experimental import pallas as pl
from jax.experimental.pallas import tpu as pltpu
from jax.sharding import Mesh, PartitionSpec as P

AXES = ("zl", "zh", "x", "core", "par")
SIZES = (4, 2, 4, 2, 8)
SAMPLES = AXES[:4]
LANES = 128


def shift(value, axis, by):
    count = lax.axis_size(axis)
    return lax.ppermute(value, axis, [(i, (i + by) % count) for i in range(count)])


def halves(value):
    high = value.astype(jnp.bfloat16)
    low = (value - high.astype(jnp.float32)).astype(jnp.bfloat16)
    return high, low


def product_kernel(place, left_ref, mine_ref, other_ref, *rest):
    out_ref, left, high, low, right = rest[-5:]
    local = mine_ref.shape[1]
    blocks = left_ref.shape[0]

    @pl.when(pl.program_id(0) == 0)
    def _():
        for g in range(left_ref.shape[2] // LANES):
            lanes = pl.ds(g * LANES, LANES)
            for a in range(blocks):
                left[g, pl.ds(a, local, stride=blocks), :] = left_ref[a, :, lanes]
            high[:, lanes], low[:, lanes] = halves(left[g])

    core = place[2]
    right[pl.ds(pl.multiple_of(core * local, local), local), :] = mine_ref[0]
    right[pl.ds(pl.multiple_of((1 - core) * local, local), local), :] = other_ref[0]
    right_high, right_low = halves(right[...])

    def dot(a, b):
        return lax.dot_general(
            a, b, (((1,), (1,)), ((), ())), preferred_element_type=jnp.float32
        )

    value = dot(high[...], right_low) + dot(low[...], right_high) + dot(high[...], right_high)
    out_ref[...] = value


def product(place, left, mine, other, total):
    blocks, local, params = left.shape
    return pl.pallas_call(
        product_kernel,
        grid_spec=pltpu.PrefetchScalarGridSpec(
            num_scalar_prefetch=1,
            grid=(2,),
            in_specs=[
                pl.BlockSpec((blocks, local, params), lambda j, place: (0, 0, 0)),
                pl.BlockSpec((1, local, params), lambda j, place: (j, 0, 0)),
                pl.BlockSpec((1, local, params), lambda j, place: (j, 0, 0)),
            ]
            + [pl.BlockSpec(memory_space=pl.ANY)] * len(total),
            out_specs=pl.BlockSpec(
                (blocks * local, 2 * local), lambda j, place: (0, place[j])
            ),
            scratch_shapes=[
                pltpu.VMEM((params // LANES, blocks * local, LANES), jnp.float32),
                pltpu.VMEM((blocks * local, params), jnp.bfloat16),
                pltpu.VMEM((blocks * local, params), jnp.bfloat16),
                pltpu.VMEM((2 * local, params), jnp.float32),
            ],
        ),
        out_shape=jax.ShapeDtypeStruct((blocks * local, 16 * local), jnp.float32),
        input_output_aliases={4: 0} if total else {},
        compiler_params=pltpu.CompilerParams(vmem_limit_bytes=24 * 1024 * 1024),
        cost_estimate=pl.CostEstimate(
            flops=2 * 3 * blocks * local * 4 * local * params,
            bytes_accessed=4 * (blocks * local * params + 4 * local * params + blocks * local * 4 * local),
            transcendentals=0,
        ),
    )(place, left, mine, other, *total)


def body(log_derivs, sample_vector):
    local, params = log_derivs.shape
    zh, x, core = (lax.axis_index(name) for name in ("zh", "x", "core"))
    x_count = lax.axis_size("x")
    left = lax.all_gather(log_derivs, "zl")
    partial_value = jnp.dot(
        sample_vector, log_derivs, precision=lax.Precision.HIGHEST, preferred_element_type=jnp.float32
    )
    projected = jnp.sum(lax.all_gather(partial_value, SAMPLES), axis=0)

    far = shift(log_derivs, "zh", 1)
    pair = jnp.stack([log_derivs, far])
    mine = [pair] + [shift(pair, "x", by) for by in (1, 3, 2)]
    other = [shift(value, "core", 1) for value in mine]

    total = ()
    for by, m, o in zip((0, 1, 3, 2), mine, other):
        source = lax.rem(x + x_count - by, x_count)
        place = jnp.stack([zh * x_count + source, (1 - zh) * x_count + source, core]).astype(jnp.int32)
        total = (product(place, left, m, o, total),)
    summed = lax.psum_scatter(total[0], "par", scatter_dimension=0, tiled=True)
    gram_tiles = summed.reshape(-1, left.shape[0], summed.shape[1])
    return (gram_tiles, projected)


def solution(mesh):
    split = Mesh(mesh.devices.reshape(SIZES), AXES)
    in_specs = (P(SAMPLES, "par"), P(SAMPLES))
    out_specs = (P(("zh", "x", "core", "par"), None, "zl"), P("par"))
    return jax.shard_map(body, mesh=split, in_specs=in_specs, out_specs=out_specs, check_vma=False)
```

time: 331 us -> 183 us (0.55)
  the two profiles are of different devices: /device:TPU:7 before, /device:TPU:417 now
where the time goes in v1:
time: 183 us
  blocking collectives  94.8 us (52%)
  starting transfers between devices  32.8 us (18%)
  waiting for transfers between devices  21.2 us (12%)
  between operations  14.2 us (8%)
  Pallas kernels  11.3 us (6%)
  local copies, waits for them, and re-layouts  6.07 us (3%)
  other arithmetic  2.01 us (1%)
    all_gather x1, blocking collectives, body(): projected = jnp.sum(lax.all_gather(partial_value, SAMPLES), axis=0)  94.8 us
    ppermute x8, starting transfers between devices, shift(): lax.ppermute(value, axis, [(i, (i + by) % count) for i in range(count)])  32.7 us
    ppermute x8, waiting for transfers between devices, shift(): lax.ppermute(value, axis, [(i, (i + by) % count) for i in range(count)])  20.5 us
    pallas_call x4, Pallas kernels, product(): pl.pallas_call(product_kernel, grid_spec=pltpu.PrefetchScalarGridSpec(num...  11.3 us
    unnamed x8, local copies, waits for them, and re-layouts  4.09 us
  transfers between devices with their start and end apart: 10, of which 2 were waited for; matrix products, arithmetic and copies ran while one was open for 1% of the time, Pallas kernels for 4%

profile of v1, /device:TPU:417, one launch (start us, length us, event | category | flops | bytes accessed | tf_op | source)
XLA Modules:
  0.0 182.6 jit_solution(10215966842822907622)
XLA Ops:
  7.2 0.0 copy-start
  7.2 0.0 all-gather.5.cloned.1.call-start
  7.2 0.7 all-gather.5.cloned.1.call-update
  7.9 0.0 reduce-scatter.2.cloned.1.call-start
  8.0 1.9 %collective-permute-start = (f32[128,512]{1,0:T(8,128)}, f32[128,512]{1,0:T(8,128)S(1)}, u32[]{:S(2)}, u32[]{:S(2)}) collective-permute-start(f32[128,512]{1,0:T(8,128)} %param.2), channel_id=1, source_target_pairs={{0,64},{64,0},{1,65},{65,1},{2,66},{66,2},{3,67},{67,3},{4,68},{68... | collective-permute-start | bytes 786440 | tf_op jit(solution)/shard_map/ppermute | solution.py:16
  9.9 17.7 %collective-permute-done = f32[128,512]{1,0:T(8,128)S(1)} collective-permute-done((f32[128,512]{1,0:T(8,128)}, f32[128,512]{1,0:T(8,128)S(1)}, u32[]{:S(2)}, u32[]{:S(2)}) %collective-permute-start) | collective-permute-done | bytes 262176 | tf_op jit(solution)/shard_map/ppermute | solution.py:16
  27.5 1.0 pad_maximum_fusion.mine_ref
  28.6 3.1 %collective-permute-start.5 = (f32[2,128,512]{2,1,0:T(8,128)S(1)}, f32[2,128,512]{2,1,0:T(8,128)S(1)}, u32[]{:S(2)}, u32[]{:S(2)}) collective-permute-start(f32[2,128,512]{2,1,0:T(8,128)S(1)} %pad_maximum_fusion.mine_ref), channel_id=1, source_target_pairs={{0,16},{16,32},{32,48},{48,0},{1,17},{17,33},{33,49},{49,1},{2,18}... | collective-permute-start | bytes 1572872 | tf_op jit(solution)/shard_map/ppermute | solution.py:16
  31.7 3.4 %collective-permute-start.3 = (f32[2,128,512]{2,1,0:T(8,128)S(1)}, f32[2,128,512]{2,1,0:T(8,128)S(1)}, u32[]{:S(2)}, u32[]{:S(2)}) collective-permute-start(f32[2,128,512]{2,1,0:T(8,128)S(1)} %pad_maximum_fusion.mine_ref), channel_id=1, source_target_pairs={{0,48},{16,0},{32,16},{48,32},{1,49},{17,1},{33,17},{49,33},{2,50}... | collective-permute-start | bytes 1572872 | tf_op jit(solution)/shard_map/ppermute | solution.py:16
  35.1 3.4 %collective-permute-start.1 = (f32[2,128,512]{2,1,0:T(8,128)S(1)}, f32[2,128,512]{2,1,0:T(8,128)S(1)}, u32[]{:S(2)}, u32[]{:S(2)}) collective-permute-start(f32[2,128,512]{2,1,0:T(8,128)S(1)} %pad_maximum_fusion.mine_ref), channel_id=1, source_target_pairs={{0,32},{16,48},{32,0},{48,16},{1,33},{17,49},{33,1},{49,17},{2,34}... | collective-permute-start | bytes 1572872 | tf_op jit(solution)/shard_map/ppermute | solution.py:16
  38.5 3.3 %collective-permute-start.7 = (f32[2,128,512]{2,1,0:T(8,128)S(1)}, f32[2,128,512]{2,1,0:T(8,128)S(1)}, u32[]{:S(2)}, u32[]{:S(2)}) collective-permute-start(f32[2,128,512]{2,1,0:T(8,128)S(1)} %pad_maximum_fusion.mine_ref), channel_id=1, source_target_pairs={{0,8},{8,0},{1,9},{9,1},{2,10},{10,2},{3,11},{11,3},{4,12},{12,4},... | collective-permute-start | bytes 1572872 | tf_op jit(solution)/shard_map/ppermute | solution.py:16
  41.8 2.8 %collective-permute-done.5.mine_ref = f32[2,128,512]{2,1,0:T(8,128)S(1)} collective-permute-done((f32[2,128,512]{2,1,0:T(8,128)S(1)}, f32[2,128,512]{2,1,0:T(8,128)S(1)}, u32[]{:S(2)}, u32[]{:S(2)}) %collective-permute-start.5) | collective-permute-done | bytes 524320 | tf_op jit(solution)/shard_map/ppermute | solution.py:16
  44.6 3.3 %collective-permute-start.6 = (f32[2,128,512]{2,1,0:T(8,128)S(1)}, f32[2,128,512]{2,1,0:T(8,128)}, u32[]{:S(2)}, u32[]{:S(2)}) collective-permute-start(f32[2,128,512]{2,1,0:T(8,128)S(1)} %collective-permute-done.5.mine_ref), channel_id=1, source_target_pairs={{0,8},{8,0},{1,9},{9,1},{2,10},{10,2},{3,11},{11,3},{4,12},{12,4},... | collective-permute-start | bytes 1572872 | tf_op jit(solution)/shard_map/ppermute | solution.py:16
  47.9 0.0 collective-permute-done.3.mine_ref
  47.9 12.4 %collective-permute-start.4 = (f32[2,128,512]{2,1,0:T(8,128)S(1)}, f32[2,128,512]{2,1,0:T(8,128)S(1)}, u32[]{:S(2)}, u32[]{:S(2)}) collective-permute-start(f32[2,128,512]{2,1,0:T(8,128)S(1)} %collective-permute-done.3.mine_ref), channel_id=1, source_target_pairs={{0,8},{8,0},{1,9},{9,1},{2,10},{10,2},{3,11},{11,3},{4,12},{12,4},... | collective-permute-start | bytes 1572872 | tf_op jit(solution)/shard_map/ppermute | solution.py:16
  60.3 0.1 add_add_fusion.3.place
  60.4 1.9 %collective-permute-start.2 = (f32[2,128,512]{2,1,0:T(8,128)S(1)}, f32[2,128,512]{2,1,0:T(8,128)}, u32[]{:S(2)}, u32[]{:S(2)}) collective-permute-start(f32[2,128,512]{2,1,0:T(8,128)S(1)} %collective-permute-done.1.mine_ref), channel_id=1, source_target_pairs={{0,8},{8,0},{1,9},{9,1},{2,10},{10,2},{3,11},{11,3},{4,12},{12,4},... | collective-permute-start | bytes 1572872 | tf_op jit(solution)/shard_map/ppermute | solution.py:16
  62.4 0.1 add_add_fusion.2.place
  62.4 0.1 add_add_fusion.1.place
  62.5 0.1 add_add_fusion.place
  62.6 1.2 copy-done.2
  63.8 2.3 %shard_map.41.rest_0_ = f32[512,2048]{1,0:T(8,128)S(1)} custom-call(s32[3]{0:T(128)S(1)} %add_add_fusion.3.place, f32[4,128,512]{2,1,0:T(8,128)S(1)} %bitcast.20, f32[2,128,512]{2,1,0:T(8,128)S(1)} %pad_maximum_fusion.mine_ref, f32[2,128,512]{2,1,0:T(8,128)S(1)} %collective-permute-done.7.other_ref), custom_call_target="tpu_custom_call" | custom-call | flops 805306368 | bytes 3145728 | tf_op jit(solution)/shard_map/pallas_call | solution.py:54
  66.2 3.3 %shard_map.42.rest_0_ = f32[512,2048]{1,0:T(8,128)S(1)} custom-call(s32[3]{0:T(128)S(1)} %add_add_fusion.2.place, f32[4,128,512]{2,1,0:T(8,128)S(1)} %bitcast.21, f32[2,128,512]{2,1,0:T(8,128)S(1)} %collective-permute-done.5.mine_ref, f32[2,128,512]{2,1,0:T(8,128)} %collective-permute-done.6.other_ref, ...), custom_call_target="tpu_custom_call", output_to_operand_aliasing={{}: (4, {})} | custom-call | flops 805306368 | bytes 3145728 | tf_op jit(solution)/shard_map/pallas_call | solution.py:54
  69.5 2.3 %shard_map.43.rest_0_ = f32[512,2048]{1,0:T(8,128)S(1)} custom-call(s32[3]{0:T(128)S(1)} %add_add_fusion.1.place, f32[4,128,512]{2,1,0:T(8,128)S(1)} %bitcast.22, f32[2,128,512]{2,1,0:T(8,128)S(1)} %collective-permute-done.3.mine_ref, f32[2,128,512]{2,1,0:T(8,128)S(1)} %collective-permute-done.4.other_ref, ...), custom_call_target="tpu_custom_call", output_to_operand_aliasing={{}: (4, {})} | custom-call | flops 805306368 | bytes 3145728 | tf_op jit(solution)/shard_map/pallas_call | solution.py:54
  71.8 3.3 %shard_map.44 = f32[512,2048]{1,0:T(8,128)S(1)} custom-call(s32[3]{0:T(128)S(1)} %add_add_fusion.place, f32[4,128,512]{2,1,0:T(8,128)S(1)} %bitcast.23, f32[2,128,512]{2,1,0:T(8,128)S(1)} %collective-permute-done.1.mine_ref, f32[2,128,512]{2,1,0:T(8,128)} %collective-permute-done.2.other_ref, ...), custom_call_target="tpu_custom_call", output_to_operand_aliasing={{}: (4, {})} | custom-call | flops 805306368 | bytes 3145728 | tf_op jit(solution)/shard_map/pallas_call | solution.py:54
  75.2 1.9 %copy-done.1 = f32[512,2048]{1,0:T(8,128)} copy-done((f32[512,2048]{1,0:T(8,128)}, f32[512,2048]{1,0:T(8,128)S(1)}, u32[]{:S(2)}) %copy-start.1) | copy-done | bytes 4194328
  77.1 0.0 reduce-scatter.2.cloned.1.call-update
  77.1 0.9 copy-done.3
  78.0 0.2 convolution_bitcast_fusion
  78.3 94.8 %all-gather.2 = f32[64,1,512]{2,1,0:T(1,128)S(1)} all-gather(f32[1,1,512]{2,1,0:T(1,128)S(1)} %convolution_bitcast_fusion), channel_id=3, replica_groups=mesh['zl'=4,'zh'=2,'x'=4,'core'=2,'par'=8] {'zl','zh','x','core'}, dimensions={0}, use_global_device_ids=true | all-gather | bytes 133120 | tf_op jit(solution)/shard_map/all_gather | solution.py:94
  173.1 0.7 reduce_sum.9
  173.8 2.0 %reshape.7 = f32[16,4,2048]{2,1,0:T(4,128)} reshape(f32[64,2048]{1,0:T(8,128)} %reduce-scatter.2.cloned.1.call-done) | data formatting | bytes 1048576 | tf_op jit(solution)/shard_map/reshape | solution.py:107
  (11 shorter events, 0.0 us)
Async XLA Ops:
  7.2 70.0 %copy-start = (f32[128]{0:T(128)S(1)}, f32[128]{0:T(128)}, u32[]{:S(2)}) copy-start(f32[128]{0:T(128)} %param.3) | copy-start | bytes 1540
  7.2 55.4 %all-gather.5.cloned.1.call-start = ((), (), s32[]{:S(2)}) async-start(), calls=%async_computation.2 | async-start | bytes 1310720 | tf_op jit(solution)/shard_map/all_gather | solution.py:90
  7.9 165.9 %reduce-scatter.2.cloned.1.call-start = ((), (), s32[]{:S(2)}) async-start(), calls=%async_computation.1 | async-start | bytes 4718592 | tf_op jit(solution)/shard_map/reduce_scatter | solution.py:106
  8.0 19.6 %collective-permute-start = (f32[128,512]{1,0:T(8,128)}, f32[128,512]{1,0:T(8,128)S(1)}, u32[]{:S(2)}, u32[]{:S(2)}) collective-permute-start(f32[128,512]{1,0:T(8,128)} %param.2), channel_id=1, source_target_pairs={{0,64},{64,0},{1,65},{65,1},{2,66},{66,2},{3,67},{67,3},{4,68},{68... | collective-permute-start | bytes 786440 | tf_op jit(solution)/shard_map/ppermute | solution.py:16
  28.6 16.1 %collective-permute-start.5 = (f32[2,128,512]{2,1,0:T(8,128)S(1)}, f32[2,128,512]{2,1,0:T(8,128)S(1)}, u32[]{:S(2)}, u32[]{:S(2)}) collective-permute-start(f32[2,128,512]{2,1,0:T(8,128)S(1)} %pad_maximum_fusion.mine_ref), channel_id=1, source_target_pairs={{0,16},{16,32},{32,48},{48,0},{1,17},{17,33},{33,49},{49,1},{2,18}... | collective-permute-start | bytes 1572872 | tf_op jit(solution)/shard_map/ppermute | solution.py:16
  31.7 16.2 %collective-permute-start.3 = (f32[2,128,512]{2,1,0:T(8,128)S(1)}, f32[2,128,512]{2,1,0:T(8,128)S(1)}, u32[]{:S(2)}, u32[]{:S(2)}) collective-permute-start(f32[2,128,512]{2,1,0:T(8,128)S(1)} %pad_maximum_fusion.mine_ref), channel_id=1, source_target_pairs={{0,48},{16,0},{32,16},{48,32},{1,49},{17,1},{33,17},{49,33},{2,50}... | collective-permute-start | bytes 1572872 | tf_op jit(solution)/shard_map/ppermute | solution.py:16
  35.1 25.4 %collective-permute-start.1 = (f32[2,128,512]{2,1,0:T(8,128)S(1)}, f32[2,128,512]{2,1,0:T(8,128)S(1)}, u32[]{:S(2)}, u32[]{:S(2)}) collective-permute-start(f32[2,128,512]{2,1,0:T(8,128)S(1)} %pad_maximum_fusion.mine_ref), channel_id=1, source_target_pairs={{0,32},{16,48},{32,0},{48,16},{1,33},{17,49},{33,1},{49,17},{2,34}... | collective-permute-start | bytes 1572872 | tf_op jit(solution)/shard_map/ppermute | solution.py:16
  38.5 24.1 %collective-permute-start.7 = (f32[2,128,512]{2,1,0:T(8,128)S(1)}, f32[2,128,512]{2,1,0:T(8,128)S(1)}, u32[]{:S(2)}, u32[]{:S(2)}) collective-permute-start(f32[2,128,512]{2,1,0:T(8,128)S(1)} %pad_maximum_fusion.mine_ref), channel_id=1, source_target_pairs={{0,8},{8,0},{1,9},{9,1},{2,10},{10,2},{3,11},{11,3},{4,12},{12,4},... | collective-permute-start | bytes 1572872 | tf_op jit(solution)/shard_map/ppermute | solution.py:16
  44.6 21.5 %collective-permute-start.6 = (f32[2,128,512]{2,1,0:T(8,128)S(1)}, f32[2,128,512]{2,1,0:T(8,128)}, u32[]{:S(2)}, u32[]{:S(2)}) collective-permute-start(f32[2,128,512]{2,1,0:T(8,128)S(1)} %collective-permute-done.5.mine_ref), channel_id=1, source_target_pairs={{0,8},{8,0},{1,9},{9,1},{2,10},{10,2},{3,11},{11,3},{4,12},{12,4},... | collective-permute-start | bytes 1572872 | tf_op jit(solution)/shard_map/ppermute | solution.py:16
  47.9 21.6 %collective-permute-start.4 = (f32[2,128,512]{2,1,0:T(8,128)S(1)}, f32[2,128,512]{2,1,0:T(8,128)S(1)}, u32[]{:S(2)}, u32[]{:S(2)}) collective-permute-start(f32[2,128,512]{2,1,0:T(8,128)S(1)} %collective-permute-done.3.mine_ref), channel_id=1, source_target_pairs={{0,8},{8,0},{1,9},{9,1},{2,10},{10,2},{3,11},{11,3},{4,12},{12,4},... | collective-permute-start | bytes 1572872 | tf_op jit(solution)/shard_map/ppermute | solution.py:16
  60.4 11.4 %collective-permute-start.2 = (f32[2,128,512]{2,1,0:T(8,128)S(1)}, f32[2,128,512]{2,1,0:T(8,128)}, u32[]{:S(2)}, u32[]{:S(2)}) collective-permute-start(f32[2,128,512]{2,1,0:T(8,128)S(1)} %collective-permute-done.1.mine_ref), channel_id=1, source_target_pairs={{0,8},{8,0},{1,9},{9,1},{2,10},{10,2},{3,11},{11,3},{4,12},{12,4},... | collective-permute-start | bytes 1572872 | tf_op jit(solution)/shard_map/ppermute | solution.py:16
  62.6 1.2 copy-start.2
  75.1 2.0 %copy-start.1 = (f32[512,2048]{1,0:T(8,128)}, f32[512,2048]{1,0:T(8,128)S(1)}, u32[]{:S(2)}) copy-start(f32[512,2048]{1,0:T(8,128)S(1)} %shard_map.44) | copy-start | bytes 12582916
  77.1 0.9 copy-start.3
Sparse Core Ops, SparseCore 0:
  10.1 33.9 all-gather.4
  77.2 55.7 reduce-scatter.1

commit v2 on v1

v2 whole, which is shorter than its diff:
```python
import jax
import jax.numpy as jnp
from jax import lax
from jax.experimental import pallas as pl
from jax.experimental.pallas import tpu as pltpu
from jax.sharding import Mesh, PartitionSpec as P

AXES = ("zl", "zh", "x", "core", "par")
SIZES = (4, 2, 4, 2, 8)
SAMPLES = AXES[:4]
LANES = 128
PIECE = (4, 3, -3, 2, -2, 1, -1, 0)
HOPS = (0, 1, 3, 2)


def shift(value, axis, by):
    count = lax.axis_size(axis)
    return lax.ppermute(value, axis, [(i, (i + by) % count) for i in range(count)])


def swap(value, axis, bit):
    return lax.ppermute(value, axis, [(i, i ^ bit) for i in range(lax.axis_size(axis))])


def beside(data, value, axis, bit):
    return lax.optimization_barrier((data, value + swap(value, axis, bit)))


def halves(value):
    high = value.astype(jnp.bfloat16)
    low = (value - high.astype(jnp.float32)).astype(jnp.bfloat16)
    return high, low


def product_kernel(place, left_ref, mine_ref, other_ref, *rest):
    outs, (left, high, low, right) = rest[:-4], rest[-4:]
    blocks, local, params = left_ref.shape
    share = local // len(PIECE)
    rows = blocks * share

    @pl.when(pl.program_id(0) == 0)
    def _():
        for g in range(params // LANES):
            lanes = pl.ds(g * LANES, LANES)
            for n in range(len(PIECE)):
                first = pl.multiple_of(place[5 + n] * share, share)
                for a in range(blocks):
                    left[g, pl.ds(n * rows + a, share, stride=blocks), :] = left_ref[
                        a, pl.ds(first, share), lanes
                    ]
            high[:, lanes], low[:, lanes] = halves(left[g])

    core = place[4]
    right[pl.ds(pl.multiple_of(core * local, local), local), :] = mine_ref[0]
    right[pl.ds(pl.multiple_of((1 - core) * local, local), local), :] = other_ref[0]
    right_high, right_low = halves(right[...])

    def dot(a, b):
        return lax.dot_general(
            a, b, (((1,), (1,)), ((), ())), preferred_element_type=jnp.float32
        )

    value = dot(high[...], right_low) + dot(low[...], right_high) + dot(high[...], right_high)
    outs[0][...] = value[: rows // 2]
    outs[1][...] = value[rows // 2 : rows]
    for n in range(1, len(PIECE)):
        outs[n + 1][...] = value[n * rows : (n + 1) * rows]


def product(place, left, mine, other):
    blocks, local, params = left.shape
    count = len(mine)
    rows = blocks * local // len(PIECE)
    heights = (rows // 2,) * 2 + (rows,) * (len(PIECE) - 1)
    return pl.pallas_call(
        product_kernel,
        grid_spec=pltpu.PrefetchScalarGridSpec(
            num_scalar_prefetch=1,
            grid=(count,),
            in_specs=[
                pl.BlockSpec((blocks, local, params), lambda j, place: (0, 0, 0)),
                pl.BlockSpec((1, local, params), lambda j, place: (j, 0, 0)),
                pl.BlockSpec((1, local, params), lambda j, place: (j, 0, 0)),
            ],
            out_specs=[
                pl.BlockSpec((h, 2 * local), lambda j, place: (0, place[j])) for h in heights
            ],
            scratch_shapes=[
                pltpu.VMEM((params // LANES, blocks * local, LANES), jnp.float32),
                pltpu.VMEM((blocks * local, params), jnp.bfloat16),
                pltpu.VMEM((blocks * local, params), jnp.bfloat16),
                pltpu.VMEM((2 * local, params), jnp.float32),
            ],
        ),
        out_shape=[
            jax.ShapeDtypeStruct((h, 2 * local * count), jnp.float32) for h in heights
        ],
        compiler_params=pltpu.CompilerParams(vmem_limit_bytes=24 * 1024 * 1024),
        cost_estimate=pl.CostEstimate(
            flops=2 * 3 * blocks * local * 2 * local * count * params,
            bytes_accessed=4 * (blocks * local * params + 2 * local * count * (params + blocks * local)),
            transcendentals=0,
        ),
    )(place, left, mine, other)


def finish_kernel(place, own_ref, right_ref, left_ref, *rest):
    value = own_ref[...] + (right_ref[...] + left_ref[...])
    rest[-1][...] = value.reshape(rest[-1].shape)


def finish(place, own, from_left, from_right, blocks, done):
    rows, columns = own.shape
    spec = pl.BlockSpec((rows, columns), lambda j, place: (0, 0))
    return pl.pallas_call(
        finish_kernel,
        grid_spec=pltpu.PrefetchScalarGridSpec(
            num_scalar_prefetch=1,
            grid=(1,),
            in_specs=[spec] * 3 + [pl.BlockSpec(memory_space=pl.ANY)] * len(done),
            out_specs=pl.BlockSpec(
                (rows // blocks, blocks, columns), lambda j, place: (0, 0, place[0])
            ),
        ),
        out_shape=jax.ShapeDtypeStruct((rows // blocks, blocks, 2 * columns), jnp.float32),
        input_output_aliases={4: 0} if done else {},
        compiler_params=pltpu.CompilerParams(vmem_limit_bytes=24 * 1024 * 1024),
        cost_estimate=pl.CostEstimate(
            flops=2 * rows * columns, bytes_accessed=16 * rows * columns, transcendentals=0
        ),
    )(place, own, from_left, from_right, *done)


def body(log_derivs, sample_vector):
    zh, x, core, par = (lax.axis_index(name) for name in ("zh", "x", "core", "par"))
    x_count, par_count = lax.axis_size("x"), lax.axis_size("par")
    left = lax.all_gather(log_derivs, "zl")
    blocks = left.shape[0]

    value = jnp.dot(
        sample_vector, log_derivs, precision=lax.Precision.HIGHEST, preferred_element_type=jnp.float32
    )
    far = swap(log_derivs, "zh", 1)
    near = jnp.stack([log_derivs] + [shift(log_derivs, "x", by) for by in HOPS[1:]])
    near, value = beside(near, value, "core", 1)
    near_other = swap(near, "core", 1)
    far, value = beside(far, value, "x", 1)
    far = jnp.stack([far] + [shift(far, "x", by) for by in HOPS[1:]])
    far, value = beside(far, value, "x", 2)
    far_other = swap(far, "core", 1)

    place = jnp.stack(
        [lax.rem(x + x_count - by, x_count) for by in HOPS]
        + [core]
        + [lax.rem(par + par_count + to, par_count) for to in PIECE]
    ).astype(jnp.int32)
    parts = [product(place, left, near, near_other), product(place, left, far, far_other)]

    half = parts[0][0].shape[0]
    going = [[p[0], p[1]] for p in parts]
    for step in range(1, 5):
        arrived = [[shift(g[0], "par", 1), shift(g[1], "par", -1)] for g in going]
        if step < 4:
            arrived, value = beside(arrived, value, *(("zh", 1), ("zl", 1), ("zl", 2))[step - 1])
        if step == 1:
            going = [
                [p[2].at[:half].add(a[0]), p[3].at[half:].add(a[1])] for p, a in zip(parts, arrived)
            ]
        elif step < 4:
            going = [
                [p[2 * step] + a[0], p[2 * step + 1] + a[1]] for p, a in zip(parts, arrived)
            ]
    done = ()
    for part, came, column in zip(parts, arrived, (zh, 1 - zh)):
        done = (finish(column.reshape(1).astype(jnp.int32), part[8], *came, blocks, done),)
    return (done[0], value)


def solution(mesh):
    split = Mesh(mesh.devices.reshape(SIZES), AXES)
    in_specs = (P(SAMPLES, "par"), P(SAMPLES))
    out_specs = (P(("zh", "x", "core", "par"), None, "zl"), P("par"))
    return jax.shard_map(body, mesh=split, in_specs=in_specs, out_specs=out_specs, check_vma=False)
```

time: 183 us -> 167 us (0.913)
  the two profiles are of different devices: /device:TPU:417 before, /device:TPU:2 now
where the time goes in v2:
time: 167 us; the launch traced here: 166 us
  starting transfers between devices  105 us (63%)
  waiting for transfers between devices  32.2 us (19%)
  between operations  14.5 us (9%)
  Pallas kernels  11 us (7%)
    ppermute x22, starting transfers between devices, shift(): lax.ppermute(value, axis, [(i, (i + by) % count) for i in range(count)])  74.5 us
    ppermute x9, starting transfers between devices, swap(): lax.ppermute(value, axis, [(i, i ^ bit) for i in range(lax.axis_size(axis...  30.5 us
    ppermute x9, waiting for transfers between devices, swap(): lax.ppermute(value, axis, [(i, i ^ bit) for i in range(lax.axis_size(axis...  18.8 us
    pallas_call x2, Pallas kernels, product(): pl.pallas_call(product_kernel, grid_spec=pltpu.PrefetchScalarGridSpec(num...  9.54 us
    ppermute x22, waiting for transfers between devices, shift(): lax.ppermute(value, axis, [(i, (i + by) % count) for i in range(count)])  9.05 us
    all_gather x1, waiting for transfers between devices, body(): left = lax.all_gather(log_derivs, 'zl')  4.29 us
  transfers between devices with their start and end apart: 32, of which 12 were waited for; matrix products, arithmetic and copies ran while one was open for 1% of the time, Pallas kernels for 6%

profile of v2, /device:TPU:2, one launch (start us, length us, event | category | flops | bytes accessed | tf_op | source)
XLA Modules:
  0.0 165.5 jit_solution(12257353585031189336)
XLA Ops:
  7.2 3.5 %collective-permute-start.1 = (f32[128,512]{1,0:T(8,128)}, f32[128,512]{1,0:T(8,128)S(1)}, u32[]{:S(2)}, u32[]{:S(2)}) collective-permute-start(f32[128,512]{1,0:T(8,128)} %param.10), channel_id=1, source_target_pairs={{0,16},{16,32},{32,48},{48,0},{1,17},{17,33},{33,49},{49,1},{2,18}... | collective-permute-start | bytes 786440 | tf_op jit(solution)/shard_map/ppermute | solution.py:18
  10.8 6.3 %collective-permute-start.2 = (f32[128,512]{1,0:T(8,128)}, f32[128,512]{1,0:T(8,128)S(1)}, u32[]{:S(2)}, u32[]{:S(2)}) collective-permute-start(f32[128,512]{1,0:T(8,128)} %param.10), channel_id=1, source_target_pairs={{0,48},{16,0},{32,16},{48,32},{1,49},{17,1},{33,17},{49,33},{2,50}... | collective-permute-start | bytes 786440 | tf_op jit(solution)/shard_map/ppermute | solution.py:18
  17.1 4.0 %collective-permute-start.3 = (f32[128,512]{1,0:T(8,128)}, f32[128,512]{1,0:T(8,128)S(1)}, u32[]{:S(2)}, u32[]{:S(2)}) collective-permute-start(f32[128,512]{1,0:T(8,128)} %param.10), channel_id=1, source_target_pairs={{0,32},{16,48},{32,0},{48,16},{1,33},{17,49},{33,1},{49,17},{2,34}... | collective-permute-start | bytes 786440 | tf_op jit(solution)/shard_map/ppermute | solution.py:18
  21.1 7.1 %collective-permute-start = (f32[128,512]{1,0:T(8,128)}, f32[128,512]{1,0:T(8,128)S(1)}, u32[]{:S(2)}, u32[]{:S(2)}) collective-permute-start(f32[128,512]{1,0:T(8,128)} %param.10), channel_id=1, source_target_pairs={{0,64},{64,0},{1,65},{65,1},{2,66},{66,2},{3,67},{67,3},{4,68},{68... | collective-permute-start | bytes 786440 | tf_op jit(solution)/shard_map/ppermute | solution.py:22
  31.6 3.3 %collective-permute-start.5 = (f32[512]{0:T(512)S(1)}, f32[512]{0:T(512)S(1)}, u32[]{:S(2)}, u32[]{:S(2)}) collective-permute-start(f32[512]{0:T(512)S(1)} %add.139), channel_id=1, source_target_pairs={{0,16},{16,0},{32,48},{48,32},{1,17},{17,1},{33,49},{49,33},{2,18}... | collective-permute-start | bytes 6152 | tf_op jit(solution)/shard_map/ppermute | solution.py:22
  35.0 2.1 %collective-permute-done.5 = f32[512]{0:T(512)S(1)} collective-permute-done((f32[512]{0:T(512)S(1)}, f32[512]{0:T(512)S(1)}, u32[]{:S(2)}, u32[]{:S(2)}) %collective-permute-start.5) | collective-permute-done | bytes 2080 | tf_op jit(solution)/shard_map/ppermute | solution.py:22
  40.8 3.9 %collective-permute-start.7 = (f32[128,512]{1,0:T(8,128)S(1)}, f32[128,512]{1,0:T(8,128)S(1)}, u32[]{:S(2)}, u32[]{:S(2)}) collective-permute-start(f32[128,512]{1,0:T(8,128)S(1)} %collective-permute-done), channel_id=1, source_target_pairs={{0,48},{16,0},{32,16},{48,32},{1,49},{17,1},{33,17},{49,33},{2,50}... | collective-permute-start | bytes 786440 | tf_op jit(solution)/shard_map/ppermute | solution.py:18
  44.7 3.4 %collective-permute-start.8 = (f32[128,512]{1,0:T(8,128)S(1)}, f32[128,512]{1,0:T(8,128)S(1)}, u32[]{:S(2)}, u32[]{:S(2)}) collective-permute-start(f32[128,512]{1,0:T(8,128)S(1)} %collective-permute-done), channel_id=1, source_target_pairs={{0,32},{16,48},{32,0},{48,16},{1,33},{17,49},{33,1},{49,17},{2,34}... | collective-permute-start | bytes 786440 | tf_op jit(solution)/shard_map/ppermute | solution.py:18
  50.0 4.0 %collective-permute-start.9 = (f32[512]{0:T(512)S(1)}, f32[512]{0:T(512)S(1)}, u32[]{:S(2)}, u32[]{:S(2)}) collective-permute-start(f32[512]{0:T(512)S(1)} %add.140), channel_id=1, source_target_pairs={{0,32},{16,48},{32,0},{48,16},{1,33},{17,49},{33,1},{49,17},{2,34}... | collective-permute-start | bytes 6152 | tf_op jit(solution)/shard_map/ppermute | solution.py:22
  54.0 3.0 %collective-permute-done.9 = f32[512]{0:T(512)S(1)} collective-permute-done((f32[512]{0:T(512)S(1)}, f32[512]{0:T(512)S(1)}, u32[]{:S(2)}, u32[]{:S(2)}) %collective-permute-start.9) | collective-permute-done | bytes 2080 | tf_op jit(solution)/shard_map/ppermute | solution.py:22
  59.1 4.3 %all-gather.3.cloned.1.call-done = f32[512,512]{1,0:T(8,128)} async-done(((f32[128,512]{1,0:T(8,128)}), f32[512,512]{1,0:T(8,128)}) %all-gather.3.cloned.1.call-update) | async-done | bytes 1048592 | tf_op jit(solution)/shard_map/all_gather | solution.py:137
  64.7 4.2 %shard_map.42 = (f32[32,1024]{1,0:T(8,128)S(1)}, f32[32,1024]{1,0:T(8,128)S(1)}, f32[64,1024]{1,0:T(8,128)S(1)}, f32[64,1024]{1,0:T(8,128)S(1)}, f32[64,1024]{1,...) custom-call(s32[13]{0:T(128)S(1)} %stack.83.place, ...), custom_call_target="tpu_custom_call" | custom-call | flops 1610612736 | bytes 5242880 | tf_op jit(solution)/shard_map/pallas_call | solution.py:75
  68.9 3.4 %collective-permute-start.12 = (f32[32,1024]{1,0:T(8,128)S(1)}, f32[32,1024]{1,0:T(8,128)S(1)}, u32[]{:S(2)}, u32[]{:S(2)}) collective-permute-start(f32[32,1024]{1,0:T(8,128)S(1)} %get-tuple-element.98), channel_id=1, source_target_pairs={{0,1},{1,2},{2,3},{3,4},{4,5},{5,6},{6,7},{7,0},{8,9},{9,10},{10,1... | collective-permute-start | bytes 393224 | tf_op jit(solution)/shard_map/ppermute | solution.py:18
  72.3 3.7 %collective-permute-start.13 = (f32[32,1024]{1,0:T(8,128)S(1)}, f32[32,1024]{1,0:T(8,128)S(1)}, u32[]{:S(2)}, u32[]{:S(2)}) collective-permute-start(f32[32,1024]{1,0:T(8,128)S(1)} %get-tuple-element.99), channel_id=1, source_target_pairs={{0,7},{1,0},{2,1},{3,2},{4,3},{5,4},{6,5},{7,6},{8,15},{9,8},{10,9... | collective-permute-start | bytes 393224 | tf_op jit(solution)/shard_map/ppermute | solution.py:18
  76.0 5.3 %shard_map.41 = (f32[32,1024]{1,0:T(8,128)S(1)}, f32[32,1024]{1,0:T(8,128)S(1)}, f32[64,1024]{1,0:T(8,128)S(1)}, f32[64,1024]{1,0:T(8,128)S(1)}, f32[64,1024]{1,...) custom-call(s32[13]{0:T(128)S(1)} %stack.83.place, ...), custom_call_target="tpu_custom_call" | custom-call | flops 1610612736 | bytes 5242880 | tf_op jit(solution)/shard_map/pallas_call | solution.py:75
  81.3 2.2 %collective-permute-start.14 = (f32[32,1024]{1,0:T(8,128)S(1)}, f32[32,1024]{1,0:T(8,128)S(1)}, u32[]{:S(2)}, u32[]{:S(2)}) collective-permute-start(f32[32,1024]{1,0:T(8,128)S(1)} %get-tuple-element.100), channel_id=1, source_target_pairs={{0,1},{1,2},{2,3},{3,4},{4,5},{5,6},{6,7},{7,0},{8,9},{9,10},{10,1... | collective-permute-start | bytes 393224 | tf_op jit(solution)/shard_map/ppermute | solution.py:18
  83.5 4.9 %collective-permute-start.15 = (f32[32,1024]{1,0:T(8,128)S(1)}, f32[32,1024]{1,0:T(8,128)S(1)}, u32[]{:S(2)}, u32[]{:S(2)}) collective-permute-start(f32[32,1024]{1,0:T(8,128)S(1)} %get-tuple-element.101), channel_id=1, source_target_pairs={{0,7},{1,0},{2,1},{3,2},{4,3},{5,4},{6,5},{7,6},{8,15},{9,8},{10,9... | collective-permute-start | bytes 393224 | tf_op jit(solution)/shard_map/ppermute | solution.py:18
  88.4 5.5 %collective-permute-start.16 = (f32[512]{0:T(512)S(1)}, f32[512]{0:T(512)S(1)}, u32[]{:S(2)}, u32[]{:S(2)}) collective-permute-start(f32[512]{0:T(512)S(1)} %add.141), channel_id=1, source_target_pairs={{0,64},{64,0},{1,65},{65,1},{2,66},{66,2},{3,67},{67,3},{4,68},{68... | collective-permute-start | bytes 6152 | tf_op jit(solution)/shard_map/ppermute | solution.py:22
  93.9 3.8 %collective-permute-done.16 = f32[512]{0:T(512)S(1)} collective-permute-done((f32[512]{0:T(512)S(1)}, f32[512]{0:T(512)S(1)}, u32[]{:S(2)}, u32[]{:S(2)}) %collective-permute-start.16) | collective-permute-done | bytes 2080 | tf_op jit(solution)/shard_map/ppermute | solution.py:22
  97.8 2.3 %collective-permute-start.20 = (f32[64,1024]{1,0:T(8,128)S(1)}, f32[64,1024]{1,0:T(8,128)S(1)}, u32[]{:S(2)}, u32[]{:S(2)}) collective-permute-start(f32[64,1024]{1,0:T(8,128)S(1)} %add_dynamic-update-slice_fusion), channel_id=1, source_target_pairs={{0,7},{1,0},{2,1},{3,2},{4,3},{5,4},{6,5},{7,6},{8,15},{9,8},{10,9... | collective-permute-start | bytes 786440 | tf_op jit(solution)/shard_map/ppermute | solution.py:18
  100.2 3.5 %collective-permute-start.19 = (f32[64,1024]{1,0:T(8,128)S(1)}, f32[64,1024]{1,0:T(8,128)S(1)}, u32[]{:S(2)}, u32[]{:S(2)}) collective-permute-start(f32[64,1024]{1,0:T(8,128)S(1)} %add_dynamic-update-slice_fusion.1), channel_id=1, source_target_pairs={{0,1},{1,2},{2,3},{3,4},{4,5},{5,6},{6,7},{7,0},{8,9},{9,10},{10,1... | collective-permute-start | bytes 786440 | tf_op jit(solution)/shard_map/ppermute | solution.py:18
  103.8 3.5 %collective-permute-start.18 = (f32[64,1024]{1,0:T(8,128)S(1)}, f32[64,1024]{1,0:T(8,128)S(1)}, u32[]{:S(2)}, u32[]{:S(2)}) collective-permute-start(f32[64,1024]{1,0:T(8,128)S(1)} %add_dynamic-update-slice_fusion.2), channel_id=1, source_target_pairs={{0,7},{1,0},{2,1},{3,2},{4,3},{5,4},{6,5},{7,6},{8,15},{9,8},{10,9... | collective-permute-start | bytes 786440 | tf_op jit(solution)/shard_map/ppermute | solution.py:18
  107.3 2.3 %collective-permute-start.17 = (f32[64,1024]{1,0:T(8,128)S(1)}, f32[64,1024]{1,0:T(8,128)S(1)}, u32[]{:S(2)}, u32[]{:S(2)}) collective-permute-start(f32[64,1024]{1,0:T(8,128)S(1)} %add_dynamic-update-slice_fusion.3), channel_id=1, source_target_pairs={{0,1},{1,2},{2,3},{3,4},{4,5},{5,6},{6,7},{7,0},{8,9},{9,10},{10,1... | collective-permute-start | bytes 786440 | tf_op jit(solution)/shard_map/ppermute | solution.py:18
  111.6 3.6 %collective-permute-done.21 = f32[512]{0:T(512)S(1)} collective-permute-done((f32[512]{0:T(512)S(1)}, f32[512]{0:T(512)S(1)}, u32[]{:S(2)}, u32[]{:S(2)}) %collective-permute-start.21) | collective-permute-done | bytes 2080 | tf_op jit(solution)/shard_map/ppermute | solution.py:22
  116.9 3.1 %collective-permute-start.25 = (f32[64,1024]{1,0:T(8,128)S(1)}, f32[64,1024]{1,0:T(8,128)S(1)}, u32[]{:S(2)}, u32[]{:S(2)}) collective-permute-start(f32[64,1024]{1,0:T(8,128)S(1)} %add.151), channel_id=1, source_target_pairs={{0,7},{1,0},{2,1},{3,2},{4,3},{5,4},{6,5},{7,6},{8,15},{9,8},{10,9... | collective-permute-start | bytes 786440 | tf_op jit(solution)/shard_map/ppermute | solution.py:18
  120.0 2.7 %collective-permute-start.24 = (f32[64,1024]{1,0:T(8,128)S(1)}, f32[64,1024]{1,0:T(8,128)S(1)}, u32[]{:S(2)}, u32[]{:S(2)}) collective-permute-start(f32[64,1024]{1,0:T(8,128)S(1)} %add.150), channel_id=1, source_target_pairs={{0,1},{1,2},{2,3},{3,4},{4,5},{5,6},{6,7},{7,0},{8,9},{9,10},{10,1... | collective-permute-start | bytes 786440 | tf_op jit(solution)/shard_map/ppermute | solution.py:18
  122.8 4.3 %collective-permute-start.23 = (f32[64,1024]{1,0:T(8,128)S(1)}, f32[64,1024]{1,0:T(8,128)S(1)}, u32[]{:S(2)}, u32[]{:S(2)}) collective-permute-start(f32[64,1024]{1,0:T(8,128)S(1)} %add.149), channel_id=1, source_target_pairs={{0,7},{1,0},{2,1},{3,2},{4,3},{5,4},{6,5},{7,6},{8,15},{9,8},{10,9... | collective-permute-start | bytes 786440 | tf_op jit(solution)/shard_map/ppermute | solution.py:18
  129.1 2.9 %collective-permute-start.26 = (f32[512]{0:T(512)S(1)}, f32[512]{0:T(512)S(1)}, u32[]{:S(2)}, u32[]{:S(2)}) collective-permute-start(f32[512]{0:T(512)S(1)} %add.147), channel_id=1, source_target_pairs={{0,256},{128,384},{256,0},{384,128},{1,257},{129,385},{257,1},{385... | collective-permute-start | bytes 6152 | tf_op jit(solution)/shard_map/ppermute | solution.py:22
  132.0 3.4 %collective-permute-done.26 = f32[512]{0:T(512)S(1)} collective-permute-done((f32[512]{0:T(512)S(1)}, f32[512]{0:T(512)S(1)}, u32[]{:S(2)}, u32[]{:S(2)}) %collective-permute-start.26) | collective-permute-done | bytes 2080 | tf_op jit(solution)/shard_map/ppermute | solution.py:22
  136.7 4.6 %collective-permute-start.30 = (f32[64,1024]{1,0:T(8,128)S(1)}, f32[64,1024]{1,0:T(8,128)S(1)}, u32[]{:S(2)}, u32[]{:S(2)}) collective-permute-start(f32[64,1024]{1,0:T(8,128)S(1)} %add.156), channel_id=1, source_target_pairs={{0,7},{1,0},{2,1},{3,2},{4,3},{5,4},{6,5},{7,6},{8,15},{9,8},{10,9... | collective-permute-start | bytes 786440 | tf_op jit(solution)/shard_map/ppermute | solution.py:18
  143.3 5.1 %collective-permute-start.28 = (f32[64,1024]{1,0:T(8,128)S(1)}, f32[64,1024]{1,0:T(8,128)S(1)}, u32[]{:S(2)}, u32[]{:S(2)}) collective-permute-start(f32[64,1024]{1,0:T(8,128)S(1)} %add.154), channel_id=1, source_target_pairs={{0,7},{1,0},{2,1},{3,2},{4,3},{5,4},{6,5},{7,6},{8,15},{9,8},{10,9... | collective-permute-start | bytes 786440 | tf_op jit(solution)/shard_map/ppermute | solution.py:18
  153.1 4.8 %collective-permute-done.27.right_ref = f32[64,1024]{1,0:T(8,128)S(1)} collective-permute-done((f32[64,1024]{1,0:T(8,128)S(1)}, f32[64,1024]{1,0:T(8,128)S(1)}, u32[]{:S(2)}, u32[]{:S(2)}) %collective-permute-start.27) | collective-permute-done | bytes 262176 | tf_op jit(solution)/shard_map/ppermute | solution.py:18
  (65 shorter events, 26.7 us)
Async XLA Ops:
  7.2 56.3 %all-gather.3.cloned.1.call-start = ((), (), s32[]{:S(2)}) async-start(), calls=%async_computation | async-start | bytes 1310720 | tf_op jit(solution)/shard_map/all_gather | solution.py:137
  7.2 24.3 %collective-permute-start.1 = (f32[128,512]{1,0:T(8,128)}, f32[128,512]{1,0:T(8,128)S(1)}, u32[]{:S(2)}, u32[]{:S(2)}) collective-permute-start(f32[128,512]{1,0:T(8,128)} %param.10), channel_id=1, source_target_pairs={{0,16},{16,32},{32,48},{48,0},{1,17},{17,33},{33,49},{49,1},{2,18}... | collective-permute-start | bytes 786440 | tf_op jit(solution)/shard_map/ppermute | solution.py:18
  10.8 20.8 %collective-permute-start.2 = (f32[128,512]{1,0:T(8,128)}, f32[128,512]{1,0:T(8,128)S(1)}, u32[]{:S(2)}, u32[]{:S(2)}) collective-permute-start(f32[128,512]{1,0:T(8,128)} %param.10), channel_id=1, source_target_pairs={{0,48},{16,0},{32,16},{48,32},{1,49},{17,1},{33,17},{49,33},{2,50}... | collective-permute-start | bytes 786440 | tf_op jit(solution)/shard_map/ppermute | solution.py:18
  17.1 14.4 %collective-permute-start.3 = (f32[128,512]{1,0:T(8,128)}, f32[128,512]{1,0:T(8,128)S(1)}, u32[]{:S(2)}, u32[]{:S(2)}) collective-permute-start(f32[128,512]{1,0:T(8,128)} %param.10), channel_id=1, source_target_pairs={{0,32},{16,48},{32,0},{48,16},{1,33},{17,49},{33,1},{49,17},{2,34}... | collective-permute-start | bytes 786440 | tf_op jit(solution)/shard_map/ppermute | solution.py:18
  21.1 17.7 %collective-permute-start = (f32[128,512]{1,0:T(8,128)}, f32[128,512]{1,0:T(8,128)S(1)}, u32[]{:S(2)}, u32[]{:S(2)}) collective-permute-start(f32[128,512]{1,0:T(8,128)} %param.10), channel_id=1, source_target_pairs={{0,64},{64,0},{1,65},{65,1},{2,66},{66,2},{3,67},{67,3},{4,68},{68... | collective-permute-start | bytes 786440 | tf_op jit(solution)/shard_map/ppermute | solution.py:22
  28.5 3.0 %collective-permute-start.4 = (f32[512]{0:T(512)S(1)}, f32[512]{0:T(512)S(1)}, u32[]{:S(2)}, u32[]{:S(2)}) collective-permute-start(f32[512]{0:T(512)S(1)} %bitcast.39), channel_id=1, source_target_pairs={{0,8},{8,0},{1,9},{9,1},{2,10},{10,2},{3,11},{11,3},{4,12},{12,4},... | collective-permute-start | bytes 6152 | tf_op jit(solution)/shard_map/ppermute | solution.py:22
  31.6 5.5 %collective-permute-start.5 = (f32[512]{0:T(512)S(1)}, f32[512]{0:T(512)S(1)}, u32[]{:S(2)}, u32[]{:S(2)}) collective-permute-start(f32[512]{0:T(512)S(1)} %add.139), channel_id=1, source_target_pairs={{0,16},{16,0},{32,48},{48,32},{1,17},{17,1},{33,49},{49,33},{2,18}... | collective-permute-start | bytes 6152 | tf_op jit(solution)/shard_map/ppermute | solution.py:22
  38.8 18.2 %collective-permute-start.6 = (f32[128,512]{1,0:T(8,128)S(1)}, f32[128,512]{1,0:T(8,128)S(1)}, u32[]{:S(2)}, u32[]{:S(2)}) collective-permute-start(f32[128,512]{1,0:T(8,128)S(1)} %collective-permute-done), channel_id=1, source_target_pairs={{0,16},{16,32},{32,48},{48,0},{1,17},{17,33},{33,49},{49,1},{2,18}... | collective-permute-start | bytes 786440 | tf_op jit(solution)/shard_map/ppermute | solution.py:18
  40.8 16.3 %collective-permute-start.7 = (f32[128,512]{1,0:T(8,128)S(1)}, f32[128,512]{1,0:T(8,128)S(1)}, u32[]{:S(2)}, u32[]{:S(2)}) collective-permute-start(f32[128,512]{1,0:T(8,128)S(1)} %collective-permute-done), channel_id=1, source_target_pairs={{0,48},{16,0},{32,16},{48,32},{1,49},{17,1},{33,17},{49,33},{2,50}... | collective-permute-start | bytes 786440 | tf_op jit(solution)/shard_map/ppermute | solution.py:18
  44.7 12.3 %collective-permute-start.8 = (f32[128,512]{1,0:T(8,128)S(1)}, f32[128,512]{1,0:T(8,128)S(1)}, u32[]{:S(2)}, u32[]{:S(2)}) collective-permute-start(f32[128,512]{1,0:T(8,128)S(1)} %collective-permute-done), channel_id=1, source_target_pairs={{0,32},{16,48},{32,0},{48,16},{1,33},{17,49},{33,1},{49,17},{2,34}... | collective-permute-start | bytes 786440 | tf_op jit(solution)/shard_map/ppermute | solution.py:18
  48.1 11.1 %collective-permute-start.11 = (f32[4,128,512]{2,1,0:T(8,128)S(1)}, f32[4,128,512]{2,1,0:T(8,128)S(1)}, u32[]{:S(2)}, u32[]{:S(2)}) collective-permute-start(f32[4,128,512]{2,1,0:T(8,128)S(1)} %pad_maximum_fusion.mine_ref), channel_id=1, source_target_pairs={{0,8},{8,0},{1,9},{9,1},{2,10},{10,2},{3,11},{11,3},{4,12},{12,4},... | collective-permute-start | bytes 3145736 | tf_op jit(solution)/shard_map/ppermute | solution.py:22
  50.0 7.0 %collective-permute-start.9 = (f32[512]{0:T(512)S(1)}, f32[512]{0:T(512)S(1)}, u32[]{:S(2)}, u32[]{:S(2)}) collective-permute-start(f32[512]{0:T(512)S(1)} %add.140), channel_id=1, source_target_pairs={{0,32},{16,48},{32,0},{48,16},{1,33},{17,49},{33,1},{49,17},{2,34}... | collective-permute-start | bytes 6152 | tf_op jit(solution)/shard_map/ppermute | solution.py:22
  57.1 18.9 %collective-permute-start.10 = (f32[4,128,512]{2,1,0:T(8,128)S(1)}, f32[4,128,512]{2,1,0:T(8,128)}, u32[]{:S(2)}, u32[]{:S(2)}) collective-permute-start(f32[4,128,512]{2,1,0:T(8,128)S(1)} %pad_maximum_fusion.1.mine_ref), channel_id=1, source_target_pairs={{0,8},{8,0},{1,9},{9,1},{2,10},{10,2},{3,11},{11,3},{4,12},{12,4},... | collective-permute-start | bytes 3145736 | tf_op jit(solution)/shard_map/ppermute | solution.py:22
  68.9 28.9 %collective-permute-start.12 = (f32[32,1024]{1,0:T(8,128)S(1)}, f32[32,1024]{1,0:T(8,128)S(1)}, u32[]{:S(2)}, u32[]{:S(2)}) collective-permute-start(f32[32,1024]{1,0:T(8,128)S(1)} %get-tuple-element.98), channel_id=1, source_target_pairs={{0,1},{1,2},{2,3},{3,4},{4,5},{5,6},{6,7},{7,0},{8,9},{9,10},{10,1... | collective-permute-start | bytes 393224 | tf_op jit(solution)/shard_map/ppermute | solution.py:18
  72.3 25.5 %collective-permute-start.13 = (f32[32,1024]{1,0:T(8,128)S(1)}, f32[32,1024]{1,0:T(8,128)S(1)}, u32[]{:S(2)}, u32[]{:S(2)}) collective-permute-start(f32[32,1024]{1,0:T(8,128)S(1)} %get-tuple-element.99), channel_id=1, source_target_pairs={{0,7},{1,0},{2,1},{3,2},{4,3},{5,4},{6,5},{7,6},{8,15},{9,8},{10,9... | collective-permute-start | bytes 393224 | tf_op jit(solution)/shard_map/ppermute | solution.py:18
  81.3 16.5 %collective-permute-start.14 = (f32[32,1024]{1,0:T(8,128)S(1)}, f32[32,1024]{1,0:T(8,128)S(1)}, u32[]{:S(2)}, u32[]{:S(2)}) collective-permute-start(f32[32,1024]{1,0:T(8,128)S(1)} %get-tuple-element.100), channel_id=1, source_target_pairs={{0,1},{1,2},{2,3},{3,4},{4,5},{5,6},{6,7},{7,0},{8,9},{9,10},{10,1... | collective-permute-start | bytes 393224 | tf_op jit(solution)/shard_map/ppermute | solution.py:18
  83.5 14.3 %collective-permute-start.15 = (f32[32,1024]{1,0:T(8,128)S(1)}, f32[32,1024]{1,0:T(8,128)S(1)}, u32[]{:S(2)}, u32[]{:S(2)}) collective-permute-start(f32[32,1024]{1,0:T(8,128)S(1)} %get-tuple-element.101), channel_id=1, source_target_pairs={{0,7},{1,0},{2,1},{3,2},{4,3},{5,4},{6,5},{7,6},{8,15},{9,8},{10,9... | collective-permute-start | bytes 393224 | tf_op jit(solution)/shard_map/ppermute | solution.py:18
  88.4 9.4 %collective-permute-start.16 = (f32[512]{0:T(512)S(1)}, f32[512]{0:T(512)S(1)}, u32[]{:S(2)}, u32[]{:S(2)}) collective-permute-start(f32[512]{0:T(512)S(1)} %add.141), channel_id=1, source_target_pairs={{0,64},{64,0},{1,65},{65,1},{2,66},{66,2},{3,67},{67,3},{4,68},{68... | collective-permute-start | bytes 6152 | tf_op jit(solution)/shard_map/ppermute | solution.py:22
  97.8 17.3 %collective-permute-start.20 = (f32[64,1024]{1,0:T(8,128)S(1)}, f32[64,1024]{1,0:T(8,128)S(1)}, u32[]{:S(2)}, u32[]{:S(2)}) collective-permute-start(f32[64,1024]{1,0:T(8,128)S(1)} %add_dynamic-update-slice_fusion), channel_id=1, source_target_pairs={{0,7},{1,0},{2,1},{3,2},{4,3},{5,4},{6,5},{7,6},{8,15},{9,8},{10,9... | collective-permute-start | bytes 786440 | tf_op jit(solution)/shard_map/ppermute | solution.py:18
  100.2 15.0 %collective-permute-start.19 = (f32[64,1024]{1,0:T(8,128)S(1)}, f32[64,1024]{1,0:T(8,128)S(1)}, u32[]{:S(2)}, u32[]{:S(2)}) collective-permute-start(f32[64,1024]{1,0:T(8,128)S(1)} %add_dynamic-update-slice_fusion.1), channel_id=1, source_target_pairs={{0,1},{1,2},{2,3},{3,4},{4,5},{5,6},{6,7},{7,0},{8,9},{9,10},{10,1... | collective-permute-start | bytes 786440 | tf_op jit(solution)/shard_map/ppermute | solution.py:18
  103.8 11.4 %collective-permute-start.18 = (f32[64,1024]{1,0:T(8,128)S(1)}, f32[64,1024]{1,0:T(8,128)S(1)}, u32[]{:S(2)}, u32[]{:S(2)}) collective-permute-start(f32[64,1024]{1,0:T(8,128)S(1)} %add_dynamic-update-slice_fusion.2), channel_id=1, source_target_pairs={{0,7},{1,0},{2,1},{3,2},{4,3},{5,4},{6,5},{7,6},{8,15},{9,8},{10,9... | collective-permute-start | bytes 786440 | tf_op jit(solution)/shard_map/ppermute | solution.py:18
  107.3 9.5 %collective-permute-start.17 = (f32[64,1024]{1,0:T(8,128)S(1)}, f32[64,1024]{1,0:T(8,128)S(1)}, u32[]{:S(2)}, u32[]{:S(2)}) collective-permute-start(f32[64,1024]{1,0:T(8,128)S(1)} %add_dynamic-update-slice_fusion.3), channel_id=1, source_target_pairs={{0,1},{1,2},{2,3},{3,4},{4,5},{5,6},{6,7},{7,0},{8,9},{9,10},{10,1... | collective-permute-start | bytes 786440 | tf_op jit(solution)/shard_map/ppermute | solution.py:18
  109.7 5.5 %collective-permute-start.21 = (f32[512]{0:T(512)S(1)}, f32[512]{0:T(512)S(1)}, u32[]{:S(2)}, u32[]{:S(2)}) collective-permute-start(f32[512]{0:T(512)S(1)} %add.142), channel_id=1, source_target_pairs={{0,128},{128,0},{256,384},{384,256},{1,129},{129,1},{257,385},{385... | collective-permute-start | bytes 6152 | tf_op jit(solution)/shard_map/ppermute | solution.py:22
  116.9 19.2 %collective-permute-start.25 = (f32[64,1024]{1,0:T(8,128)S(1)}, f32[64,1024]{1,0:T(8,128)S(1)}, u32[]{:S(2)}, u32[]{:S(2)}) collective-permute-start(f32[64,1024]{1,0:T(8,128)S(1)} %add.151), channel_id=1, source_target_pairs={{0,7},{1,0},{2,1},{3,2},{4,3},{5,4},{6,5},{7,6},{8,15},{9,8},{10,9... | collective-permute-start | bytes 786440 | tf_op jit(solution)/shard_map/ppermute | solution.py:18
  120.0 16.0 %collective-permute-start.24 = (f32[64,1024]{1,0:T(8,128)S(1)}, f32[64,1024]{1,0:T(8,128)S(1)}, u32[]{:S(2)}, u32[]{:S(2)}) collective-permute-start(f32[64,1024]{1,0:T(8,128)S(1)} %add.150), channel_id=1, source_target_pairs={{0,1},{1,2},{2,3},{3,4},{4,5},{5,6},{6,7},{7,0},{8,9},{9,10},{10,1... | collective-permute-start | bytes 786440 | tf_op jit(solution)/shard_map/ppermute | solution.py:18
  122.8 13.3 %collective-permute-start.23 = (f32[64,1024]{1,0:T(8,128)S(1)}, f32[64,1024]{1,0:T(8,128)S(1)}, u32[]{:S(2)}, u32[]{:S(2)}) collective-permute-start(f32[64,1024]{1,0:T(8,128)S(1)} %add.149), channel_id=1, source_target_pairs={{0,7},{1,0},{2,1},{3,2},{4,3},{5,4},{6,5},{7,6},{8,15},{9,8},{10,9... | collective-permute-start | bytes 786440 | tf_op jit(solution)/shard_map/ppermute | solution.py:18
  127.2 9.5 %collective-permute-start.22 = (f32[64,1024]{1,0:T(8,128)S(1)}, f32[64,1024]{1,0:T(8,128)S(1)}, u32[]{:S(2)}, u32[]{:S(2)}) collective-permute-start(f32[64,1024]{1,0:T(8,128)S(1)} %add.148), channel_id=1, source_target_pairs={{0,1},{1,2},{2,3},{3,4},{4,5},{5,6},{6,7},{7,0},{8,9},{9,10},{10,1... | collective-permute-start | bytes 786440 | tf_op jit(solution)/shard_map/ppermute | solution.py:18
  129.1 6.4 %collective-permute-start.26 = (f32[512]{0:T(512)S(1)}, f32[512]{0:T(512)S(1)}, u32[]{:S(2)}, u32[]{:S(2)}) collective-permute-start(f32[512]{0:T(512)S(1)} %add.147), channel_id=1, source_target_pairs={{0,256},{128,384},{256,0},{384,128},{1,257},{129,385},{257,1},{385... | collective-permute-start | bytes 6152 | tf_op jit(solution)/shard_map/ppermute | solution.py:22
  136.7 13.7 %collective-permute-start.30 = (f32[64,1024]{1,0:T(8,128)S(1)}, f32[64,1024]{1,0:T(8,128)S(1)}, u32[]{:S(2)}, u32[]{:S(2)}) collective-permute-start(f32[64,1024]{1,0:T(8,128)S(1)} %add.156), channel_id=1, source_target_pairs={{0,7},{1,0},{2,1},{3,2},{4,3},{5,4},{6,5},{7,6},{8,15},{9,8},{10,9... | collective-permute-start | bytes 786440 | tf_op jit(solution)/shard_map/ppermute | solution.py:18
  141.3 11.0 %collective-permute-start.29 = (f32[64,1024]{1,0:T(8,128)S(1)}, f32[64,1024]{1,0:T(8,128)S(1)}, u32[]{:S(2)}, u32[]{:S(2)}) collective-permute-start(f32[64,1024]{1,0:T(8,128)S(1)} %add.155), channel_id=1, source_target_pairs={{0,1},{1,2},{2,3},{3,4},{4,5},{5,6},{6,7},{7,0},{8,9},{9,10},{10,1... | collective-permute-start | bytes 786440 | tf_op jit(solution)/shard_map/ppermute | solution.py:18
  143.3 9.8 %collective-permute-start.28 = (f32[64,1024]{1,0:T(8,128)S(1)}, f32[64,1024]{1,0:T(8,128)S(1)}, u32[]{:S(2)}, u32[]{:S(2)}) collective-permute-start(f32[64,1024]{1,0:T(8,128)S(1)} %add.154), channel_id=1, source_target_pairs={{0,7},{1,0},{2,1},{3,2},{4,3},{5,4},{6,5},{7,6},{8,15},{9,8},{10,9... | collective-permute-start | bytes 786440 | tf_op jit(solution)/shard_map/ppermute | solution.py:18
  148.4 9.5 %collective-permute-start.27 = (f32[64,1024]{1,0:T(8,128)S(1)}, f32[64,1024]{1,0:T(8,128)S(1)}, u32[]{:S(2)}, u32[]{:S(2)}) collective-permute-start(f32[64,1024]{1,0:T(8,128)S(1)} %add.153), channel_id=1, source_target_pairs={{0,1},{1,2},{2,3},{3,4},{4,5},{5,6},{6,7},{7,0},{8,9},{9,10},{10,1... | collective-permute-start | bytes 786440 | tf_op jit(solution)/shard_map/ppermute | solution.py:18
  (3 other events, 43.3 us)
Sparse Core Ops, SparseCore 0:
  28.3 35.0 all-gather.2

commit v3 on v1

v3 whole, which is shorter than its diff:
```python
import jax
import jax.numpy as jnp
from jax import lax
from jax.experimental import pallas as pl
from jax.experimental.pallas import tpu as pltpu
from jax.sharding import Mesh, PartitionSpec as P

AXES = ("zl", "zh", "x", "core", "par")
SIZES = (4, 2, 4, 2, 8)
SAMPLES = AXES[:4]
LANES = 128
HOPS = (0, 1, 3, 2)
BUTTERFLY = (("core", 1), ("x", 1), ("x", 2), ("zh", 1), ("zl", 1), ("zl", 2))
VMEM = pltpu.CompilerParams(vmem_limit_bytes=24 * 1024 * 1024)


def shift(value, axis, by):
    count = lax.axis_size(axis)
    return lax.ppermute(value, axis, [(i, (i + by) % count) for i in range(count)])


def swap(value, axis, bit):
    return lax.ppermute(value, axis, [(i, i ^ bit) for i in range(lax.axis_size(axis))])


def halves(value):
    high = value.astype(jnp.bfloat16)
    low = (value - high.astype(jnp.float32)).astype(jnp.bfloat16)
    return high, low


def begin_kernel(data_ref, vector_ref, copy_ref, value_ref):
    copy_ref[...] = data_ref[...]
    value_ref[...] = lax.dot_general(
        vector_ref[...],
        data_ref[...],
        (((1,), (0,)), ((), ())),
        precision=lax.Precision.HIGHEST,
        preferred_element_type=jnp.float32,
    )


def begin(data, vector):
    local, params = data.shape
    return pl.pallas_call(
        begin_kernel,
        out_shape=[
            jax.ShapeDtypeStruct(data.shape, jnp.float32),
            jax.ShapeDtypeStruct((1, params), jnp.float32),
        ],
        compiler_params=VMEM,
        cost_estimate=pl.CostEstimate(
            flops=12 * data.size, bytes_accessed=8 * data.size, transcendentals=0
        ),
    )(data, vector.reshape(1, local))


def left_kernel(left_ref, high_ref, low_ref, rows):
    blocks, local, params = left_ref.shape
    for g in range(params // LANES):
        lanes = pl.ds(g * LANES, LANES)
        for a in range(blocks):
            rows[g, pl.ds(a, local, stride=blocks), :] = left_ref[a, :, lanes]
        high_ref[:, lanes], low_ref[:, lanes] = halves(rows[g])


def left_halves(left):
    blocks, local, params = left.shape
    shape = (blocks * local, params)
    return pl.pallas_call(
        left_kernel,
        out_shape=[jax.ShapeDtypeStruct(shape, jnp.bfloat16)] * 2,
        scratch_shapes=[pltpu.VMEM((params // LANES, blocks * local, LANES), jnp.float32)],
        compiler_params=VMEM,
        cost_estimate=pl.CostEstimate(
            flops=4 * left.size, bytes_accessed=8 * left.size, transcendentals=0
        ),
    )(left)


def product_kernel(place, high_ref, low_ref, near_ref, near_other_ref, far_ref, far_other_ref, out_ref, right):
    local = near_ref.shape[1]
    count = pl.num_programs(0) // 2
    core = place[2 * count]

    def gather(mine_ref, other_ref):
        right[pl.ds(pl.multiple_of(core * local, local), local), :] = mine_ref[0]
        right[pl.ds(pl.multiple_of((1 - core) * local, local), local), :] = other_ref[0]

    @pl.when(pl.program_id(0) < count)
    def _():
        gather(near_ref, near_other_ref)

    @pl.when(pl.program_id(0) >= count)
    def _():
        gather(far_ref, far_other_ref)

    high, low = halves(right[...])

    def dot(a, b):
        return lax.dot_general(
            a, b, (((1,), (1,)), ((), ())), preferred_element_type=jnp.float32
        )

    out_ref[...] = dot(high_ref[...], low) + dot(low_ref[...], high) + dot(high_ref[...], high)


def product(place, left, near, near_other, far, far_other):
    rows, params = left[0].shape
    count, local, _ = near.shape
    whole = pl.BlockSpec((rows, params), lambda j, place: (0, 0))
    first = pl.BlockSpec((1, local, params), lambda j, place: (jnp.minimum(j, count - 1), 0, 0))
    second = pl.BlockSpec((1, local, params), lambda j, place: (jnp.maximum(j - count, 0), 0, 0))
    columns = 4 * count * local
    return pl.pallas_call(
        product_kernel,
        grid_spec=pltpu.PrefetchScalarGridSpec(
            num_scalar_prefetch=1,
            grid=(2 * count,),
            in_specs=[whole, whole, first, first, second, second],
            out_specs=pl.BlockSpec((rows, 2 * local), lambda j, place: (0, place[j])),
            scratch_shapes=[pltpu.VMEM((2 * local, params), jnp.float32)],
        ),
        out_shape=jax.ShapeDtypeStruct((rows, columns), jnp.float32),
        compiler_params=pltpu.CompilerParams(vmem_limit_bytes=58 * 1024 * 1024),
        cost_estimate=pl.CostEstimate(
            flops=6 * rows * columns * params,
            bytes_accessed=4 * (rows * params + columns * params + rows * columns),
            transcendentals=0,
        ),
    )(place, *left, near, near_other, far, far_other)


def body(log_derivs, sample_vector):
    zh, x, core = (lax.axis_index(name) for name in ("zh", "x", "core"))
    x_count = lax.axis_size("x")
    left = lax.all_gather(log_derivs, "zl")
    blocks = left.shape[0]

    copy, value = begin(log_derivs, sample_vector)
    far = swap(copy, "zh", 1)
    near = jnp.stack([copy] + [shift(copy, "x", by) for by in HOPS[1:]])
    near_other = swap(near, "core", 1)
    far = jnp.stack([far] + [shift(far, "x", by) for by in HOPS[1:]])
    far_other = swap(far, "core", 1)

    source = [lax.rem(x + x_count - by, x_count) for by in HOPS]
    place = jnp.stack(
        [zh * x_count + s for s in source] + [(1 - zh) * x_count + s for s in source] + [core]
    ).astype(jnp.int32)
    total = product(place, left_halves(left), near, near_other, far, far_other)

    total, value = lax.optimization_barrier((total, value))
    summed = lax.psum_scatter(total, "par", scatter_dimension=0, tiled=True)
    for axis, bit in BUTTERFLY:
        value = value + swap(value, axis, bit)
    return (summed.reshape(-1, blocks, summed.shape[1]), value[0])


def solution(mesh):
    split = Mesh(mesh.devices.reshape(SIZES), AXES)
    in_specs = (P(SAMPLES, "par"), P(SAMPLES))
    out_specs = (P(("zh", "x", "core", "par"), None, "zl"), P("par"))
    return jax.shard_map(body, mesh=split, in_specs=in_specs, out_specs=out_specs, check_vma=False)
```

time: 183 us -> 148 us (0.81)
  the two profiles are of different devices: /device:TPU:417 before, /device:TPU:7 now
where the time goes in v3:
time: 148 us; the launch traced here: 146 us
  waiting for transfers between devices  56.1 us (38%)
  starting transfers between devices  55.7 us (38%)
  between operations  14.3 us (10%)
  Pallas kernels  10.9 us (7%)
  local copies, waits for them, and re-layouts  8.19 us (6%)
    ppermute x9, starting transfers between devices, swap(): lax.ppermute(value, axis, [(i, i ^ bit) for i in range(lax.axis_size(axis...  37.1 us
    reduce_scatter x1, waiting for transfers between devices, body(): summed = lax.psum_scatter(total, 'par', scatter_dimension=0, tiled=True)  24 us
    ppermute x6, starting transfers between devices, shift(): lax.ppermute(value, axis, [(i, (i + by) % count) for i in range(count)])  18.6 us
    all_gather x1, waiting for transfers between devices, body(): left = lax.all_gather(log_derivs, 'zl')  14.1 us
    ppermute x9, waiting for transfers between devices, swap(): lax.ppermute(value, axis, [(i, i ^ bit) for i in range(lax.axis_size(axis...  14 us
    pallas_call x1, Pallas kernels, product(): pl.pallas_call(product_kernel, grid_spec=pltpu.PrefetchScalarGridSpec(num...  10.2 us
    unnamed x16, local copies, waits for them, and re-layouts  5.55 us
    ppermute x6, waiting for transfers between devices, shift(): lax.ppermute(value, axis, [(i, (i + by) % count) for i in range(count)])  3.86 us
  transfers between devices with their start and end apart: 17, of which 9 were waited for; matrix products, arithmetic and copies ran while one was open for 1% of the time, Pallas kernels for 0%

profile of v3, /device:TPU:7, one launch (start us, length us, event | category | flops | bytes accessed | tf_op | source)
XLA Modules:
  0.0 145.9 jit_solution(13900588286738196890)
XLA Ops:
  7.2 0.9 copy-done.1
  9.1 10.6 %collective-permute-start.4 = (f32[128,512]{1,0:T(8,128)S(1)}, f32[128,512]{1,0:T(8,128)S(1)}, u32[]{:S(2)}, u32[]{:S(2)}) collective-permute-start(f32[128,512]{1,0:T(8,128)S(1)} %get-tuple-element.10), channel_id=1, source_target_pairs={{0,64},{64,0},{1,65},{65,1},{2,66},{66,2},{3,67},{67,3},{4,68},{68... | collective-permute-start | bytes 786440 | tf_op jit(solution)/shard_map/ppermute | solution.py:23
  19.7 3.0 %collective-permute-start.2 = (f32[128,512]{1,0:T(8,128)S(1)}, f32[128,512]{1,0:T(8,128)S(1)}, u32[]{:S(2)}, u32[]{:S(2)}) collective-permute-start(f32[128,512]{1,0:T(8,128)S(1)} %get-tuple-element.10), channel_id=1, source_target_pairs={{0,32},{16,48},{32,0},{48,16},{1,33},{17,49},{33,1},{49,17},{2,34}... | collective-permute-start | bytes 786440 | tf_op jit(solution)/shard_map/ppermute | solution.py:19
  22.8 1.9 %collective-permute-start.1 = (f32[128,512]{1,0:T(8,128)S(1)}, f32[128,512]{1,0:T(8,128)S(1)}, u32[]{:S(2)}, u32[]{:S(2)}) collective-permute-start(f32[128,512]{1,0:T(8,128)S(1)} %get-tuple-element.10), channel_id=1, source_target_pairs={{0,48},{16,0},{32,16},{48,32},{1,49},{17,1},{33,17},{49,33},{2,50}... | collective-permute-start | bytes 786440 | tf_op jit(solution)/shard_map/ppermute | solution.py:19
  24.7 4.6 %collective-permute-start = (f32[128,512]{1,0:T(8,128)S(1)}, f32[128,512]{1,0:T(8,128)S(1)}, u32[]{:S(2)}, u32[]{:S(2)}) collective-permute-start(f32[128,512]{1,0:T(8,128)S(1)} %get-tuple-element.10), channel_id=1, source_target_pairs={{0,16},{16,32},{32,48},{48,0},{1,17},{17,33},{33,49},{49,1},{2,18}... | collective-permute-start | bytes 786440 | tf_op jit(solution)/shard_map/ppermute | solution.py:19
  29.3 2.5 %collective-permute-start.7 = (f32[128,512]{1,0:T(8,128)S(1)}, f32[128,512]{1,0:T(8,128)S(1)}, u32[]{:S(2)}, u32[]{:S(2)}) collective-permute-start(f32[128,512]{1,0:T(8,128)S(1)} %collective-permute-done.4), channel_id=1, source_target_pairs={{0,32},{16,48},{32,0},{48,16},{1,33},{17,49},{33,1},{49,17},{2,34}... | collective-permute-start | bytes 786440 | tf_op jit(solution)/shard_map/ppermute | solution.py:19
  31.9 2.5 %collective-permute-start.6 = (f32[128,512]{1,0:T(8,128)S(1)}, f32[128,512]{1,0:T(8,128)S(1)}, u32[]{:S(2)}, u32[]{:S(2)}) collective-permute-start(f32[128,512]{1,0:T(8,128)S(1)} %collective-permute-done.4), channel_id=1, source_target_pairs={{0,48},{16,0},{32,16},{48,32},{1,49},{17,1},{33,17},{49,33},{2,50}... | collective-permute-start | bytes 786440 | tf_op jit(solution)/shard_map/ppermute | solution.py:19
  34.4 4.0 %collective-permute-start.5 = (f32[128,512]{1,0:T(8,128)S(1)}, f32[128,512]{1,0:T(8,128)S(1)}, u32[]{:S(2)}, u32[]{:S(2)}) collective-permute-start(f32[128,512]{1,0:T(8,128)S(1)} %collective-permute-done.4), channel_id=1, source_target_pairs={{0,16},{16,32},{32,48},{48,0},{1,17},{17,33},{33,49},{49,1},{2,18}... | collective-permute-start | bytes 786440 | tf_op jit(solution)/shard_map/ppermute | solution.py:19
  38.5 5.7 %collective-permute-start.3 = (f32[4,128,512]{2,1,0:T(8,128)S(1)}, f32[4,128,512]{2,1,0:T(8,128)S(1)}, u32[]{:S(2)}, u32[]{:S(2)}) collective-permute-start(f32[4,128,512]{2,1,0:T(8,128)S(1)} %pad_maximum_fusion.near_ref), channel_id=1, source_target_pairs={{0,8},{8,0},{1,9},{9,1},{2,10},{10,2},{3,11},{11,3},{4,12},{12,4},... | collective-permute-start | bytes 3145736 | tf_op jit(solution)/shard_map/ppermute | solution.py:23
  44.3 3.8 %collective-permute-done.6 = f32[128,512]{1,0:T(8,128)S(1)} collective-permute-done((f32[128,512]{1,0:T(8,128)S(1)}, f32[128,512]{1,0:T(8,128)S(1)}, u32[]{:S(2)}, u32[]{:S(2)}) %collective-permute-start.6) | collective-permute-done | bytes 262176 | tf_op jit(solution)/shard_map/ppermute | solution.py:19
  48.2 2.5 %collective-permute-start.8 = (f32[4,128,512]{2,1,0:T(8,128)S(1)}, f32[4,128,512]{2,1,0:T(8,128)}, u32[]{:S(2)}, u32[]{:S(2)}) collective-permute-start(f32[4,128,512]{2,1,0:T(8,128)S(1)} %pad_maximum_fusion.1.far_ref), channel_id=1, source_target_pairs={{0,8},{8,0},{1,9},{9,1},{2,10},{10,2},{3,11},{11,3},{4,12},{12,4},... | collective-permute-start | bytes 3145736 | tf_op jit(solution)/shard_map/ppermute | solution.py:23
  50.7 0.7 stack.69.place
  51.4 14.1 %all-gather.3.cloned.1.call-done = f32[512,512]{1,0:T(8,128)} async-done(((f32[128,512]{1,0:T(8,128)}), f32[512,512]{1,0:T(8,128)}) %all-gather.3.cloned.1.call-update) | async-done | bytes 1048592 | tf_op jit(solution)/shard_map/all_gather | solution.py:137
  65.5 1.2 copy-done
  67.2 0.8 copy-done.3
  68.0 0.9 copy-done.4
  68.9 1.1 copy-done.7
  69.9 10.2 %shard_map.43 = f32[512,2048]{1,0:T(8,128)} custom-call(s32[9]{0:T(128)} %stack.69.place, bf16[512,512]{1,0:T(8,128)(2,1)} %copy-done.3, bf16[512,512]{1,0:T(8,128)(2,1)} %copy-done.4, f32[4,128,512]{2,1,0:T(8,128)} %copy-done.5, f32[4,128,512]{2,1,0:T(8,128)} %copy-done.7, f32[4,128,512]{2,1,0:T(8,128)} %copy-done.6, ...), custom_call_target="tpu_custom_call" | custom-call | flops 3221225472 | bytes 9437184 | tf_op jit(solution)/shard_map/pallas_call | solution.py:115
  80.1 2.8 %collective-permute-start.9 = (f32[1,512]{1,0:T(1,128)S(1)}, f32[1,512]{1,0:T(1,128)S(1)}, u32[]{:S(2)}, u32[]{:S(2)}) collective-permute-start(f32[1,512]{1,0:T(1,128)S(1)} %get-tuple-element.13), channel_id=1, source_target_pairs={{0,8},{8,0},{1,9},{9,1},{2,10},{10,2},{3,11},{11,3},{4,12},{12,4},... | collective-permute-start | bytes 6152 | tf_op jit(solution)/shard_map/ppermute | solution.py:23
  82.9 0.8 collective-permute-done.9
  83.7 2.5 %collective-permute-start.10 = (f32[1,512]{1,0:T(1,128)S(1)}, f32[1,512]{1,0:T(1,128)S(1)}, u32[]{:S(2)}, u32[]{:S(2)}) collective-permute-start(f32[1,512]{1,0:T(1,128)S(1)} %add.68), channel_id=1, source_target_pairs={{0,16},{16,0},{32,48},{48,32},{1,17},{17,1},{33,49},{49,33},{2,18}... | collective-permute-start | bytes 6152 | tf_op jit(solution)/shard_map/ppermute | solution.py:23
  86.2 1.8 %collective-permute-done.10 = f32[1,512]{1,0:T(1,128)S(1)} collective-permute-done((f32[1,512]{1,0:T(1,128)S(1)}, f32[1,512]{1,0:T(1,128)S(1)}, u32[]{:S(2)}, u32[]{:S(2)}) %collective-permute-start.10) | collective-permute-done | bytes 2080 | tf_op jit(solution)/shard_map/ppermute | solution.py:23
  88.1 3.1 %collective-permute-start.11 = (f32[1,512]{1,0:T(1,128)S(1)}, f32[1,512]{1,0:T(1,128)S(1)}, u32[]{:S(2)}, u32[]{:S(2)}) collective-permute-start(f32[1,512]{1,0:T(1,128)S(1)} %add.69), channel_id=1, source_target_pairs={{0,32},{16,48},{32,0},{48,16},{1,33},{17,49},{33,1},{49,17},{2,34}... | collective-permute-start | bytes 6152 | tf_op jit(solution)/shard_map/ppermute | solution.py:23
  91.2 2.7 %collective-permute-done.11 = f32[1,512]{1,0:T(1,128)S(1)} collective-permute-done((f32[1,512]{1,0:T(1,128)S(1)}, f32[1,512]{1,0:T(1,128)S(1)}, u32[]{:S(2)}, u32[]{:S(2)}) %collective-permute-start.11) | collective-permute-done | bytes 2080 | tf_op jit(solution)/shard_map/ppermute | solution.py:23
  93.9 5.3 %collective-permute-start.12 = (f32[1,512]{1,0:T(1,128)S(1)}, f32[1,512]{1,0:T(1,128)S(1)}, u32[]{:S(2)}, u32[]{:S(2)}) collective-permute-start(f32[1,512]{1,0:T(1,128)S(1)} %add.70), channel_id=1, source_target_pairs={{0,64},{64,0},{1,65},{65,1},{2,66},{66,2},{3,67},{67,3},{4,68},{68... | collective-permute-start | bytes 6152 | tf_op jit(solution)/shard_map/ppermute | solution.py:23
  99.2 2.9 %collective-permute-done.12 = f32[1,512]{1,0:T(1,128)S(1)} collective-permute-done((f32[1,512]{1,0:T(1,128)S(1)}, f32[1,512]{1,0:T(1,128)S(1)}, u32[]{:S(2)}, u32[]{:S(2)}) %collective-permute-start.12) | collective-permute-done | bytes 2080 | tf_op jit(solution)/shard_map/ppermute | solution.py:23
  102.1 1.9 %collective-permute-start.13 = (f32[1,512]{1,0:T(1,128)S(1)}, f32[1,512]{1,0:T(1,128)S(1)}, u32[]{:S(2)}, u32[]{:S(2)}) collective-permute-start(f32[1,512]{1,0:T(1,128)S(1)} %add.71), channel_id=1, source_target_pairs={{0,128},{128,0},{256,384},{384,256},{1,129},{129,1},{257,385},{385... | collective-permute-start | bytes 6152 | tf_op jit(solution)/shard_map/ppermute | solution.py:23
  104.0 2.8 %collective-permute-done.13 = f32[1,512]{1,0:T(1,128)S(1)} collective-permute-done((f32[1,512]{1,0:T(1,128)S(1)}, f32[1,512]{1,0:T(1,128)S(1)}, u32[]{:S(2)}, u32[]{:S(2)}) %collective-permute-start.13) | collective-permute-done | bytes 2080 | tf_op jit(solution)/shard_map/ppermute | solution.py:23
  106.9 2.6 %collective-permute-start.14 = (f32[1,512]{1,0:T(1,128)S(1)}, f32[1,512]{1,0:T(1,128)S(1)}, u32[]{:S(2)}, u32[]{:S(2)}) collective-permute-start(f32[1,512]{1,0:T(1,128)S(1)} %add.72), channel_id=1, source_target_pairs={{0,256},{128,384},{256,0},{384,128},{1,257},{129,385},{257,1},{385... | collective-permute-start | bytes 6152 | tf_op jit(solution)/shard_map/ppermute | solution.py:23
  109.5 3.0 %collective-permute-done.14 = f32[1,512]{1,0:T(1,128)S(1)} collective-permute-done((f32[1,512]{1,0:T(1,128)S(1)}, f32[1,512]{1,0:T(1,128)S(1)}, u32[]{:S(2)}, u32[]{:S(2)}) %collective-permute-start.14) | collective-permute-done | bytes 2080 | tf_op jit(solution)/shard_map/ppermute | solution.py:23
  113.1 24.0 %reduce-scatter.2.cloned.1.call-done = f32[64,2048]{1,0:T(8,128)} async-done(((f32[512,2048]{1,0:T(8,128)}), f32[64,2048]{1,0:T(8,128)}) %reduce-scatter.2.cloned.1.call-update) | async-done | bytes 524304 | tf_op jit(solution)/shard_map/reduce_scatter | solution.py:154
  137.1 2.0 %reshape.11 = f32[16,4,2048]{2,1,0:T(4,128)} reshape(f32[64,2048]{1,0:T(8,128)} %reduce-scatter.2.cloned.1.call-done) | data formatting | bytes 1048576 | tf_op jit(solution)/shard_map/reshape | solution.py:157
  (33 shorter events, 2.2 us)
Async XLA Ops:
  7.2 58.3 %all-gather.3.cloned.1.call-start = ((), (), s32[]{:S(2)}) async-start(), calls=%async_computation.2 | async-start | bytes 1310720 | tf_op jit(solution)/shard_map/all_gather | solution.py:137
  7.2 1.0 copy-start.1
  8.2 0.7 copy-start.2
  9.1 20.3 %collective-permute-start.4 = (f32[128,512]{1,0:T(8,128)S(1)}, f32[128,512]{1,0:T(8,128)S(1)}, u32[]{:S(2)}, u32[]{:S(2)}) collective-permute-start(f32[128,512]{1,0:T(8,128)S(1)} %get-tuple-element.10), channel_id=1, source_target_pairs={{0,64},{64,0},{1,65},{65,1},{2,66},{66,2},{3,67},{67,3},{4,68},{68... | collective-permute-start | bytes 786440 | tf_op jit(solution)/shard_map/ppermute | solution.py:23
  19.7 14.7 %collective-permute-start.2 = (f32[128,512]{1,0:T(8,128)S(1)}, f32[128,512]{1,0:T(8,128)S(1)}, u32[]{:S(2)}, u32[]{:S(2)}) collective-permute-start(f32[128,512]{1,0:T(8,128)S(1)} %get-tuple-element.10), channel_id=1, source_target_pairs={{0,32},{16,48},{32,0},{48,16},{1,33},{17,49},{33,1},{49,17},{2,34}... | collective-permute-start | bytes 786440 | tf_op jit(solution)/shard_map/ppermute | solution.py:19
  22.8 15.7 %collective-permute-start.1 = (f32[128,512]{1,0:T(8,128)S(1)}, f32[128,512]{1,0:T(8,128)S(1)}, u32[]{:S(2)}, u32[]{:S(2)}) collective-permute-start(f32[128,512]{1,0:T(8,128)S(1)} %get-tuple-element.10), channel_id=1, source_target_pairs={{0,48},{16,0},{32,16},{48,32},{1,49},{17,1},{33,17},{49,33},{2,50}... | collective-permute-start | bytes 786440 | tf_op jit(solution)/shard_map/ppermute | solution.py:19
  24.7 13.7 %collective-permute-start = (f32[128,512]{1,0:T(8,128)S(1)}, f32[128,512]{1,0:T(8,128)S(1)}, u32[]{:S(2)}, u32[]{:S(2)}) collective-permute-start(f32[128,512]{1,0:T(8,128)S(1)} %get-tuple-element.10), channel_id=1, source_target_pairs={{0,16},{16,32},{32,48},{48,0},{1,17},{17,33},{33,49},{49,1},{2,18}... | collective-permute-start | bytes 786440 | tf_op jit(solution)/shard_map/ppermute | solution.py:19
  29.3 107.8 %reduce-scatter.2.cloned.1.call-start = ((), (), s32[]{:S(2)}) async-start(), calls=%async_computation.1 | async-start | bytes 4718592 | tf_op jit(solution)/shard_map/reduce_scatter | solution.py:154
  29.3 14.9 %collective-permute-start.7 = (f32[128,512]{1,0:T(8,128)S(1)}, f32[128,512]{1,0:T(8,128)S(1)}, u32[]{:S(2)}, u32[]{:S(2)}) collective-permute-start(f32[128,512]{1,0:T(8,128)S(1)} %collective-permute-done.4), channel_id=1, source_target_pairs={{0,32},{16,48},{32,0},{48,16},{1,33},{17,49},{33,1},{49,17},{2,34}... | collective-permute-start | bytes 786440 | tf_op jit(solution)/shard_map/ppermute | solution.py:19
  31.9 16.2 %collective-permute-start.6 = (f32[128,512]{1,0:T(8,128)S(1)}, f32[128,512]{1,0:T(8,128)S(1)}, u32[]{:S(2)}, u32[]{:S(2)}) collective-permute-start(f32[128,512]{1,0:T(8,128)S(1)} %collective-permute-done.4), channel_id=1, source_target_pairs={{0,48},{16,0},{32,16},{48,32},{1,49},{17,1},{33,17},{49,33},{2,50}... | collective-permute-start | bytes 786440 | tf_op jit(solution)/shard_map/ppermute | solution.py:19
  34.4 13.8 %collective-permute-start.5 = (f32[128,512]{1,0:T(8,128)S(1)}, f32[128,512]{1,0:T(8,128)S(1)}, u32[]{:S(2)}, u32[]{:S(2)}) collective-permute-start(f32[128,512]{1,0:T(8,128)S(1)} %collective-permute-done.4), channel_id=1, source_target_pairs={{0,16},{16,32},{32,48},{48,0},{1,17},{17,33},{33,49},{49,1},{2,18}... | collective-permute-start | bytes 786440 | tf_op jit(solution)/shard_map/ppermute | solution.py:19
  38.5 30.3 %copy-start.5 = (f32[4,128,512]{2,1,0:T(8,128)}, f32[4,128,512]{2,1,0:T(8,128)S(1)}, u32[]{:S(2)}) copy-start(f32[4,128,512]{2,1,0:T(8,128)S(1)} %pad_maximum_fusion.near_ref) | copy-start | bytes 3145732
  38.5 30.3 %collective-permute-start.3 = (f32[4,128,512]{2,1,0:T(8,128)S(1)}, f32[4,128,512]{2,1,0:T(8,128)S(1)}, u32[]{:S(2)}, u32[]{:S(2)}) collective-permute-start(f32[4,128,512]{2,1,0:T(8,128)S(1)} %pad_maximum_fusion.near_ref), channel_id=1, source_target_pairs={{0,8},{8,0},{1,9},{9,1},{2,10},{10,2},{3,11},{11,3},{4,12},{12,4},... | collective-permute-start | bytes 3145736 | tf_op jit(solution)/shard_map/ppermute | solution.py:23
  48.2 20.6 %copy-start.6 = (f32[4,128,512]{2,1,0:T(8,128)}, f32[4,128,512]{2,1,0:T(8,128)S(1)}, u32[]{:S(2)}) copy-start(f32[4,128,512]{2,1,0:T(8,128)S(1)} %pad_maximum_fusion.1.far_ref) | copy-start | bytes 3145732
  48.2 20.6 %collective-permute-start.8 = (f32[4,128,512]{2,1,0:T(8,128)S(1)}, f32[4,128,512]{2,1,0:T(8,128)}, u32[]{:S(2)}, u32[]{:S(2)}) collective-permute-start(f32[4,128,512]{2,1,0:T(8,128)S(1)} %pad_maximum_fusion.1.far_ref), channel_id=1, source_target_pairs={{0,8},{8,0},{1,9},{9,1},{2,10},{10,2},{3,11},{11,3},{4,12},{12,4},... | collective-permute-start | bytes 3145736 | tf_op jit(solution)/shard_map/ppermute | solution.py:23
  65.5 1.2 copy-start
  67.2 0.8 copy-start.3
  68.0 0.9 copy-start.4
  68.8 1.1 copy-start.7
  80.1 3.6 %collective-permute-start.9 = (f32[1,512]{1,0:T(1,128)S(1)}, f32[1,512]{1,0:T(1,128)S(1)}, u32[]{:S(2)}, u32[]{:S(2)}) collective-permute-start(f32[1,512]{1,0:T(1,128)S(1)} %get-tuple-element.13), channel_id=1, source_target_pairs={{0,8},{8,0},{1,9},{9,1},{2,10},{10,2},{3,11},{11,3},{4,12},{12,4},... | collective-permute-start | bytes 6152 | tf_op jit(solution)/shard_map/ppermute | solution.py:23
  83.7 4.3 %collective-permute-start.10 = (f32[1,512]{1,0:T(1,128)S(1)}, f32[1,512]{1,0:T(1,128)S(1)}, u32[]{:S(2)}, u32[]{:S(2)}) collective-permute-start(f32[1,512]{1,0:T(1,128)S(1)} %add.68), channel_id=1, source_target_pairs={{0,16},{16,0},{32,48},{48,32},{1,17},{17,1},{33,49},{49,33},{2,18}... | collective-permute-start | bytes 6152 | tf_op jit(solution)/shard_map/ppermute | solution.py:23
  88.1 5.8 %collective-permute-start.11 = (f32[1,512]{1,0:T(1,128)S(1)}, f32[1,512]{1,0:T(1,128)S(1)}, u32[]{:S(2)}, u32[]{:S(2)}) collective-permute-start(f32[1,512]{1,0:T(1,128)S(1)} %add.69), channel_id=1, source_target_pairs={{0,32},{16,48},{32,0},{48,16},{1,33},{17,49},{33,1},{49,17},{2,34}... | collective-permute-start | bytes 6152 | tf_op jit(solution)/shard_map/ppermute | solution.py:23
  93.9 8.2 %collective-permute-start.12 = (f32[1,512]{1,0:T(1,128)S(1)}, f32[1,512]{1,0:T(1,128)S(1)}, u32[]{:S(2)}, u32[]{:S(2)}) collective-permute-start(f32[1,512]{1,0:T(1,128)S(1)} %add.70), channel_id=1, source_target_pairs={{0,64},{64,0},{1,65},{65,1},{2,66},{66,2},{3,67},{67,3},{4,68},{68... | collective-permute-start | bytes 6152 | tf_op jit(solution)/shard_map/ppermute | solution.py:23
  102.1 4.7 %collective-permute-start.13 = (f32[1,512]{1,0:T(1,128)S(1)}, f32[1,512]{1,0:T(1,128)S(1)}, u32[]{:S(2)}, u32[]{:S(2)}) collective-permute-start(f32[1,512]{1,0:T(1,128)S(1)} %add.71), channel_id=1, source_target_pairs={{0,128},{128,0},{256,384},{384,256},{1,129},{129,1},{257,385},{385... | collective-permute-start | bytes 6152 | tf_op jit(solution)/shard_map/ppermute | solution.py:23
  106.9 5.6 %collective-permute-start.14 = (f32[1,512]{1,0:T(1,128)S(1)}, f32[1,512]{1,0:T(1,128)S(1)}, u32[]{:S(2)}, u32[]{:S(2)}) collective-permute-start(f32[1,512]{1,0:T(1,128)S(1)} %add.72), channel_id=1, source_target_pairs={{0,256},{128,384},{256,0},{384,128},{1,257},{129,385},{257,1},{385... | collective-permute-start | bytes 6152 | tf_op jit(solution)/shard_map/ppermute | solution.py:23
Sparse Core Ops, SparseCore 0:
  29.4 36.0 all-gather.2
  80.3 56.7 reduce-scatter.1

commit v4 on v3

--- a/solution.py
+++ b/solution.py
@@ -1,3 +1,5 @@
+import functools
+
 import jax
 import jax.numpy as jnp
 from jax import lax
@@ -78,62 +80,64 @@
     )(left)
 
 
-def product_kernel(place, high_ref, low_ref, near_ref, near_other_ref, far_ref, far_other_ref, out_ref, right):
-    local = near_ref.shape[1]
-    count = pl.num_programs(0) // 2
-    core = place[2 * count]
-
-    def gather(mine_ref, other_ref):
-        right[pl.ds(pl.multiple_of(core * local, local), local), :] = mine_ref[0]
-        right[pl.ds(pl.multiple_of((1 - core) * local, local), local), :] = other_ref[0]
-
-    @pl.when(pl.program_id(0) < count)
-    def _():
-        gather(near_ref, near_other_ref)
-
-    @pl.when(pl.program_id(0) >= count)
-    def _():
-        gather(far_ref, far_other_ref)
-
-    high, low = halves(right[...])
+def product_kernel(is_far, high_ref, low_ref, mine_ref, other_ref, *rest):
+    out_hbm, right, value, sent = rest[-4:]
+    count, local, _ = mine_ref.shape
+    x, core = lax.axis_index("x"), lax.axis_index("core")
+    half = lax.axis_index("zh")
+    if is_far:
+        half = 1 - half
+    mine = pl.ds(pl.multiple_of(core * local, local), local)
+    other = pl.ds(pl.multiple_of((1 - core) * local, local), local)
 
     def dot(a, b):
         return lax.dot_general(
             a, b, (((1,), (1,)), ((), ())), preferred_element_type=jnp.float32
         )
 
-    out_ref[...] = dot(high_ref[...], low) + dot(low_ref[...], high) + dot(high_ref[...], high)
+    copies = []
+    for n in range(count):
+        right[n % 2, mine, :] = mine_ref[n]
+        right[n % 2, other, :] = other_ref[n]
+        high, low = halves(right[n % 2])
+        value[n] = dot(high_ref[...], low) + dot(low_ref[...], high) + dot(high_ref[...], high)
+        source = lax.rem(x + (count - HOPS[n]), count)
+        first = pl.multiple_of((half * count + source) * 2 * local, 2 * local)
+        copies.append(
+            pltpu.make_async_copy(value.at[n], out_hbm.at[:, pl.ds(first, 2 * local)], sent.at[n])
+        )
+        copies[-1].start()
+    for copy in copies:
+        copy.wait()
 
 
-def product(place, left, near, near_other, far, far_other):
+def product(left, mine, other, total):
     rows, params = left[0].shape
-    count, local, _ = near.shape
-    whole = pl.BlockSpec((rows, params), lambda j, place: (0, 0))
-    first = pl.BlockSpec((1, local, params), lambda j, place: (jnp.minimum(j, count - 1), 0, 0))
-    second = pl.BlockSpec((1, local, params), lambda j, place: (jnp.maximum(j - count, 0), 0, 0))
+    count, local, _ = mine.shape
     columns = 4 * count * local
+    whole = pl.BlockSpec(memory_space=pltpu.VMEM)
+    hbm = pl.BlockSpec(memory_space=pltpu.HBM)
     return pl.pallas_call(
-        product_kernel,
-        grid_spec=pltpu.PrefetchScalarGridSpec(
-            num_scalar_prefetch=1,
-            grid=(2 * count,),
-            in_specs=[whole, whole, first, first, second, second],
-            out_specs=pl.BlockSpec((rows, 2 * local), lambda j, place: (0, place[j])),
-            scratch_shapes=[pltpu.VMEM((2 * local, params), jnp.float32)],
-        ),
-        out_shape=jax.ShapeDtypeStruct((rows, columns), jnp.float32),
-        compiler_params=pltpu.CompilerParams(vmem_limit_bytes=58 * 1024 * 1024),
+        functools.partial(product_kernel, bool(total)),
+        in_specs=[whole] * 4 + [hbm] * len(total),
+        out_specs=hbm,
+        out_shape=pltpu.HBM((rows, columns), jnp.float32),
+        input_output_aliases={4: 0} if total else {},
+        scratch_shapes=[
+            pltpu.VMEM((2, 2 * local, params), jnp.float32),
+            pltpu.VMEM((count, rows, 2 * local), jnp.float32),
+            pltpu.SemaphoreType.DMA((count,)),
+        ],
+        compiler_params=VMEM,
         cost_estimate=pl.CostEstimate(
-            flops=6 * rows * columns * params,
-            bytes_accessed=4 * (rows * params + columns * params + rows * columns),
+            flops=3 * rows * columns * params,
+            bytes_accessed=2 * (rows * params + columns * params + rows * columns),
             transcendentals=0,
         ),
-    )(place, *left, near, near_other, far, far_other)
+    )(*left, mine, other, *total)
 
 
 def body(log_derivs, sample_vector):
-    zh, x, core = (lax.axis_index(name) for name in ("zh", "x", "core"))
-    x_count = lax.axis_size("x")
     left = lax.all_gather(log_derivs, "zl")
     blocks = left.shape[0]
 
@@ -142,13 +146,12 @@
     near = jnp.stack([copy] + [shift(copy, "x", by) for by in HOPS[1:]])
     near_other = swap(near, "core", 1)
     far = jnp.stack([far] + [shift(far, "x", by) for by in HOPS[1:]])
+    far, left = lax.optimization_barrier((far, left))
     far_other = swap(far, "core", 1)
 
-    source = [lax.rem(x + x_count - by, x_count) for by in HOPS]
-    place = jnp.stack(
-        [zh * x_count + s for s in source] + [(1 - zh) * x_count + s for s in source] + [core]
-    ).astype(jnp.int32)
-    total = product(place, left_halves(left), near, near_other, far, far_other)
+    left = left_halves(left)
+    total = product(left, near, near_other, ())
+    total = product(left, far, far_other, (total,))
 
     total, value = lax.optimization_barrier((total, value))
     summed = lax.psum_scatter(total, "par", scatter_dimension=0, tiled=True)

time: 148 us -> 132 us (0.89)
  waiting for transfers between devices: 56.1 us -> 46.4 us
  Pallas kernels: 10.9 us -> 7.29 us
  local copies, waits for them, and re-layouts: 8.19 us -> 4.8 us
  starting transfers between devices: 55.7 us -> 57.5 us
    all_gather x1, waiting for transfers between devices: 14.1 us -> 2.14 us  [body(): left = lax.all_gather(log_derivs, 'zl')]
    pallas_call x1 -> x2, Pallas kernels: 10.2 us -> 6.61 us  [product(): pl.pallas_call(functools.partial(product_kernel, bool(total)), in_specs=[...]
    reduce_scatter x1, waiting for transfers between devices: 24 us -> 27.6 us  [body(): summed = lax.psum_scatter(total, 'par', scatter_dimension=0, tiled=True)]
    unnamed x16 -> x6, local copies, waits for them, and re-layouts: 5.55 us -> 2.82 us
    ppermute x9, waiting for transfers between devices: 14 us -> 12.1 us  [swap(): lax.ppermute(value, axis, [(i, i ^ bit) for i in range(lax.axis_size(axis...]
    ppermute x9, starting transfers between devices: 37.1 us -> 38.8 us  [swap(): lax.ppermute(value, axis, [(i, i ^ bit) for i in range(lax.axis_size(axis...]
  transfers between devices with their start and end apart: 17 -> 17, of which waited for: 9 -> 9; matrix products, arithmetic and copies ran while one was open for 1% -> 1% of each run, Pallas kernels for 0% -> 3%
where the time goes in v4:
time: 132 us; the launch traced here: 131 us
  starting transfers between devices  57.5 us (44%)
  waiting for transfers between devices  46.4 us (35%)
  between operations  14.3 us (11%)
  Pallas kernels  7.29 us (6%)
  local copies, waits for them, and re-layouts  4.8 us (4%)
    ppermute x9, starting transfers between devices, swap(): lax.ppermute(value, axis, [(i, i ^ bit) for i in range(lax.axis_size(axis...  38.8 us
    reduce_scatter x1, waiting for transfers between devices, body(): summed = lax.psum_scatter(total, 'par', scatter_dimension=0, tiled=True)  27.6 us
    ppermute x6, starting transfers between devices, shift(): lax.ppermute(value, axis, [(i, (i + by) % count) for i in range(count)])  18.6 us
    ppermute x9, waiting for transfers between devices, swap(): lax.ppermute(value, axis, [(i, i ^ bit) for i in range(lax.axis_size(axis...  12.1 us
    pallas_call x2, Pallas kernels, product(): pl.pallas_call(functools.partial(product_kernel, bool(total)), in_specs=[...  6.61 us
    ppermute x6, waiting for transfers between devices, shift(): lax.ppermute(value, axis, [(i, (i + by) % count) for i in range(count)])  3.87 us
    unnamed x6, local copies, waits for them, and re-layouts  2.82 us
  transfers between devices with their start and end apart: 17, of which 9 were waited for; matrix products, arithmetic and copies ran while one was open for 1% of the time, Pallas kernels for 3%

profile of v4, /device:TPU:7, one launch (start us, length us, event | category | flops | bytes accessed | tf_op | source)
XLA Modules:
  0.0 131.0 jit_solution(9112614886923164405)
XLA Ops:
  7.2 0.7 all-gather.3.cloned.1.call-update
  8.0 0.9 copy-done.1
  8.9 0.7 copy-done.2
  9.8 10.6 %collective-permute-start = (f32[128,512]{1,0:T(8,128)S(1)}, f32[128,512]{1,0:T(8,128)S(1)}, u32[]{:S(2)}, u32[]{:S(2)}) collective-permute-start(f32[128,512]{1,0:T(8,128)S(1)} %get-tuple-element.10), channel_id=1, source_target_pairs={{0,64},{64,0},{1,65},{65,1},{2,66},{66,2},{3,67},{67,3},{4,68},{68... | collective-permute-start | bytes 786440 | tf_op jit(solution)/shard_map/ppermute | solution.py:25
  20.4 3.0 %collective-permute-start.7 = (f32[128,512]{1,0:T(8,128)S(1)}, f32[128,512]{1,0:T(8,128)S(1)}, u32[]{:S(2)}, u32[]{:S(2)}) collective-permute-start(f32[128,512]{1,0:T(8,128)S(1)} %get-tuple-element.10), channel_id=1, source_target_pairs={{0,32},{16,48},{32,0},{48,16},{1,33},{17,49},{33,1},{49,17},{2,34}... | collective-permute-start | bytes 786440 | tf_op jit(solution)/shard_map/ppermute | solution.py:21
  23.5 1.9 %collective-permute-start.6 = (f32[128,512]{1,0:T(8,128)S(1)}, f32[128,512]{1,0:T(8,128)S(1)}, u32[]{:S(2)}, u32[]{:S(2)}) collective-permute-start(f32[128,512]{1,0:T(8,128)S(1)} %get-tuple-element.10), channel_id=1, source_target_pairs={{0,48},{16,0},{32,16},{48,32},{1,49},{17,1},{33,17},{49,33},{2,50}... | collective-permute-start | bytes 786440 | tf_op jit(solution)/shard_map/ppermute | solution.py:21
  25.4 4.6 %collective-permute-start.5 = (f32[128,512]{1,0:T(8,128)S(1)}, f32[128,512]{1,0:T(8,128)S(1)}, u32[]{:S(2)}, u32[]{:S(2)}) collective-permute-start(f32[128,512]{1,0:T(8,128)S(1)} %get-tuple-element.10), channel_id=1, source_target_pairs={{0,16},{16,32},{32,48},{48,0},{1,17},{17,33},{33,49},{49,1},{2,18}... | collective-permute-start | bytes 786440 | tf_op jit(solution)/shard_map/ppermute | solution.py:21
  30.0 2.5 %collective-permute-start.3 = (f32[128,512]{1,0:T(8,128)S(1)}, f32[128,512]{1,0:T(8,128)S(1)}, u32[]{:S(2)}, u32[]{:S(2)}) collective-permute-start(f32[128,512]{1,0:T(8,128)S(1)} %collective-permute-done), channel_id=1, source_target_pairs={{0,32},{16,48},{32,0},{48,16},{1,33},{17,49},{33,1},{49,17},{2,34}... | collective-permute-start | bytes 786440 | tf_op jit(solution)/shard_map/ppermute | solution.py:21
  32.6 2.5 %collective-permute-start.2 = (f32[128,512]{1,0:T(8,128)S(1)}, f32[128,512]{1,0:T(8,128)S(1)}, u32[]{:S(2)}, u32[]{:S(2)}) collective-permute-start(f32[128,512]{1,0:T(8,128)S(1)} %collective-permute-done), channel_id=1, source_target_pairs={{0,48},{16,0},{32,16},{48,32},{1,49},{17,1},{33,17},{49,33},{2,50}... | collective-permute-start | bytes 786440 | tf_op jit(solution)/shard_map/ppermute | solution.py:21
  35.0 4.0 %collective-permute-start.1 = (f32[128,512]{1,0:T(8,128)S(1)}, f32[128,512]{1,0:T(8,128)S(1)}, u32[]{:S(2)}, u32[]{:S(2)}) collective-permute-start(f32[128,512]{1,0:T(8,128)S(1)} %collective-permute-done), channel_id=1, source_target_pairs={{0,16},{16,32},{32,48},{48,0},{1,17},{17,33},{33,49},{49,1},{2,18}... | collective-permute-start | bytes 786440 | tf_op jit(solution)/shard_map/ppermute | solution.py:21
  39.2 5.8 %collective-permute-start.8 = (f32[4,128,512]{2,1,0:T(8,128)S(1)}, f32[4,128,512]{2,1,0:T(8,128)S(1)}, u32[]{:S(2)}, u32[]{:S(2)}) collective-permute-start(f32[4,128,512]{2,1,0:T(8,128)S(1)} %pad_maximum_fusion.1.mine_ref), channel_id=1, source_target_pairs={{0,8},{8,0},{1,9},{9,1},{2,10},{10,2},{3,11},{11,3},{4,12},{12,4},... | collective-permute-start | bytes 3145736 | tf_op jit(solution)/shard_map/ppermute | solution.py:25
  45.0 3.9 %collective-permute-done.2 = f32[128,512]{1,0:T(8,128)S(1)} collective-permute-done((f32[128,512]{1,0:T(8,128)S(1)}, f32[128,512]{1,0:T(8,128)S(1)}, u32[]{:S(2)}, u32[]{:S(2)}) %collective-permute-start.2) | collective-permute-done | bytes 262176 | tf_op jit(solution)/shard_map/ppermute | solution.py:21
  49.0 2.1 %all-gather.3.cloned.1.call-done = f32[512,512]{1,0:T(8,128)} async-done(((f32[128,512]{1,0:T(8,128)}), f32[512,512]{1,0:T(8,128)}) %all-gather.3.cloned.1.call-update) | async-done | bytes 1048592 | tf_op jit(solution)/shard_map/all_gather | solution.py:141
  51.1 2.8 %collective-permute-start.4 = (f32[4,128,512]{2,1,0:T(8,128)S(1)}, f32[4,128,512]{2,1,0:T(8,128)S(1)}, u32[]{:S(2)}, u32[]{:S(2)}) collective-permute-start(f32[4,128,512]{2,1,0:T(8,128)S(1)} %pad_maximum_fusion.mine_ref), channel_id=1, source_target_pairs={{0,8},{8,0},{1,9},{9,1},{2,10},{10,2},{3,11},{11,3},{4,12},{12,4},... | collective-permute-start | bytes 3145736 | tf_op jit(solution)/shard_map/ppermute | solution.py:25
  53.9 1.2 copy-done
  55.6 3.3 %shard_map.43.rest_0_ = f32[512,2048]{1,0:T(8,128)} custom-call(bf16[512,512]{1,0:T(8,128)(2,1)S(1)} %get-tuple-element.12.high_ref, bf16[512,512]{1,0:T(8,128)(2,1)S(1)} %get-tuple-element.13.low_ref, f32[4,128,512]{2,1,0:T(8,128)S(1)} %pad_maximum_fusion.1.mine_ref, f32[4,128,512]{2,1,0:T(8,128)S(1)} %collective-permute-done.8.other_ref), custom_call_target="tpu_custom_call" | custom-call | flops 1610612736 | bytes 4718592 | tf_op jit(solution)/shard_map/pallas_call | solution.py:120
  58.9 3.3 %shard_map.44 = f32[512,2048]{1,0:T(8,128)} custom-call(bf16[512,512]{1,0:T(8,128)(2,1)S(1)} %get-tuple-element.12.high_ref, bf16[512,512]{1,0:T(8,128)(2,1)S(1)} %get-tuple-element.13.low_ref, f32[4,128,512]{2,1,0:T(8,128)S(1)} %pad_maximum_fusion.mine_ref, f32[4,128,512]{2,1,0:T(8,128)S(1)} %collective-permute-done.4.other_ref, ...), custom_call_target="tpu_custom_call", output_to_operand_aliasing={{}: (4, {})} | custom-call | flops 1610612736 | bytes 4718592 | tf_op jit(solution)/shard_map/pallas_call | solution.py:120
  62.2 1.9 %collective-permute-start.9 = (f32[1,512]{1,0:T(1,128)S(1)}, f32[1,512]{1,0:T(1,128)S(1)}, u32[]{:S(2)}, u32[]{:S(2)}) collective-permute-start(f32[1,512]{1,0:T(1,128)S(1)} %get-tuple-element.17), channel_id=1, source_target_pairs={{0,8},{8,0},{1,9},{9,1},{2,10},{10,2},{3,11},{11,3},{4,12},{12,4},... | collective-permute-start | bytes 6152 | tf_op jit(solution)/shard_map/ppermute | solution.py:25
  64.2 1.1 collective-permute-done.9
  65.3 2.4 %collective-permute-start.10 = (f32[1,512]{1,0:T(1,128)S(1)}, f32[1,512]{1,0:T(1,128)S(1)}, u32[]{:S(2)}, u32[]{:S(2)}) collective-permute-start(f32[1,512]{1,0:T(1,128)S(1)} %add.20), channel_id=1, source_target_pairs={{0,16},{16,0},{32,48},{48,32},{1,17},{17,1},{33,49},{49,33},{2,18}... | collective-permute-start | bytes 6152 | tf_op jit(solution)/shard_map/ppermute | solution.py:25
  67.7 1.9 %collective-permute-done.10 = f32[1,512]{1,0:T(1,128)S(1)} collective-permute-done((f32[1,512]{1,0:T(1,128)S(1)}, f32[1,512]{1,0:T(1,128)S(1)}, u32[]{:S(2)}, u32[]{:S(2)}) %collective-permute-start.10) | collective-permute-done | bytes 2080 | tf_op jit(solution)/shard_map/ppermute | solution.py:25
  69.6 3.1 %collective-permute-start.11 = (f32[1,512]{1,0:T(1,128)S(1)}, f32[1,512]{1,0:T(1,128)S(1)}, u32[]{:S(2)}, u32[]{:S(2)}) collective-permute-start(f32[1,512]{1,0:T(1,128)S(1)} %add.21), channel_id=1, source_target_pairs={{0,32},{16,48},{32,0},{48,16},{1,33},{17,49},{33,1},{49,17},{2,34}... | collective-permute-start | bytes 6152 | tf_op jit(solution)/shard_map/ppermute | solution.py:25
  72.7 2.7 %collective-permute-done.11 = f32[1,512]{1,0:T(1,128)S(1)} collective-permute-done((f32[1,512]{1,0:T(1,128)S(1)}, f32[1,512]{1,0:T(1,128)S(1)}, u32[]{:S(2)}, u32[]{:S(2)}) %collective-permute-start.11) | collective-permute-done | bytes 2080 | tf_op jit(solution)/shard_map/ppermute | solution.py:25
  75.4 6.0 %collective-permute-start.12 = (f32[1,512]{1,0:T(1,128)S(1)}, f32[1,512]{1,0:T(1,128)S(1)}, u32[]{:S(2)}, u32[]{:S(2)}) collective-permute-start(f32[1,512]{1,0:T(1,128)S(1)} %add.22), channel_id=1, source_target_pairs={{0,64},{64,0},{1,65},{65,1},{2,66},{66,2},{3,67},{67,3},{4,68},{68... | collective-permute-start | bytes 6152 | tf_op jit(solution)/shard_map/ppermute | solution.py:25
  81.5 2.2 %collective-permute-done.12 = f32[1,512]{1,0:T(1,128)S(1)} collective-permute-done((f32[1,512]{1,0:T(1,128)S(1)}, f32[1,512]{1,0:T(1,128)S(1)}, u32[]{:S(2)}, u32[]{:S(2)}) %collective-permute-start.12) | collective-permute-done | bytes 2080 | tf_op jit(solution)/shard_map/ppermute | solution.py:25
  83.7 2.7 %collective-permute-start.13 = (f32[1,512]{1,0:T(1,128)S(1)}, f32[1,512]{1,0:T(1,128)S(1)}, u32[]{:S(2)}, u32[]{:S(2)}) collective-permute-start(f32[1,512]{1,0:T(1,128)S(1)} %add.23), channel_id=1, source_target_pairs={{0,128},{128,0},{256,384},{384,256},{1,129},{129,1},{257,385},{385... | collective-permute-start | bytes 6152 | tf_op jit(solution)/shard_map/ppermute | solution.py:25
  86.3 2.0 %collective-permute-done.13 = f32[1,512]{1,0:T(1,128)S(1)} collective-permute-done((f32[1,512]{1,0:T(1,128)S(1)}, f32[1,512]{1,0:T(1,128)S(1)}, u32[]{:S(2)}, u32[]{:S(2)}) %collective-permute-start.13) | collective-permute-done | bytes 2080 | tf_op jit(solution)/shard_map/ppermute | solution.py:25
  88.4 3.4 %collective-permute-start.14 = (f32[1,512]{1,0:T(1,128)S(1)}, f32[1,512]{1,0:T(1,128)S(1)}, u32[]{:S(2)}, u32[]{:S(2)}) collective-permute-start(f32[1,512]{1,0:T(1,128)S(1)} %add.24), channel_id=1, source_target_pairs={{0,256},{128,384},{256,0},{384,128},{1,257},{129,385},{257,1},{385... | collective-permute-start | bytes 6152 | tf_op jit(solution)/shard_map/ppermute | solution.py:25
  91.8 2.2 %collective-permute-done.14 = f32[1,512]{1,0:T(1,128)S(1)} collective-permute-done((f32[1,512]{1,0:T(1,128)S(1)}, f32[1,512]{1,0:T(1,128)S(1)}, u32[]{:S(2)}, u32[]{:S(2)}) %collective-permute-start.14) | collective-permute-done | bytes 2080 | tf_op jit(solution)/shard_map/ppermute | solution.py:25
  94.0 0.6 add.25
  94.6 27.6 %reduce-scatter.2.cloned.1.call-done = f32[64,2048]{1,0:T(8,128)} async-done(((f32[512,2048]{1,0:T(8,128)}), f32[64,2048]{1,0:T(8,128)}) %reduce-scatter.2.cloned.1.call-update) | async-done | bytes 524304 | tf_op jit(solution)/shard_map/reduce_scatter | solution.py:157
  122.1 2.0 %reshape.11 = f32[16,4,2048]{2,1,0:T(4,128)} reshape(f32[64,2048]{1,0:T(8,128)} %reduce-scatter.2.cloned.1.call-done) | data formatting | bytes 1048576 | tf_op jit(solution)/shard_map/reshape | solution.py:160
  (23 shorter events, 1.0 us)
Async XLA Ops:
  7.2 43.9 %all-gather.3.cloned.1.call-start = ((), (), s32[]{:S(2)}) async-start(), calls=%async_computation.2 | async-start | bytes 1310720 | tf_op jit(solution)/shard_map/all_gather | solution.py:141
  7.9 114.2 %reduce-scatter.2.cloned.1.call-start = ((), (), s32[]{:S(2)}) async-start(), calls=%async_computation.1 | async-start | bytes 4718592 | tf_op jit(solution)/shard_map/reduce_scatter | solution.py:157
  7.9 1.0 copy-start.1
  8.9 0.7 copy-start.2
  9.8 20.2 %collective-permute-start = (f32[128,512]{1,0:T(8,128)S(1)}, f32[128,512]{1,0:T(8,128)S(1)}, u32[]{:S(2)}, u32[]{:S(2)}) collective-permute-start(f32[128,512]{1,0:T(8,128)S(1)} %get-tuple-element.10), channel_id=1, source_target_pairs={{0,64},{64,0},{1,65},{65,1},{2,66},{66,2},{3,67},{67,3},{4,68},{68... | collective-permute-start | bytes 786440 | tf_op jit(solution)/shard_map/ppermute | solution.py:25
  20.4 14.6 %collective-permute-start.7 = (f32[128,512]{1,0:T(8,128)S(1)}, f32[128,512]{1,0:T(8,128)S(1)}, u32[]{:S(2)}, u32[]{:S(2)}) collective-permute-start(f32[128,512]{1,0:T(8,128)S(1)} %get-tuple-element.10), channel_id=1, source_target_pairs={{0,32},{16,48},{32,0},{48,16},{1,33},{17,49},{33,1},{49,17},{2,34}... | collective-permute-start | bytes 786440 | tf_op jit(solution)/shard_map/ppermute | solution.py:21
  23.5 15.6 %collective-permute-start.6 = (f32[128,512]{1,0:T(8,128)S(1)}, f32[128,512]{1,0:T(8,128)S(1)}, u32[]{:S(2)}, u32[]{:S(2)}) collective-permute-start(f32[128,512]{1,0:T(8,128)S(1)} %get-tuple-element.10), channel_id=1, source_target_pairs={{0,48},{16,0},{32,16},{48,32},{1,49},{17,1},{33,17},{49,33},{2,50}... | collective-permute-start | bytes 786440 | tf_op jit(solution)/shard_map/ppermute | solution.py:21
  25.4 13.7 %collective-permute-start.5 = (f32[128,512]{1,0:T(8,128)S(1)}, f32[128,512]{1,0:T(8,128)S(1)}, u32[]{:S(2)}, u32[]{:S(2)}) collective-permute-start(f32[128,512]{1,0:T(8,128)S(1)} %get-tuple-element.10), channel_id=1, source_target_pairs={{0,16},{16,32},{32,48},{48,0},{1,17},{17,33},{33,49},{49,1},{2,18}... | collective-permute-start | bytes 786440 | tf_op jit(solution)/shard_map/ppermute | solution.py:21
  30.0 15.0 %collective-permute-start.3 = (f32[128,512]{1,0:T(8,128)S(1)}, f32[128,512]{1,0:T(8,128)S(1)}, u32[]{:S(2)}, u32[]{:S(2)}) collective-permute-start(f32[128,512]{1,0:T(8,128)S(1)} %collective-permute-done), channel_id=1, source_target_pairs={{0,32},{16,48},{32,0},{48,16},{1,33},{17,49},{33,1},{49,17},{2,34}... | collective-permute-start | bytes 786440 | tf_op jit(solution)/shard_map/ppermute | solution.py:21
  32.6 16.3 %collective-permute-start.2 = (f32[128,512]{1,0:T(8,128)S(1)}, f32[128,512]{1,0:T(8,128)S(1)}, u32[]{:S(2)}, u32[]{:S(2)}) collective-permute-start(f32[128,512]{1,0:T(8,128)S(1)} %collective-permute-done), channel_id=1, source_target_pairs={{0,48},{16,0},{32,16},{48,32},{1,49},{17,1},{33,17},{49,33},{2,50}... | collective-permute-start | bytes 786440 | tf_op jit(solution)/shard_map/ppermute | solution.py:21
  35.0 13.8 %collective-permute-start.1 = (f32[128,512]{1,0:T(8,128)S(1)}, f32[128,512]{1,0:T(8,128)S(1)}, u32[]{:S(2)}, u32[]{:S(2)}) collective-permute-start(f32[128,512]{1,0:T(8,128)S(1)} %collective-permute-done), channel_id=1, source_target_pairs={{0,16},{16,32},{32,48},{48,0},{1,17},{17,33},{33,49},{49,1},{2,18}... | collective-permute-start | bytes 786440 | tf_op jit(solution)/shard_map/ppermute | solution.py:21
  39.2 16.4 %collective-permute-start.8 = (f32[4,128,512]{2,1,0:T(8,128)S(1)}, f32[4,128,512]{2,1,0:T(8,128)S(1)}, u32[]{:S(2)}, u32[]{:S(2)}) collective-permute-start(f32[4,128,512]{2,1,0:T(8,128)S(1)} %pad_maximum_fusion.1.mine_ref), channel_id=1, source_target_pairs={{0,8},{8,0},{1,9},{9,1},{2,10},{10,2},{3,11},{11,3},{4,12},{12,4},... | collective-permute-start | bytes 3145736 | tf_op jit(solution)/shard_map/ppermute | solution.py:25
  51.1 7.8 %collective-permute-start.4 = (f32[4,128,512]{2,1,0:T(8,128)S(1)}, f32[4,128,512]{2,1,0:T(8,128)S(1)}, u32[]{:S(2)}, u32[]{:S(2)}) collective-permute-start(f32[4,128,512]{2,1,0:T(8,128)S(1)} %pad_maximum_fusion.mine_ref), channel_id=1, source_target_pairs={{0,8},{8,0},{1,9},{9,1},{2,10},{10,2},{3,11},{11,3},{4,12},{12,4},... | collective-permute-start | bytes 3145736 | tf_op jit(solution)/shard_map/ppermute | solution.py:25
  53.9 1.2 copy-start
  62.2 3.1 %collective-permute-start.9 = (f32[1,512]{1,0:T(1,128)S(1)}, f32[1,512]{1,0:T(1,128)S(1)}, u32[]{:S(2)}, u32[]{:S(2)}) collective-permute-start(f32[1,512]{1,0:T(1,128)S(1)} %get-tuple-element.17), channel_id=1, source_target_pairs={{0,8},{8,0},{1,9},{9,1},{2,10},{10,2},{3,11},{11,3},{4,12},{12,4},... | collective-permute-start | bytes 6152 | tf_op jit(solution)/shard_map/ppermute | solution.py:25
  65.3 4.3 %collective-permute-start.10 = (f32[1,512]{1,0:T(1,128)S(1)}, f32[1,512]{1,0:T(1,128)S(1)}, u32[]{:S(2)}, u32[]{:S(2)}) collective-permute-start(f32[1,512]{1,0:T(1,128)S(1)} %add.20), channel_id=1, source_target_pairs={{0,16},{16,0},{32,48},{48,32},{1,17},{17,1},{33,49},{49,33},{2,18}... | collective-permute-start | bytes 6152 | tf_op jit(solution)/shard_map/ppermute | solution.py:25
  69.6 5.8 %collective-permute-start.11 = (f32[1,512]{1,0:T(1,128)S(1)}, f32[1,512]{1,0:T(1,128)S(1)}, u32[]{:S(2)}, u32[]{:S(2)}) collective-permute-start(f32[1,512]{1,0:T(1,128)S(1)} %add.21), channel_id=1, source_target_pairs={{0,32},{16,48},{32,0},{48,16},{1,33},{17,49},{33,1},{49,17},{2,34}... | collective-permute-start | bytes 6152 | tf_op jit(solution)/shard_map/ppermute | solution.py:25
  75.4 8.2 %collective-permute-start.12 = (f32[1,512]{1,0:T(1,128)S(1)}, f32[1,512]{1,0:T(1,128)S(1)}, u32[]{:S(2)}, u32[]{:S(2)}) collective-permute-start(f32[1,512]{1,0:T(1,128)S(1)} %add.22), channel_id=1, source_target_pairs={{0,64},{64,0},{1,65},{65,1},{2,66},{66,2},{3,67},{67,3},{4,68},{68... | collective-permute-start | bytes 6152 | tf_op jit(solution)/shard_map/ppermute | solution.py:25
  83.7 4.7 %collective-permute-start.13 = (f32[1,512]{1,0:T(1,128)S(1)}, f32[1,512]{1,0:T(1,128)S(1)}, u32[]{:S(2)}, u32[]{:S(2)}) collective-permute-start(f32[1,512]{1,0:T(1,128)S(1)} %add.23), channel_id=1, source_target_pairs={{0,128},{128,0},{256,384},{384,256},{1,129},{129,1},{257,385},{385... | collective-permute-start | bytes 6152 | tf_op jit(solution)/shard_map/ppermute | solution.py:25
  88.4 5.6 %collective-permute-start.14 = (f32[1,512]{1,0:T(1,128)S(1)}, f32[1,512]{1,0:T(1,128)S(1)}, u32[]{:S(2)}, u32[]{:S(2)}) collective-permute-start(f32[1,512]{1,0:T(1,128)S(1)} %add.24), channel_id=1, source_target_pairs={{0,256},{128,384},{256,0},{384,128},{1,257},{129,385},{257,1},{385... | collective-permute-start | bytes 6152 | tf_op jit(solution)/shard_map/ppermute | solution.py:25
Sparse Core Ops, SparseCore 0:
  10.1 40.9 all-gather.2
  62.3 59.7 reduce-scatter.1

commit v5 on v4

v5 whole, which is shorter than its diff:
```python
import functools

import jax
import jax.numpy as jnp
from jax import lax
from jax.experimental import pallas as pl
from jax.experimental.pallas import tpu as pltpu
from jax.sharding import Mesh, PartitionSpec as P

AXES = ("zl", "zh", "x", "core", "par")
SIZES = (4, 2, 4, 2, 8)
SAMPLES = AXES[:4]
LANES = 128
EXTRA = 8
HOPS = (0, 1, 3, 2)
PLACES = (4, 3, -3, 2, -2, 1, -1, 0)
STEPPED = 3
VMEM = pltpu.CompilerParams(vmem_limit_bytes=24 * 1024 * 1024)
IN_VMEM = pl.BlockSpec(memory_space=pltpu.VMEM)
IN_HBM = pl.BlockSpec(memory_space=pltpu.HBM)


def shift(value, axis, by):
    count = lax.axis_size(axis)
    return lax.ppermute(value, axis, [(i, (i + by) % count) for i in range(count)])


def swap(value, axis, bit):
    return lax.ppermute(value, axis, [(i, i ^ bit) for i in range(lax.axis_size(axis))])


def cost(flops, elements):
    return pl.CostEstimate(flops=flops, bytes_accessed=4 * elements, transcendentals=0)


def halves(value):
    high = value.astype(jnp.bfloat16)
    low = (value - high.astype(jnp.float32)).astype(jnp.bfloat16)
    return high, low


def begin_kernel(data_ref, vector_ref, out_ref):
    local, params = data_ref.shape
    out_ref[:local, :] = data_ref[...]
    term = lax.dot_general(
        vector_ref[...],
        data_ref[...],
        (((1,), (0,)), ((), ())),
        precision=lax.Precision.HIGHEST,
        preferred_element_type=jnp.float32,
    )
    out_ref[local:, :] = jnp.broadcast_to(term, (EXTRA, params))


def begin(data, vector):
    local, params = data.shape
    return pl.pallas_call(
        begin_kernel,
        out_shape=jax.ShapeDtypeStruct((local + EXTRA, params), jnp.float32),
        compiler_params=VMEM,
        cost_estimate=cost(12 * data.size, 2 * data.size),
    )(data, vector.reshape(1, local))


def left_kernel(left_ref, high_ref, low_ref, rows):
    blocks, local, params = left_ref.shape
    for g in range(params // LANES):
        lanes = pl.ds(g * LANES, LANES)
        for a in range(blocks):
            rows[g, pl.ds(a, local, stride=blocks), :] = left_ref[a, :, lanes]
        high_ref[:, lanes], low_ref[:, lanes] = halves(rows[g])


def left_halves(left):
    blocks, local, params = left.shape
    shape = (blocks * local, params)
    return pl.pallas_call(
        left_kernel,
        out_shape=[jax.ShapeDtypeStruct(shape, jnp.bfloat16)] * 2,
        scratch_shapes=[pltpu.VMEM((params // LANES, blocks * local, LANES), jnp.float32)],
        compiler_params=VMEM,
        cost_estimate=cost(4 * left.size, 2 * left.size),
    )(left)


def block_product(high_ref, low_ref, mine_ref, other_ref, n, right):
    local = right.shape[0] // 2
    core = lax.axis_index("core")
    right[pl.ds(pl.multiple_of(core * local, local), local), :] = mine_ref[n, :local, :]
    right[pl.ds(pl.multiple_of((1 - core) * local, local), local), :] = other_ref[n, :local, :]
    high, low = halves(right[...])

    def dot(a, b):
        return lax.dot_general(
            a, b, (((1,), (1,)), ((), ())), preferred_element_type=jnp.float32
        )

    return dot(high_ref[...], low) + dot(low_ref[...], high) + dot(high_ref[...], high)


def product_kernel(high_ref, low_ref, near_ref, near_other_ref, far_ref, far_other_ref, *rest):
    (*outs, total_hbm, term_ref), (right, value, steps, sent) = rest[:-4], rest[-4:]
    count, places = near_ref.shape[0], len(PLACES)
    local = near_ref.shape[1] - EXTRA
    width = value.shape[2]
    copies = []
    for m, n in enumerate(range(STEPPED, 2 * count)):
        pair = (near_ref, near_other_ref) if n < count else (far_ref, far_other_ref)
        value[m] = block_product(high_ref, low_ref, *pair, n % count, right.at[m % 2])
        copies.append(
            pltpu.make_async_copy(
                value.at[m], total_hbm.at[:, pl.ds(m * width, width)], sent.at[m]
            )
        )
        copies[-1].start()

    for n in range(STEPPED):
        steps[:, n * width : (n + 1) * width] = block_product(
            high_ref, low_ref, near_ref, near_other_ref, n, right.at[n % 2]
        )
    par = lax.axis_index("par")
    rows = steps.shape[0] // places
    for n, to in enumerate(PLACES):
        first = pl.multiple_of(lax.rem(par + (places + to), places) * rows, rows)
        if n:
            outs[n + 1][...] = steps[pl.ds(first, rows), :]
        else:
            outs[0][...] = steps[pl.ds(first, rows // 2), :]
            outs[1][...] = steps[pl.ds(pl.multiple_of(first + rows // 2, rows // 2), rows // 2), :]

    def pairs(ref):
        row = [ref[HOPS.index(by), pl.ds(local, 1), :] for by in range(count)]
        return (row[0] + row[2]) + (row[1] + row[3])

    near_term = pairs(near_ref) + pairs(near_other_ref)
    far_term = pairs(far_ref) + pairs(far_other_ref)
    term_ref[...] = near_term + far_term
    for copy in copies:
        copy.wait()


def product(left, near, near_other, far, far_other):
    total_rows, params = left[0].shape
    count, height, _ = near.shape
    width = 2 * (height - EXTRA)
    blocks = 2 * count - STEPPED
    rows = total_rows // len(PLACES)
    heights = (rows // 2,) * 2 + (rows,) * (len(PLACES) - 1)
    *parts, total, term = pl.pallas_call(
        product_kernel,
        in_specs=[IN_VMEM] * 6,
        out_specs=[IN_VMEM] * len(heights) + [IN_HBM, IN_VMEM],
        out_shape=[jax.ShapeDtypeStruct((h, STEPPED * width), jnp.float32) for h in heights]
        + [
            pltpu.HBM((total_rows, blocks * width), jnp.float32),
            jax.ShapeDtypeStruct((1, params), jnp.float32),
        ],
        scratch_shapes=[
            pltpu.VMEM((2, width, params), jnp.float32),
            pltpu.VMEM((blocks, total_rows, width), jnp.float32),
            pltpu.VMEM((total_rows, STEPPED * width), jnp.float32),
            pltpu.SemaphoreType.DMA((blocks,)),
        ],
        compiler_params=VMEM,
        cost_estimate=cost(12 * total_rows * count * width * params, 2 * count * width * (params + total_rows)),
    )(*left, near, near_other, far, far_other)
    return parts, total, term


def write_kernel(first_block, *rest):
    out_hbm, value, sent = rest[-3:]
    terms = rest[:-3][: 3 if first_block == 0 else 1]
    count = len(HOPS)
    x, zh = lax.axis_index("x"), lax.axis_index("zh")
    blocks, _, _, width = value.shape
    copies = []
    for m in range(blocks):
        columns = pl.ds(m * width, width)
        total = terms[0][:, columns]
        if len(terms) == 3:
            total = total + (terms[1][:, columns] + terms[2][:, columns])
        value[m] = total.reshape(value.shape[1:])
        n = first_block + m
        half = zh if n < count else 1 - zh
        source = lax.rem(x + (count - HOPS[n % count]), count)
        first = pl.multiple_of((half * count + source) * width, width)
        copies.append(
            pltpu.make_async_copy(value.at[m], out_hbm.at[:, :, pl.ds(first, width)], sent.at[m])
        )
        copies[-1].start()
    for copy in copies:
        copy.wait()


def write(first_block, terms, width, blocks, done):
    rows, columns = terms[0].shape
    shape = (rows // blocks, blocks)
    return pl.pallas_call(
        functools.partial(write_kernel, first_block),
        in_specs=[IN_VMEM] * len(terms) + [IN_HBM] * len(done),
        out_specs=IN_HBM,
        out_shape=pltpu.HBM(shape + (2 * len(HOPS) * width,), jnp.float32),
        input_output_aliases={len(terms): 0} if done else {},
        scratch_shapes=[
            pltpu.VMEM((columns // width,) + shape + (width,), jnp.float32),
            pltpu.SemaphoreType.DMA((columns // width,)),
        ],
        compiler_params=VMEM,
        cost_estimate=cost(2 * rows * columns, (len(terms) + 1) * rows * columns),
    )(*terms, *done)


def body(log_derivs, sample_vector):
    left = lax.all_gather(log_derivs, "zl")
    blocks, local, _ = left.shape

    own = begin(log_derivs, sample_vector)
    far = swap(own, "zh", 1)
    near = jnp.stack([own] + [shift(own, "x", by) for by in HOPS[1:]])
    near_other = swap(near, "core", 1)
    far = jnp.stack([far] + [shift(far, "x", by) for by in HOPS[1:]])
    far, left = lax.optimization_barrier((far, left))
    far_other = swap(far, "core", 1)

    left = left_halves(left)
    parts, total, value = product(left, near, near_other, far, far_other)
    summed = lax.psum_scatter(total, "par", scatter_dimension=0, tiled=True)
    half = parts[0].shape[0]
    going = [parts[0], parts[1]]
    for step in range(1, 5):
        came = [shift(going[0], "par", 1), shift(going[1], "par", -1)]
        if step in (2, 3):
            value = value + swap(value, "zl", step - 1)
            came, value = lax.optimization_barrier((came, value))
        if step == 1:
            going = [parts[2].at[:half].add(came[0]), parts[3].at[half:].add(came[1])]
        elif step < 4:
            going = [parts[2 * step] + came[0], parts[2 * step + 1] + came[1]]
    done = write(0, [parts[8]] + came, 2 * local, blocks, ())
    summed, done = lax.optimization_barrier((summed, done))
    return (write(STEPPED, [summed], 2 * local, blocks, (done,)), value[0])


def solution(mesh):
    split = Mesh(mesh.devices.reshape(SIZES), AXES)
    in_specs = (P(SAMPLES, "par"), P(SAMPLES))
    out_specs = (P(("zh", "x", "core", "par"), None, "zl"), P("par"))
    return jax.shard_map(body, mesh=split, in_specs=in_specs, out_specs=out_specs, check_vma=False)
```

time: 132 us -> 134 us (1.015)
  the two profiles are of different devices: /device:TPU:7 before, /device:TPU:64 now
where the time goes in v5:
time: 134 us; the launch traced here: 133 us
  starting transfers between devices  66.7 us (50%)
  waiting for transfers between devices  35.3 us (26%)
  between operations  14.4 us (11%)
  local copies, waits for them, and re-layouts  8.18 us (6%)
  Pallas kernels  7.27 us (5%)
    ppermute x14, starting transfers between devices, shift(): lax.ppermute(value, axis, [(i, (i + by) % count) for i in range(count)])  49 us
    ppermute x14, waiting for transfers between devices, shift(): lax.ppermute(value, axis, [(i, (i + by) % count) for i in range(count)])  20.2 us
    ppermute x5, starting transfers between devices, swap(): lax.ppermute(value, axis, [(i, i ^ bit) for i in range(lax.axis_size(axis...  17.7 us
    ppermute x5, waiting for transfers between devices, swap(): lax.ppermute(value, axis, [(i, i ^ bit) for i in range(lax.axis_size(axis...  14.3 us
    unnamed x20, local copies, waits for them, and re-layouts  8.18 us
    pallas_call x1, Pallas kernels, product(): pl.pallas_call(product_kernel, in_specs=[IN_VMEM] * 6, out_specs=[IN_VMEM...  5.12 us
  transfers between devices with their start and end apart: 21, of which 12 were waited for; matrix products, arithmetic and copies ran while one was open for 1% of the time, Pallas kernels for 1%

profile of v5, /device:TPU:64, one launch (start us, length us, event | category | flops | bytes accessed | tf_op | source)
XLA Modules:
  0.0 132.7 jit_solution(14065030930223236178)
XLA Ops:
  9.8 10.0 %collective-permute-start = (f32[136,512]{1,0:T(8,128)S(1)}, f32[136,512]{1,0:T(8,128)S(1)}, u32[]{:S(2)}, u32[]{:S(2)}) collective-permute-start(f32[136,512]{1,0:T(8,128)S(1)} %shard_map.41), channel_id=1, source_target_pairs={{0,64},{64,0},{1,65},{65,1},{2,66},{66,2},{3,67},{67,3},{4,68},{68... | collective-permute-start | bytes 835592 | tf_op jit(solution)/shard_map/ppermute | solution.py:29
  19.8 4.9 %collective-permute-start.6 = (f32[136,512]{1,0:T(8,128)S(1)}, f32[136,512]{1,0:T(8,128)S(1)}, u32[]{:S(2)}, u32[]{:S(2)}) collective-permute-start(f32[136,512]{1,0:T(8,128)S(1)} %shard_map.41), channel_id=1, source_target_pairs={{0,32},{16,48},{32,0},{48,16},{1,33},{17,49},{33,1},{49,17},{2,34}... | collective-permute-start | bytes 835592 | tf_op jit(solution)/shard_map/ppermute | solution.py:25
  24.8 3.0 %collective-permute-start.5 = (f32[136,512]{1,0:T(8,128)S(1)}, f32[136,512]{1,0:T(8,128)S(1)}, u32[]{:S(2)}, u32[]{:S(2)}) collective-permute-start(f32[136,512]{1,0:T(8,128)S(1)} %shard_map.41), channel_id=1, source_target_pairs={{0,48},{16,0},{32,16},{48,32},{1,49},{17,1},{33,17},{49,33},{2,50}... | collective-permute-start | bytes 835592 | tf_op jit(solution)/shard_map/ppermute | solution.py:25
  27.8 2.8 %collective-permute-start.4 = (f32[136,512]{1,0:T(8,128)S(1)}, f32[136,512]{1,0:T(8,128)S(1)}, u32[]{:S(2)}, u32[]{:S(2)}) collective-permute-start(f32[136,512]{1,0:T(8,128)S(1)} %shard_map.41), channel_id=1, source_target_pairs={{0,16},{16,32},{32,48},{48,0},{1,17},{17,33},{33,49},{49,1},{2,18}... | collective-permute-start | bytes 835592 | tf_op jit(solution)/shard_map/ppermute | solution.py:25
  30.6 6.2 %collective-permute-done = f32[136,512]{1,0:T(8,128)S(1)} collective-permute-done((f32[136,512]{1,0:T(8,128)S(1)}, f32[136,512]{1,0:T(8,128)S(1)}, u32[]{:S(2)}, u32[]{:S(2)}) %collective-permute-start) | collective-permute-done | bytes 278560 | tf_op jit(solution)/shard_map/ppermute | solution.py:29
  36.8 5.1 %collective-permute-start.3 = (f32[136,512]{1,0:T(8,128)S(1)}, f32[136,512]{1,0:T(8,128)S(1)}, u32[]{:S(2)}, u32[]{:S(2)}) collective-permute-start(f32[136,512]{1,0:T(8,128)S(1)} %collective-permute-done), channel_id=1, source_target_pairs={{0,32},{16,48},{32,0},{48,16},{1,33},{17,49},{33,1},{49,17},{2,34}... | collective-permute-start | bytes 835592 | tf_op jit(solution)/shard_map/ppermute | solution.py:25
  41.9 3.0 %collective-permute-start.2 = (f32[136,512]{1,0:T(8,128)S(1)}, f32[136,512]{1,0:T(8,128)S(1)}, u32[]{:S(2)}, u32[]{:S(2)}) collective-permute-start(f32[136,512]{1,0:T(8,128)S(1)} %collective-permute-done), channel_id=1, source_target_pairs={{0,48},{16,0},{32,16},{48,32},{1,49},{17,1},{33,17},{49,33},{2,50}... | collective-permute-start | bytes 835592 | tf_op jit(solution)/shard_map/ppermute | solution.py:25
  44.9 2.9 %collective-permute-start.1 = (f32[136,512]{1,0:T(8,128)S(1)}, f32[136,512]{1,0:T(8,128)S(1)}, u32[]{:S(2)}, u32[]{:S(2)}) collective-permute-start(f32[136,512]{1,0:T(8,128)S(1)} %collective-permute-done), channel_id=1, source_target_pairs={{0,16},{16,32},{32,48},{48,0},{1,17},{17,33},{33,49},{49,1},{2,18}... | collective-permute-start | bytes 835592 | tf_op jit(solution)/shard_map/ppermute | solution.py:25
  47.9 1.9 %collective-permute-start.7 = (f32[4,136,512]{2,1,0:T(8,128)S(1)}, f32[4,136,512]{2,1,0:T(8,128)S(1)}, u32[]{:S(2)}, u32[]{:S(2)}) collective-permute-start(f32[4,136,512]{2,1,0:T(8,128)S(1)} %pad_maximum_fusion.1.near_ref), channel_id=1, source_target_pairs={{0,8},{8,0},{1,9},{9,1},{2,10},{10,2},{3,11},{11,3},{4,12},{12,4},... | collective-permute-start | bytes 3342344 | tf_op jit(solution)/shard_map/ppermute | solution.py:29
  50.4 4.2 %collective-permute-done.1 = f32[136,512]{1,0:T(8,128)S(1)} collective-permute-done((f32[136,512]{1,0:T(8,128)S(1)}, f32[136,512]{1,0:T(8,128)S(1)}, u32[]{:S(2)}, u32[]{:S(2)}) %collective-permute-start.1) | collective-permute-done | bytes 278560 | tf_op jit(solution)/shard_map/ppermute | solution.py:25
  54.7 1.9 %collective-permute-start.8 = (f32[4,136,512]{2,1,0:T(8,128)S(1)}, f32[4,136,512]{2,1,0:T(8,128)S(1)}, u32[]{:S(2)}, u32[]{:S(2)}) collective-permute-start(f32[4,136,512]{2,1,0:T(8,128)S(1)} %pad_maximum_fusion.far_ref), channel_id=1, source_target_pairs={{0,8},{8,0},{1,9},{9,1},{2,10},{10,2},{3,11},{11,3},{4,12},{12,4},... | collective-permute-start | bytes 3342344 | tf_op jit(solution)/shard_map/ppermute | solution.py:29
  56.6 1.2 copy-done.1
  58.3 1.0 copy-done.6
  59.4 1.2 copy-done.7
  60.6 5.1 %shard_map.43 = (f32[32,768]{1,0:T(8,128)S(1)}, f32[32,768]{1,0:T(8,128)S(1)}, f32[64,768]{1,0:T(8,128)S(1)}, f32[64,768]{1,0:T(8,128)S(1)}, f32[64,768]{1,0:T(8...) custom-call(bf16[512,512]{1,0:T(8,128)(2,1)S(1)} %get-tuple-element., ...), custom_call_target="tpu_custom_call" | custom-call | flops 3221225472 | bytes 8388608 | tf_op jit(solution)/shard_map/pallas_call | solution.py:149
  67.9 5.7 %collective-permute-start.11 = (f32[32,768]{1,0:T(8,128)S(1)}, f32[32,768]{1,0:T(8,128)S(1)}, u32[]{:S(2)}, u32[]{:S(2)}) collective-permute-start(f32[32,768]{1,0:T(8,128)S(1)} %copy-done.9), channel_id=1, source_target_pairs={{0,7},{1,0},{2,1},{3,2},{4,3},{5,4},{6,5},{7,6},{8,15},{9,8},{10,9... | collective-permute-start | bytes 294920 | tf_op jit(solution)/shard_map/ppermute | solution.py:25
  73.6 1.9 %collective-permute-start.9 = (f32[32,768]{1,0:T(8,128)S(1)}, f32[32,768]{1,0:T(8,128)S(1)}, u32[]{:S(2)}, u32[]{:S(2)}) collective-permute-start(f32[32,768]{1,0:T(8,128)S(1)} %get-tuple-element.58), channel_id=1, source_target_pairs={{0,1},{1,2},{2,3},{3,4},{4,5},{5,6},{6,7},{7,0},{8,9},{9,10},{10,1... | collective-permute-start | bytes 294920 | tf_op jit(solution)/shard_map/ppermute | solution.py:25
  76.3 5.6 %collective-permute-start.12 = (f32[64,768]{1,0:T(8,128)S(1)}, f32[64,768]{1,0:T(8,128)S(1)}, u32[]{:S(2)}, u32[]{:S(2)}) collective-permute-start(f32[64,768]{1,0:T(8,128)S(1)} %add_dynamic-update-slice_fusion), channel_id=1, source_target_pairs={{0,7},{1,0},{2,1},{3,2},{4,3},{5,4},{6,5},{7,6},{8,15},{9,8},{10,9... | collective-permute-start | bytes 589832 | tf_op jit(solution)/shard_map/ppermute | solution.py:25
  82.0 1.9 %collective-permute-start.10 = (f32[64,768]{1,0:T(8,128)S(1)}, f32[64,768]{1,0:T(8,128)S(1)}, u32[]{:S(2)}, u32[]{:S(2)}) collective-permute-start(f32[64,768]{1,0:T(8,128)S(1)} %add_dynamic-update-slice_fusion.1), channel_id=1, source_target_pairs={{0,1},{1,2},{2,3},{3,4},{4,5},{5,6},{6,7},{7,0},{8,9},{9,10},{10,1... | collective-permute-start | bytes 589832 | tf_op jit(solution)/shard_map/ppermute | solution.py:25
  83.9 1.9 %collective-permute-start.13 = (f32[1,512]{1,0:T(1,128)S(1)}, f32[1,512]{1,0:T(1,128)S(1)}, u32[]{:S(2)}, u32[]{:S(2)}) collective-permute-start(f32[1,512]{1,0:T(1,128)S(1)} %get-tuple-element.61), channel_id=1, source_target_pairs={{0,128},{128,0},{256,384},{384,256},{1,129},{129,1},{257,385},{385... | collective-permute-start | bytes 6152 | tf_op jit(solution)/shard_map/ppermute | solution.py:29
  85.8 3.6 %collective-permute-done.13 = f32[1,512]{1,0:T(1,128)S(1)} collective-permute-done((f32[1,512]{1,0:T(1,128)S(1)}, f32[1,512]{1,0:T(1,128)S(1)}, u32[]{:S(2)}, u32[]{:S(2)}) %collective-permute-start.13) | collective-permute-done | bytes 2080 | tf_op jit(solution)/shard_map/ppermute | solution.py:29
  90.1 6.3 %collective-permute-done.10 = f32[64,768]{1,0:T(8,128)S(1)} collective-permute-done((f32[64,768]{1,0:T(8,128)S(1)}, f32[64,768]{1,0:T(8,128)S(1)}, u32[]{:S(2)}, u32[]{:S(2)}) %collective-permute-start.10) | collective-permute-done | bytes 196640 | tf_op jit(solution)/shard_map/ppermute | solution.py:25
  96.5 1.9 %collective-permute-start.15 = (f32[64,768]{1,0:T(8,128)S(1)}, f32[64,768]{1,0:T(8,128)S(1)}, u32[]{:S(2)}, u32[]{:S(2)}) collective-permute-start(f32[64,768]{1,0:T(8,128)S(1)} %add.38), channel_id=1, source_target_pairs={{0,7},{1,0},{2,1},{3,2},{4,3},{5,4},{6,5},{7,6},{8,15},{9,8},{10,9... | collective-permute-start | bytes 589832 | tf_op jit(solution)/shard_map/ppermute | solution.py:25
  98.4 3.9 %collective-permute-start.14 = (f32[64,768]{1,0:T(8,128)S(1)}, f32[64,768]{1,0:T(8,128)S(1)}, u32[]{:S(2)}, u32[]{:S(2)}) collective-permute-start(f32[64,768]{1,0:T(8,128)S(1)} %add.37), channel_id=1, source_target_pairs={{0,1},{1,2},{2,3},{3,4},{4,5},{5,6},{6,7},{7,0},{8,9},{9,10},{10,1... | collective-permute-start | bytes 589832 | tf_op jit(solution)/shard_map/ppermute | solution.py:25
  102.3 1.9 %collective-permute-start.16 = (f32[1,512]{1,0:T(1,128)S(1)}, f32[1,512]{1,0:T(1,128)S(1)}, u32[]{:S(2)}, u32[]{:S(2)}) collective-permute-start(f32[1,512]{1,0:T(1,128)S(1)} %add.36), channel_id=1, source_target_pairs={{0,256},{128,384},{256,0},{384,128},{1,257},{129,385},{257,1},{385... | collective-permute-start | bytes 6152 | tf_op jit(solution)/shard_map/ppermute | solution.py:29
  104.3 4.4 %collective-permute-done.16 = f32[1,512]{1,0:T(1,128)S(1)} collective-permute-done((f32[1,512]{1,0:T(1,128)S(1)}, f32[1,512]{1,0:T(1,128)S(1)}, u32[]{:S(2)}, u32[]{:S(2)}) %collective-permute-start.16) | collective-permute-done | bytes 2080 | tf_op jit(solution)/shard_map/ppermute | solution.py:29
  109.3 1.7 %collective-permute-done.14 = f32[64,768]{1,0:T(8,128)S(1)} collective-permute-done((f32[64,768]{1,0:T(8,128)S(1)}, f32[64,768]{1,0:T(8,128)S(1)}, u32[]{:S(2)}, u32[]{:S(2)}) %collective-permute-start.14) | collective-permute-done | bytes 196640 | tf_op jit(solution)/shard_map/ppermute | solution.py:25
  111.0 2.0 %collective-permute-start.18 = (f32[64,768]{1,0:T(8,128)S(1)}, f32[64,768]{1,0:T(8,128)S(1)}, u32[]{:S(2)}, u32[]{:S(2)}) collective-permute-start(f32[64,768]{1,0:T(8,128)S(1)} %add.41), channel_id=1, source_target_pairs={{0,7},{1,0},{2,1},{3,2},{4,3},{5,4},{6,5},{7,6},{8,15},{9,8},{10,9... | collective-permute-start | bytes 589832 | tf_op jit(solution)/shard_map/ppermute | solution.py:25
  113.0 4.4 %collective-permute-start.17 = (f32[64,768]{1,0:T(8,128)S(1)}, f32[64,768]{1,0:T(8,128)S(1)}, u32[]{:S(2)}, u32[]{:S(2)}) collective-permute-start(f32[64,768]{1,0:T(8,128)S(1)} %add.40), channel_id=1, source_target_pairs={{0,1},{1,2},{2,3},{3,4},{4,5},{5,6},{6,7},{7,0},{8,9},{9,10},{10,1... | collective-permute-start | bytes 589832 | tf_op jit(solution)/shard_map/ppermute | solution.py:25
  117.4 4.2 %collective-permute-done.18.rest_2_ = f32[64,768]{1,0:T(8,128)S(1)} collective-permute-done((f32[64,768]{1,0:T(8,128)S(1)}, f32[64,768]{1,0:T(8,128)S(1)}, u32[]{:S(2)}, u32[]{:S(2)}) %collective-permute-start.18) | collective-permute-done | bytes 196640 | tf_op jit(solution)/shard_map/ppermute | solution.py:25
  121.6 1.8 %collective-permute-done.17.rest_1_ = f32[64,768]{1,0:T(8,128)S(1)} collective-permute-done((f32[64,768]{1,0:T(8,128)S(1)}, f32[64,768]{1,0:T(8,128)S(1)}, u32[]{:S(2)}, u32[]{:S(2)}) %collective-permute-start.17) | collective-permute-done | bytes 196640 | tf_op jit(solution)/shard_map/ppermute | solution.py:25
  124.1 1.0 copy-done.2
  (47 shorter events, 9.8 us)
Async XLA Ops:
  7.2 47.5 %all-gather.3.cloned.1.call-start = ((), (), s32[]{:S(2)}) async-start(), calls=%async_computation.2 | async-start | bytes 1310720 | tf_op jit(solution)/shard_map/all_gather | solution.py:214
  7.9 116.2 %reduce-scatter.2.cloned.1.call-start = ((), (), s32[]{:S(2)}) async-start(), calls=%async_computation.1 | async-start | bytes 2949120 | tf_op jit(solution)/shard_map/reduce_scatter | solution.py:227
  7.9 1.0 copy-start
  8.9 0.7 copy-start.5
  9.8 27.0 %collective-permute-start = (f32[136,512]{1,0:T(8,128)S(1)}, f32[136,512]{1,0:T(8,128)S(1)}, u32[]{:S(2)}, u32[]{:S(2)}) collective-permute-start(f32[136,512]{1,0:T(8,128)S(1)} %shard_map.41), channel_id=1, source_target_pairs={{0,64},{64,0},{1,65},{65,1},{2,66},{66,2},{3,67},{67,3},{4,68},{68... | collective-permute-start | bytes 835592 | tf_op jit(solution)/shard_map/ppermute | solution.py:29
  19.8 25.1 %collective-permute-start.6 = (f32[136,512]{1,0:T(8,128)S(1)}, f32[136,512]{1,0:T(8,128)S(1)}, u32[]{:S(2)}, u32[]{:S(2)}) collective-permute-start(f32[136,512]{1,0:T(8,128)S(1)} %shard_map.41), channel_id=1, source_target_pairs={{0,32},{16,48},{32,0},{48,16},{1,33},{17,49},{33,1},{49,17},{2,34}... | collective-permute-start | bytes 835592 | tf_op jit(solution)/shard_map/ppermute | solution.py:25
  24.8 23.0 %collective-permute-start.5 = (f32[136,512]{1,0:T(8,128)S(1)}, f32[136,512]{1,0:T(8,128)S(1)}, u32[]{:S(2)}, u32[]{:S(2)}) collective-permute-start(f32[136,512]{1,0:T(8,128)S(1)} %shard_map.41), channel_id=1, source_target_pairs={{0,48},{16,0},{32,16},{48,32},{1,49},{17,1},{33,17},{49,33},{2,50}... | collective-permute-start | bytes 835592 | tf_op jit(solution)/shard_map/ppermute | solution.py:25
  27.8 20.0 %collective-permute-start.4 = (f32[136,512]{1,0:T(8,128)S(1)}, f32[136,512]{1,0:T(8,128)S(1)}, u32[]{:S(2)}, u32[]{:S(2)}) collective-permute-start(f32[136,512]{1,0:T(8,128)S(1)} %shard_map.41), channel_id=1, source_target_pairs={{0,16},{16,32},{32,48},{48,0},{1,17},{17,33},{33,49},{49,1},{2,18}... | collective-permute-start | bytes 835592 | tf_op jit(solution)/shard_map/ppermute | solution.py:25
  36.8 13.0 %collective-permute-start.3 = (f32[136,512]{1,0:T(8,128)S(1)}, f32[136,512]{1,0:T(8,128)S(1)}, u32[]{:S(2)}, u32[]{:S(2)}) collective-permute-start(f32[136,512]{1,0:T(8,128)S(1)} %collective-permute-done), channel_id=1, source_target_pairs={{0,32},{16,48},{32,0},{48,16},{1,33},{17,49},{33,1},{49,17},{2,34}... | collective-permute-start | bytes 835592 | tf_op jit(solution)/shard_map/ppermute | solution.py:25
  41.9 8.4 %collective-permute-start.2 = (f32[136,512]{1,0:T(8,128)S(1)}, f32[136,512]{1,0:T(8,128)S(1)}, u32[]{:S(2)}, u32[]{:S(2)}) collective-permute-start(f32[136,512]{1,0:T(8,128)S(1)} %collective-permute-done), channel_id=1, source_target_pairs={{0,48},{16,0},{32,16},{48,32},{1,49},{17,1},{33,17},{49,33},{2,50}... | collective-permute-start | bytes 835592 | tf_op jit(solution)/shard_map/ppermute | solution.py:25
  44.9 9.7 %collective-permute-start.1 = (f32[136,512]{1,0:T(8,128)S(1)}, f32[136,512]{1,0:T(8,128)S(1)}, u32[]{:S(2)}, u32[]{:S(2)}) collective-permute-start(f32[136,512]{1,0:T(8,128)S(1)} %collective-permute-done), channel_id=1, source_target_pairs={{0,16},{16,32},{32,48},{48,0},{1,17},{17,33},{33,49},{49,1},{2,18}... | collective-permute-start | bytes 835592 | tf_op jit(solution)/shard_map/ppermute | solution.py:25
  47.9 10.4 %collective-permute-start.7 = (f32[4,136,512]{2,1,0:T(8,128)S(1)}, f32[4,136,512]{2,1,0:T(8,128)S(1)}, u32[]{:S(2)}, u32[]{:S(2)}) collective-permute-start(f32[4,136,512]{2,1,0:T(8,128)S(1)} %pad_maximum_fusion.1.near_ref), channel_id=1, source_target_pairs={{0,8},{8,0},{1,9},{9,1},{2,10},{10,2},{3,11},{11,3},{4,12},{12,4},... | collective-permute-start | bytes 3342344 | tf_op jit(solution)/shard_map/ppermute | solution.py:29
  54.7 4.6 %collective-permute-start.8 = (f32[4,136,512]{2,1,0:T(8,128)S(1)}, f32[4,136,512]{2,1,0:T(8,128)S(1)}, u32[]{:S(2)}, u32[]{:S(2)}) collective-permute-start(f32[4,136,512]{2,1,0:T(8,128)S(1)} %pad_maximum_fusion.far_ref), channel_id=1, source_target_pairs={{0,8},{8,0},{1,9},{9,1},{2,10},{10,2},{3,11},{11,3},{4,12},{12,4},... | collective-permute-start | bytes 3342344 | tf_op jit(solution)/shard_map/ppermute | solution.py:29
  56.6 1.2 copy-start.1
  58.3 1.0 copy-start.6
  59.4 1.2 copy-start.7
  65.7 0.7 copy-start.3
  66.4 0.6 copy-start.8
  67.0 0.9 copy-start.9
  67.0 9.2 %copy-start.4 = (f32[64,768]{1,0:T(8,128)S(1)}, f32[64,768]{1,0:T(8,128)}, u32[]{:S(2)}) copy-start(f32[64,768]{1,0:T(8,128)} %copy-done.3) | copy-start | bytes 589828
  67.9 8.3 %collective-permute-start.11 = (f32[32,768]{1,0:T(8,128)S(1)}, f32[32,768]{1,0:T(8,128)S(1)}, u32[]{:S(2)}, u32[]{:S(2)}) collective-permute-start(f32[32,768]{1,0:T(8,128)S(1)} %copy-done.9), channel_id=1, source_target_pairs={{0,7},{1,0},{2,1},{3,2},{4,3},{5,4},{6,5},{7,6},{8,15},{9,8},{10,9... | collective-permute-start | bytes 294920 | tf_op jit(solution)/shard_map/ppermute | solution.py:25
  73.6 8.3 %collective-permute-start.9 = (f32[32,768]{1,0:T(8,128)S(1)}, f32[32,768]{1,0:T(8,128)S(1)}, u32[]{:S(2)}, u32[]{:S(2)}) collective-permute-start(f32[32,768]{1,0:T(8,128)S(1)} %get-tuple-element.58), channel_id=1, source_target_pairs={{0,1},{1,2},{2,3},{3,4},{4,5},{5,6},{6,7},{7,0},{8,9},{9,10},{10,1... | collective-permute-start | bytes 294920 | tf_op jit(solution)/shard_map/ppermute | solution.py:25
  76.3 13.8 %collective-permute-start.12 = (f32[64,768]{1,0:T(8,128)S(1)}, f32[64,768]{1,0:T(8,128)S(1)}, u32[]{:S(2)}, u32[]{:S(2)}) collective-permute-start(f32[64,768]{1,0:T(8,128)S(1)} %add_dynamic-update-slice_fusion), channel_id=1, source_target_pairs={{0,7},{1,0},{2,1},{3,2},{4,3},{5,4},{6,5},{7,6},{8,15},{9,8},{10,9... | collective-permute-start | bytes 589832 | tf_op jit(solution)/shard_map/ppermute | solution.py:25
  82.0 14.5 %collective-permute-start.10 = (f32[64,768]{1,0:T(8,128)S(1)}, f32[64,768]{1,0:T(8,128)S(1)}, u32[]{:S(2)}, u32[]{:S(2)}) collective-permute-start(f32[64,768]{1,0:T(8,128)S(1)} %add_dynamic-update-slice_fusion.1), channel_id=1, source_target_pairs={{0,1},{1,2},{2,3},{3,4},{4,5},{5,6},{6,7},{7,0},{8,9},{9,10},{10,1... | collective-permute-start | bytes 589832 | tf_op jit(solution)/shard_map/ppermute | solution.py:25
  83.9 5.5 %collective-permute-start.13 = (f32[1,512]{1,0:T(1,128)S(1)}, f32[1,512]{1,0:T(1,128)S(1)}, u32[]{:S(2)}, u32[]{:S(2)}) collective-permute-start(f32[1,512]{1,0:T(1,128)S(1)} %get-tuple-element.61), channel_id=1, source_target_pairs={{0,128},{128,0},{256,384},{384,256},{1,129},{129,1},{257,385},{385... | collective-permute-start | bytes 6152 | tf_op jit(solution)/shard_map/ppermute | solution.py:29
  96.5 12.9 %collective-permute-start.15 = (f32[64,768]{1,0:T(8,128)S(1)}, f32[64,768]{1,0:T(8,128)S(1)}, u32[]{:S(2)}, u32[]{:S(2)}) collective-permute-start(f32[64,768]{1,0:T(8,128)S(1)} %add.38), channel_id=1, source_target_pairs={{0,7},{1,0},{2,1},{3,2},{4,3},{5,4},{6,5},{7,6},{8,15},{9,8},{10,9... | collective-permute-start | bytes 589832 | tf_op jit(solution)/shard_map/ppermute | solution.py:25
  98.4 12.6 %collective-permute-start.14 = (f32[64,768]{1,0:T(8,128)S(1)}, f32[64,768]{1,0:T(8,128)S(1)}, u32[]{:S(2)}, u32[]{:S(2)}) collective-permute-start(f32[64,768]{1,0:T(8,128)S(1)} %add.37), channel_id=1, source_target_pairs={{0,1},{1,2},{2,3},{3,4},{4,5},{5,6},{6,7},{7,0},{8,9},{9,10},{10,1... | collective-permute-start | bytes 589832 | tf_op jit(solution)/shard_map/ppermute | solution.py:25
  102.3 6.4 %collective-permute-start.16 = (f32[1,512]{1,0:T(1,128)S(1)}, f32[1,512]{1,0:T(1,128)S(1)}, u32[]{:S(2)}, u32[]{:S(2)}) collective-permute-start(f32[1,512]{1,0:T(1,128)S(1)} %add.36), channel_id=1, source_target_pairs={{0,256},{128,384},{256,0},{384,128},{1,257},{129,385},{257,1},{385... | collective-permute-start | bytes 6152 | tf_op jit(solution)/shard_map/ppermute | solution.py:29
  111.0 10.5 %collective-permute-start.18 = (f32[64,768]{1,0:T(8,128)S(1)}, f32[64,768]{1,0:T(8,128)S(1)}, u32[]{:S(2)}, u32[]{:S(2)}) collective-permute-start(f32[64,768]{1,0:T(8,128)S(1)} %add.41), channel_id=1, source_target_pairs={{0,7},{1,0},{2,1},{3,2},{4,3},{5,4},{6,5},{7,6},{8,15},{9,8},{10,9... | collective-permute-start | bytes 589832 | tf_op jit(solution)/shard_map/ppermute | solution.py:25
  113.0 10.4 %collective-permute-start.17 = (f32[64,768]{1,0:T(8,128)S(1)}, f32[64,768]{1,0:T(8,128)S(1)}, u32[]{:S(2)}, u32[]{:S(2)}) collective-permute-start(f32[64,768]{1,0:T(8,128)S(1)} %add.40), channel_id=1, source_target_pairs={{0,1},{1,2},{2,3},{3,4},{4,5},{5,6},{6,7},{7,0},{8,9},{9,10},{10,1... | collective-permute-start | bytes 589832 | tf_op jit(solution)/shard_map/ppermute | solution.py:25
  124.1 1.0 copy-start.2
Sparse Core Ops, SparseCore 0:
  10.1 39.7 all-gather.2
  67.2 56.1 reduce-scatter.1

commit v6 on v5

v6 whole, which is shorter than its diff:
```python
import jax
import jax.numpy as jnp
from jax import lax
from jax.experimental import pallas as pl
from jax.experimental.pallas import tpu as pltpu
from jax.sharding import Mesh, PartitionSpec as P

AXES = ("zl", "zh", "x", "core", "par")
SIZES = (4, 2, 4, 2, 8)
SAMPLES = AXES[:4]
LANES = 128
EXTRA = 8
HOPS = (0, 1, 3, 2)
VMEM = pltpu.CompilerParams(vmem_limit_bytes=24 * 1024 * 1024)
IN_VMEM = pl.BlockSpec(memory_space=pltpu.VMEM)
IN_HBM = pl.BlockSpec(memory_space=pltpu.HBM)


def shift(value, axis, by):
    count = lax.axis_size(axis)
    return lax.ppermute(value, axis, [(i, (i + by) % count) for i in range(count)])


def swap(value, axis, bit):
    return lax.ppermute(value, axis, [(i, i ^ bit) for i in range(lax.axis_size(axis))])


def cost(flops, elements):
    return pl.CostEstimate(flops=flops, bytes_accessed=4 * elements, transcendentals=0)


def halves(value):
    high = value.astype(jnp.bfloat16)
    low = (value - high.astype(jnp.float32)).astype(jnp.bfloat16)
    return high, low


def begin_kernel(data_ref, vector_ref, out_ref):
    local, params = data_ref.shape
    out_ref[:local, :] = data_ref[...]
    term = lax.dot_general(
        vector_ref[...],
        data_ref[...],
        (((1,), (0,)), ((), ())),
        precision=lax.Precision.HIGHEST,
        preferred_element_type=jnp.float32,
    )
    out_ref[local:, :] = jnp.broadcast_to(term, (EXTRA, params))


def begin(data, vector):
    local, params = data.shape
    return pl.pallas_call(
        begin_kernel,
        out_shape=jax.ShapeDtypeStruct((local + EXTRA, params), jnp.float32),
        compiler_params=VMEM,
        cost_estimate=cost(12 * data.size, 2 * data.size),
    )(data, vector.reshape(1, local))


def left_kernel(left_ref, high_ref, low_ref, rows):
    blocks, local, params = left_ref.shape
    for g in range(params // LANES):
        lanes = pl.ds(g * LANES, LANES)
        for a in range(blocks):
            rows[g, pl.ds(a, local, stride=blocks), :] = left_ref[a, :, lanes]
        high_ref[:, lanes], low_ref[:, lanes] = halves(rows[g])


def left_halves(left):
    blocks, local, params = left.shape
    shape = (blocks * local, params)
    return pl.pallas_call(
        left_kernel,
        out_shape=[jax.ShapeDtypeStruct(shape, jnp.bfloat16)] * 2,
        scratch_shapes=[pltpu.VMEM((params // LANES, blocks * local, LANES), jnp.float32)],
        compiler_params=VMEM,
        cost_estimate=cost(4 * left.size, 2 * left.size),
    )(left)


def block_product(high_ref, low_ref, mine_ref, other_ref, n, right):
    local = right.shape[0] // 2
    core = lax.axis_index("core")
    right[pl.ds(pl.multiple_of(core * local, local), local), :] = mine_ref[n, :local, :]
    right[pl.ds(pl.multiple_of((1 - core) * local, local), local), :] = other_ref[n, :local, :]
    high, low = halves(right[...])

    def dot(a, b):
        return lax.dot_general(
            a, b, (((1,), (1,)), ((), ())), preferred_element_type=jnp.float32
        )

    return dot(high_ref[...], low) + dot(low_ref[...], high) + dot(high_ref[...], high)


def product_kernel(high_ref, low_ref, near_ref, near_other_ref, far_ref, far_other_ref, total_hbm, term_ref, right, value, sent):
    count = near_ref.shape[0]
    local = near_ref.shape[1] - EXTRA
    width = value.shape[2]
    copies = []
    for n in range(2 * count):
        pair = (near_ref, near_other_ref) if n < count else (far_ref, far_other_ref)
        value[n] = block_product(high_ref, low_ref, *pair, n % count, right.at[n % 2])
        copies.append(
            pltpu.make_async_copy(
                value.at[n], total_hbm.at[:, pl.ds(n * width, width)], sent.at[n]
            )
        )
        copies[-1].start()

    def pairs(ref):
        row = [ref[HOPS.index(by), pl.ds(local, 1), :] for by in range(count)]
        return (row[0] + row[2]) + (row[1] + row[3])

    near_term = pairs(near_ref) + pairs(near_other_ref)
    far_term = pairs(far_ref) + pairs(far_other_ref)
    term_ref[...] = near_term + far_term
    for copy in copies:
        copy.wait()


def product(left, near, near_other, far, far_other):
    rows, params = left[0].shape
    count, height, _ = near.shape
    width = 2 * (height - EXTRA)
    blocks = 2 * count
    return pl.pallas_call(
        product_kernel,
        in_specs=[IN_VMEM] * 6,
        out_specs=[IN_HBM, IN_VMEM],
        out_shape=[
            pltpu.HBM((rows, blocks * width), jnp.float32),
            jax.ShapeDtypeStruct((1, params), jnp.float32),
        ],
        scratch_shapes=[
            pltpu.VMEM((2, width, params), jnp.float32),
            pltpu.VMEM((blocks, rows, width), jnp.float32),
            pltpu.SemaphoreType.DMA((blocks,)),
        ],
        compiler_params=VMEM,
        cost_estimate=cost(6 * rows * blocks * width * params, blocks * width * (params + rows)),
    )(*left, near, near_other, far, far_other)


def write_kernel(sum_ref, out_hbm, value, sent):
    count = len(HOPS)
    x, zh = lax.axis_index("x"), lax.axis_index("zh")
    blocks, _, _, width = value.shape
    copies = []
    for n in range(blocks):
        value[n] = sum_ref[:, pl.ds(n * width, width)].reshape(value.shape[1:])
        half = zh if n < count else 1 - zh
        source = lax.rem(x + (count - HOPS[n % count]), count)
        first = pl.multiple_of((half * count + source) * width, width)
        copies.append(
            pltpu.make_async_copy(value.at[n], out_hbm.at[:, :, pl.ds(first, width)], sent.at[n])
        )
        copies[-1].start()
    for copy in copies:
        copy.wait()


def write(summed, blocks):
    rows, columns = summed.shape
    count = 2 * len(HOPS)
    shape = (rows // blocks, blocks)
    return pl.pallas_call(
        write_kernel,
        in_specs=[IN_VMEM],
        out_specs=IN_HBM,
        out_shape=pltpu.HBM(shape + (columns,), jnp.float32),
        scratch_shapes=[
            pltpu.VMEM((count,) + shape + (columns // count,), jnp.float32),
            pltpu.SemaphoreType.DMA((count,)),
        ],
        compiler_params=VMEM,
        cost_estimate=cost(0, 2 * rows * columns),
    )(summed)


def body(log_derivs, sample_vector):
    left = lax.all_gather(log_derivs, "zl")
    blocks = left.shape[0]

    own = begin(log_derivs, sample_vector)
    far = swap(own, "zh", 1)
    near = jnp.stack([own] + [shift(own, "x", by) for by in HOPS[1:]])
    near_other = swap(near, "core", 1)
    far = jnp.stack([far] + [shift(far, "x", by) for by in HOPS[1:]])
    far, left = lax.optimization_barrier((far, left))
    far_other = swap(far, "core", 1)

    left = left_halves(left)
    total, value = product(left, near, near_other, far, far_other)
    summed = lax.psum_scatter(total, "par", scatter_dimension=0, tiled=True)
    for bit in (1, 2):
        value = value + swap(value, "zl", bit)
    return (write(summed, blocks), value[0])


def solution(mesh):
    split = Mesh(mesh.devices.reshape(SIZES), AXES)
    in_specs = (P(SAMPLES, "par"), P(SAMPLES))
    out_specs = (P(("zh", "x", "core", "par"), None, "zl"), P("par"))
    return jax.shard_map(body, mesh=split, in_specs=in_specs, out_specs=out_specs, check_vma=False)
```

time: 134 us -> 134 us (level)
  the two profiles are of different devices: /device:TPU:64 before, /device:TPU:7 now
where the time goes in v6:
time: 134 us; the launch traced here: 133 us
  waiting for transfers between devices  62.5 us (47%)
  starting transfers between devices  44.7 us (33%)
  between operations  14.2 us (11%)
  Pallas kernels  6.95 us (5%)
  local copies, waits for them, and re-layouts  3.86 us (3%)
    reduce_scatter x1, waiting for transfers between devices, body(): summed = lax.psum_scatter(total, 'par', scatter_dimension=0, tiled=True)  51.6 us
    ppermute x5, starting transfers between devices, swap(): lax.ppermute(value, axis, [(i, i ^ bit) for i in range(lax.axis_size(axis...  26.1 us
    ppermute x6, starting transfers between devices, shift(): lax.ppermute(value, axis, [(i, (i + by) % count) for i in range(count)])  18.6 us
    pallas_call x1, Pallas kernels, product(): pl.pallas_call(product_kernel, in_specs=[IN_VMEM] * 6, out_specs=[IN_HBM,...  5.43 us
    ppermute x6, waiting for transfers between devices, shift(): lax.ppermute(value, axis, [(i, (i + by) % count) for i in range(count)])  5.3 us
    unnamed x8, local copies, waits for them, and re-layouts  3.86 us
    ppermute x5, waiting for transfers between devices, swap(): lax.ppermute(value, axis, [(i, i ^ bit) for i in range(lax.axis_size(axis...  3.3 us
  transfers between devices with their start and end apart: 13, of which 7 were waited for; matrix products, arithmetic and copies ran while one was open for 1% of the time, Pallas kernels for 0%

profile of v6, /device:TPU:7, one launch (start us, length us, event | category | flops | bytes accessed | tf_op | source)
XLA Modules:
  0.0 133.1 jit_solution(2447741488744227124)
XLA Ops:
  7.2 0.0 all-gather.3.cloned.1.call-start
  7.2 0.7 all-gather.3.cloned.1.call-update
  7.9 0.0 reduce-scatter.2.cloned.1.call-start
  8.0 0.9 copy-done
  8.9 0.7 copy-done.3
  9.6 0.2 shard_map.41
  9.8 10.6 %collective-permute-start = (f32[136,512]{1,0:T(8,128)S(1)}, f32[136,512]{1,0:T(8,128)S(1)}, u32[]{:S(2)}, u32[]{:S(2)}) collective-permute-start(f32[136,512]{1,0:T(8,128)S(1)} %shard_map.41), channel_id=1, source_target_pairs={{0,64},{64,0},{1,65},{65,1},{2,66},{66,2},{3,67},{67,3},{4,68},{68... | collective-permute-start | bytes 835592 | tf_op jit(solution)/shard_map/ppermute | solution.py:25
  20.4 3.0 %collective-permute-start.6 = (f32[136,512]{1,0:T(8,128)S(1)}, f32[136,512]{1,0:T(8,128)S(1)}, u32[]{:S(2)}, u32[]{:S(2)}) collective-permute-start(f32[136,512]{1,0:T(8,128)S(1)} %shard_map.41), channel_id=1, source_target_pairs={{0,32},{16,48},{32,0},{48,16},{1,33},{17,49},{33,1},{49,17},{2,34}... | collective-permute-start | bytes 835592 | tf_op jit(solution)/shard_map/ppermute | solution.py:21
  23.5 1.9 %collective-permute-start.5 = (f32[136,512]{1,0:T(8,128)S(1)}, f32[136,512]{1,0:T(8,128)S(1)}, u32[]{:S(2)}, u32[]{:S(2)}) collective-permute-start(f32[136,512]{1,0:T(8,128)S(1)} %shard_map.41), channel_id=1, source_target_pairs={{0,48},{16,0},{32,16},{48,32},{1,49},{17,1},{33,17},{49,33},{2,50}... | collective-permute-start | bytes 835592 | tf_op jit(solution)/shard_map/ppermute | solution.py:21
  25.4 4.6 %collective-permute-start.4 = (f32[136,512]{1,0:T(8,128)S(1)}, f32[136,512]{1,0:T(8,128)S(1)}, u32[]{:S(2)}, u32[]{:S(2)}) collective-permute-start(f32[136,512]{1,0:T(8,128)S(1)} %shard_map.41), channel_id=1, source_target_pairs={{0,16},{16,32},{32,48},{48,0},{1,17},{17,33},{33,49},{49,1},{2,18}... | collective-permute-start | bytes 835592 | tf_op jit(solution)/shard_map/ppermute | solution.py:21
  30.0 2.5 %collective-permute-start.3 = (f32[136,512]{1,0:T(8,128)S(1)}, f32[136,512]{1,0:T(8,128)S(1)}, u32[]{:S(2)}, u32[]{:S(2)}) collective-permute-start(f32[136,512]{1,0:T(8,128)S(1)} %collective-permute-done), channel_id=1, source_target_pairs={{0,32},{16,48},{32,0},{48,16},{1,33},{17,49},{33,1},{49,17},{2,34}... | collective-permute-start | bytes 835592 | tf_op jit(solution)/shard_map/ppermute | solution.py:21
  32.5 2.5 %collective-permute-start.2 = (f32[136,512]{1,0:T(8,128)S(1)}, f32[136,512]{1,0:T(8,128)S(1)}, u32[]{:S(2)}, u32[]{:S(2)}) collective-permute-start(f32[136,512]{1,0:T(8,128)S(1)} %collective-permute-done), channel_id=1, source_target_pairs={{0,48},{16,0},{32,16},{48,32},{1,49},{17,1},{33,17},{49,33},{2,50}... | collective-permute-start | bytes 835592 | tf_op jit(solution)/shard_map/ppermute | solution.py:21
  35.0 4.0 %collective-permute-start.1 = (f32[136,512]{1,0:T(8,128)S(1)}, f32[136,512]{1,0:T(8,128)S(1)}, u32[]{:S(2)}, u32[]{:S(2)}) collective-permute-start(f32[136,512]{1,0:T(8,128)S(1)} %collective-permute-done), channel_id=1, source_target_pairs={{0,16},{16,32},{32,48},{48,0},{1,17},{17,33},{33,49},{49,1},{2,18}... | collective-permute-start | bytes 835592 | tf_op jit(solution)/shard_map/ppermute | solution.py:21
  39.1 0.8 collective-permute-done.5
  39.8 0.1 pad_maximum_fusion.1.near_ref
  39.9 5.7 %collective-permute-start.7 = (f32[4,136,512]{2,1,0:T(8,128)S(1)}, f32[4,136,512]{2,1,0:T(8,128)S(1)}, u32[]{:S(2)}, u32[]{:S(2)}) collective-permute-start(f32[4,136,512]{2,1,0:T(8,128)S(1)} %pad_maximum_fusion.1.near_ref), channel_id=1, source_target_pairs={{0,8},{8,0},{1,9},{9,1},{2,10},{10,2},{3,11},{11,3},{4,12},{12,4},... | collective-permute-start | bytes 3342344 | tf_op jit(solution)/shard_map/ppermute | solution.py:25
  45.7 4.5 %collective-permute-done.2 = f32[136,512]{1,0:T(8,128)S(1)} collective-permute-done((f32[136,512]{1,0:T(8,128)S(1)}, f32[136,512]{1,0:T(8,128)S(1)}, u32[]{:S(2)}, u32[]{:S(2)}) %collective-permute-start.2) | collective-permute-done | bytes 278560 | tf_op jit(solution)/shard_map/ppermute | solution.py:21
  50.2 0.1 pad_maximum_fusion.far_ref
  50.3 1.6 %all-gather.3.cloned.1.call-done = f32[512,512]{1,0:T(8,128)} async-done(((f32[128,512]{1,0:T(8,128)}), f32[512,512]{1,0:T(8,128)}) %all-gather.3.cloned.1.call-update) | async-done | bytes 1048592 | tf_op jit(solution)/shard_map/all_gather | solution.py:183
  52.0 2.4 %collective-permute-start.8 = (f32[4,136,512]{2,1,0:T(8,128)S(1)}, f32[4,136,512]{2,1,0:T(8,128)S(1)}, u32[]{:S(2)}, u32[]{:S(2)}) collective-permute-start(f32[4,136,512]{2,1,0:T(8,128)S(1)} %pad_maximum_fusion.far_ref), channel_id=1, source_target_pairs={{0,8},{8,0},{1,9},{9,1},{2,10},{10,2},{3,11},{11,3},{4,12},{12,4},... | collective-permute-start | bytes 3342344 | tf_op jit(solution)/shard_map/ppermute | solution.py:25
  54.3 1.2 copy-done.1
  55.5 0.4 shard_map.42
  56.0 0.7 collective-permute-done.8.far_other_ref
  56.7 5.4 %shard_map.43 = (f32[512,2048]{1,0:T(8,128)}, f32[1,512]{1,0:T(1,128)S(1)}) custom-call(bf16[512,512]{1,0:T(8,128)(2,1)S(1)} %get-tuple-element.9.high_ref, bf16[512,512]{1,0:T(8,128)(2,1)S(1)} %get-tuple-element.10.low_ref, f32[4,136,512]{2,1,0:T(8,128)S(1)} %pad_maximum_fusion.1.near_ref, f32[4,136,512]{2,1,0:T(8,128)S(1)} %collective-permute-done.7.near_other_ref, ...), custom_call_target="tpu_custom_call" | custom-call | flops 3221225472 | bytes 8388608 | tf_op jit(solution)/shard_map/pallas_call | solution.py:128
  62.1 3.8 %collective-permute-start.9 = (f32[1,512]{1,0:T(1,128)S(1)}, f32[1,512]{1,0:T(1,128)S(1)}, u32[]{:S(2)}, u32[]{:S(2)}) collective-permute-start(f32[1,512]{1,0:T(1,128)S(1)} %get-tuple-element.13), channel_id=1, source_target_pairs={{0,128},{128,0},{256,384},{384,256},{1,129},{129,1},{257,385},{385... | collective-permute-start | bytes 6152 | tf_op jit(solution)/shard_map/ppermute | solution.py:25
  65.9 1.0 collective-permute-done.9
  66.9 3.6 %collective-permute-start.10 = (f32[1,512]{1,0:T(1,128)S(1)}, f32[1,512]{1,0:T(1,128)S(1)}, u32[]{:S(2)}, u32[]{:S(2)}) collective-permute-start(f32[1,512]{1,0:T(1,128)S(1)} %add.8), channel_id=1, source_target_pairs={{0,256},{128,384},{256,0},{384,128},{1,257},{129,385},{257,1},{385... | collective-permute-start | bytes 6152 | tf_op jit(solution)/shard_map/ppermute | solution.py:25
  70.5 1.6 %collective-permute-done.10 = f32[1,512]{1,0:T(1,128)S(1)} collective-permute-done((f32[1,512]{1,0:T(1,128)S(1)}, f32[1,512]{1,0:T(1,128)S(1)}, u32[]{:S(2)}, u32[]{:S(2)}) %collective-permute-start.10) | collective-permute-done | bytes 2080 | tf_op jit(solution)/shard_map/ppermute | solution.py:25
  72.1 0.6 add.9
  72.7 51.6 %reduce-scatter.2.cloned.1.call-done.sum_ref = f32[64,2048]{1,0:T(8,128)} async-done(((f32[512,2048]{1,0:T(8,128)}), f32[64,2048]{1,0:T(8,128)}) %reduce-scatter.2.cloned.1.call-update) | async-done | bytes 524304 | tf_op jit(solution)/shard_map/reduce_scatter | solution.py:196
  124.3 1.0 copy-done.2
  125.3 0.9 shard_map.44
  (12 shorter events, 0.0 us)
Async XLA Ops:
  7.2 44.8 %all-gather.3.cloned.1.call-start = ((), (), s32[]{:S(2)}) async-start(), calls=%async_computation.2 | async-start | bytes 1310720 | tf_op jit(solution)/shard_map/all_gather | solution.py:183
  7.9 116.4 %reduce-scatter.2.cloned.1.call-start = ((), (), s32[]{:S(2)}) async-start(), calls=%async_computation.1 | async-start | bytes 4718592 | tf_op jit(solution)/shard_map/reduce_scatter | solution.py:196
  7.9 1.0 copy-start
  8.9 0.7 copy-start.3
  9.8 20.2 %collective-permute-start = (f32[136,512]{1,0:T(8,128)S(1)}, f32[136,512]{1,0:T(8,128)S(1)}, u32[]{:S(2)}, u32[]{:S(2)}) collective-permute-start(f32[136,512]{1,0:T(8,128)S(1)} %shard_map.41), channel_id=1, source_target_pairs={{0,64},{64,0},{1,65},{65,1},{2,66},{66,2},{3,67},{67,3},{4,68},{68... | collective-permute-start | bytes 835592 | tf_op jit(solution)/shard_map/ppermute | solution.py:25
  20.4 14.6 %collective-permute-start.6 = (f32[136,512]{1,0:T(8,128)S(1)}, f32[136,512]{1,0:T(8,128)S(1)}, u32[]{:S(2)}, u32[]{:S(2)}) collective-permute-start(f32[136,512]{1,0:T(8,128)S(1)} %shard_map.41), channel_id=1, source_target_pairs={{0,32},{16,48},{32,0},{48,16},{1,33},{17,49},{33,1},{49,17},{2,34}... | collective-permute-start | bytes 835592 | tf_op jit(solution)/shard_map/ppermute | solution.py:21
  23.5 16.3 %collective-permute-start.5 = (f32[136,512]{1,0:T(8,128)S(1)}, f32[136,512]{1,0:T(8,128)S(1)}, u32[]{:S(2)}, u32[]{:S(2)}) collective-permute-start(f32[136,512]{1,0:T(8,128)S(1)} %shard_map.41), channel_id=1, source_target_pairs={{0,48},{16,0},{32,16},{48,32},{1,49},{17,1},{33,17},{49,33},{2,50}... | collective-permute-start | bytes 835592 | tf_op jit(solution)/shard_map/ppermute | solution.py:21
  25.4 14.4 %collective-permute-start.4 = (f32[136,512]{1,0:T(8,128)S(1)}, f32[136,512]{1,0:T(8,128)S(1)}, u32[]{:S(2)}, u32[]{:S(2)}) collective-permute-start(f32[136,512]{1,0:T(8,128)S(1)} %shard_map.41), channel_id=1, source_target_pairs={{0,16},{16,32},{32,48},{48,0},{1,17},{17,33},{33,49},{49,1},{2,18}... | collective-permute-start | bytes 835592 | tf_op jit(solution)/shard_map/ppermute | solution.py:21
  30.0 15.7 %collective-permute-start.3 = (f32[136,512]{1,0:T(8,128)S(1)}, f32[136,512]{1,0:T(8,128)S(1)}, u32[]{:S(2)}, u32[]{:S(2)}) collective-permute-start(f32[136,512]{1,0:T(8,128)S(1)} %collective-permute-done), channel_id=1, source_target_pairs={{0,32},{16,48},{32,0},{48,16},{1,33},{17,49},{33,1},{49,17},{2,34}... | collective-permute-start | bytes 835592 | tf_op jit(solution)/shard_map/ppermute | solution.py:21
  32.5 17.7 %collective-permute-start.2 = (f32[136,512]{1,0:T(8,128)S(1)}, f32[136,512]{1,0:T(8,128)S(1)}, u32[]{:S(2)}, u32[]{:S(2)}) collective-permute-start(f32[136,512]{1,0:T(8,128)S(1)} %collective-permute-done), channel_id=1, source_target_pairs={{0,48},{16,0},{32,16},{48,32},{1,49},{17,1},{33,17},{49,33},{2,50}... | collective-permute-start | bytes 835592 | tf_op jit(solution)/shard_map/ppermute | solution.py:21
  35.0 15.2 %collective-permute-start.1 = (f32[136,512]{1,0:T(8,128)S(1)}, f32[136,512]{1,0:T(8,128)S(1)}, u32[]{:S(2)}, u32[]{:S(2)}) collective-permute-start(f32[136,512]{1,0:T(8,128)S(1)} %collective-permute-done), channel_id=1, source_target_pairs={{0,16},{16,32},{32,48},{48,0},{1,17},{17,33},{33,49},{49,1},{2,18}... | collective-permute-start | bytes 835592 | tf_op jit(solution)/shard_map/ppermute | solution.py:21
  39.9 16.1 %collective-permute-start.7 = (f32[4,136,512]{2,1,0:T(8,128)S(1)}, f32[4,136,512]{2,1,0:T(8,128)S(1)}, u32[]{:S(2)}, u32[]{:S(2)}) collective-permute-start(f32[4,136,512]{2,1,0:T(8,128)S(1)} %pad_maximum_fusion.1.near_ref), channel_id=1, source_target_pairs={{0,8},{8,0},{1,9},{9,1},{2,10},{10,2},{3,11},{11,3},{4,12},{12,4},... | collective-permute-start | bytes 3342344 | tf_op jit(solution)/shard_map/ppermute | solution.py:25
  52.0 4.7 %collective-permute-start.8 = (f32[4,136,512]{2,1,0:T(8,128)S(1)}, f32[4,136,512]{2,1,0:T(8,128)S(1)}, u32[]{:S(2)}, u32[]{:S(2)}) collective-permute-start(f32[4,136,512]{2,1,0:T(8,128)S(1)} %pad_maximum_fusion.far_ref), channel_id=1, source_target_pairs={{0,8},{8,0},{1,9},{9,1},{2,10},{10,2},{3,11},{11,3},{4,12},{12,4},... | collective-permute-start | bytes 3342344 | tf_op jit(solution)/shard_map/ppermute | solution.py:25
  54.3 1.2 copy-start.1
  62.1 4.7 %collective-permute-start.9 = (f32[1,512]{1,0:T(1,128)S(1)}, f32[1,512]{1,0:T(1,128)S(1)}, u32[]{:S(2)}, u32[]{:S(2)}) collective-permute-start(f32[1,512]{1,0:T(1,128)S(1)} %get-tuple-element.13), channel_id=1, source_target_pairs={{0,128},{128,0},{256,384},{384,256},{1,129},{129,1},{257,385},{385... | collective-permute-start | bytes 6152 | tf_op jit(solution)/shard_map/ppermute | solution.py:25
  66.9 5.2 %collective-permute-start.10 = (f32[1,512]{1,0:T(1,128)S(1)}, f32[1,512]{1,0:T(1,128)S(1)}, u32[]{:S(2)}, u32[]{:S(2)}) collective-permute-start(f32[1,512]{1,0:T(1,128)S(1)} %add.8), channel_id=1, source_target_pairs={{0,256},{128,384},{256,0},{384,128},{1,257},{129,385},{257,1},{385... | collective-permute-start | bytes 6152 | tf_op jit(solution)/shard_map/ppermute | solution.py:25
  124.3 1.0 copy-start.2
Sparse Core Ops, SparseCore 0:
  10.1 41.8 all-gather.2
  62.3 61.9 reduce-scatter.1

commit v7 on v4

v7 whole, which is shorter than its diff:
```python
import jax
import jax.numpy as jnp
from jax import lax
from jax.experimental import pallas as pl
from jax.experimental.pallas import tpu as pltpu
from jax.sharding import Mesh, PartitionSpec as P

AXES = ("zl", "zh", "x", "core", "par")
SIZES = (4, 2, 4, 2, 8)
SAMPLES = AXES[:4]
LANES = 128
HOPS = (0, 1, 3, 2)
BUTTERFLY = (("core", 1), ("x", 1), ("x", 2), ("zh", 1), ("zl", 1), ("zl", 2))
VMEM = pltpu.CompilerParams(vmem_limit_bytes=24 * 1024 * 1024)


def shift(value, axis, by):
    count = lax.axis_size(axis)
    return lax.ppermute(value, axis, [(i, (i + by) % count) for i in range(count)])


def swap(value, axis, bit):
    return lax.ppermute(value, axis, [(i, i ^ bit) for i in range(lax.axis_size(axis))])


def halves(value):
    high = value.astype(jnp.bfloat16)
    low = (value - high.astype(jnp.float32)).astype(jnp.bfloat16)
    return high, low


def term_kernel(data_ref, vector_ref, term_ref):
    term_ref[...] = lax.dot_general(
        vector_ref[...],
        data_ref[...],
        (((1,), (0,)), ((), ())),
        precision=lax.Precision.HIGHEST,
        preferred_element_type=jnp.float32,
    )


def term(data, vector):
    local, params = data.shape
    return pl.pallas_call(
        term_kernel,
        out_shape=jax.ShapeDtypeStruct((1, params), jnp.float32),
        compiler_params=VMEM,
        cost_estimate=pl.CostEstimate(
            flops=12 * data.size, bytes_accessed=4 * data.size, transcendentals=0
        ),
    )(data, vector.reshape(1, local))


def left_kernel(left_ref, high_ref, low_ref, rows):
    blocks, local, params = left_ref.shape
    for g in range(params // LANES):
        lanes = pl.ds(g * LANES, LANES)
        for a in range(blocks):
            rows[g, pl.ds(a, local, stride=blocks), :] = left_ref[a, :, lanes]
        high_ref[:, lanes], low_ref[:, lanes] = halves(rows[g])


def left_halves(left):
    blocks, local, params = left.shape
    shape = (blocks * local, params)
    return pl.pallas_call(
        left_kernel,
        out_shape=[jax.ShapeDtypeStruct(shape, jnp.bfloat16)] * 2,
        scratch_shapes=[pltpu.VMEM((params // LANES, blocks * local, LANES), jnp.float32)],
        compiler_params=VMEM,
        cost_estimate=pl.CostEstimate(
            flops=4 * left.size, bytes_accessed=8 * left.size, transcendentals=0
        ),
    )(left)


def multiply(high_ref, low_ref, mine_ref, other_ref, n, right):
    local = mine_ref.shape[1]
    core = lax.axis_index("core")
    right[pl.ds(pl.multiple_of(core * local, local), local), :] = mine_ref[n]
    right[pl.ds(pl.multiple_of((1 - core) * local, local), local), :] = other_ref[n]
    high, low = halves(right[...])

    def dot(a, b):
        return lax.dot_general(
            a, b, (((1,), (1,)), ((), ())), preferred_element_type=jnp.float32
        )

    return dot(high_ref[...], low) + dot(low_ref[...], high) + dot(high_ref[...], high)


def near_kernel(high_ref, low_ref, mine_ref, other_ref, out_ref, right):
    for n in range(out_ref.shape[0]):
        out_ref[n] = multiply(high_ref, low_ref, mine_ref, other_ref, n, right.at[n % 2])


def far_kernel(near_value, high_ref, low_ref, mine_ref, other_ref, total_hbm, far_value, right, sent):
    count, _, width = far_value.shape
    x, zh = lax.axis_index("x"), lax.axis_index("zh")

    def send(value, half, n):
        source = lax.rem(x + (count - HOPS[n % count]), count)
        first = pl.multiple_of((half * count + source) * width, width)
        return pltpu.make_async_copy(
            value.at[n % count], total_hbm.at[:, pl.ds(first, width)], sent.at[n]
        )

    copies = [send(near_value, zh, n) for n in range(count)]
    for copy in copies:
        copy.start()
    for n in range(count):
        far_value[n] = multiply(high_ref, low_ref, mine_ref, other_ref, n, right.at[n % 2])
        copies.append(send(far_value, 1 - zh, count + n))
        copies[-1].start()
    for copy in copies:
        copy.wait()


def product(left, near, near_other, far, far_other):
    rows, params = left[0].shape
    count, local, _ = near.shape
    width = 2 * local
    whole = pl.BlockSpec(memory_space=pltpu.VMEM)
    value = (count, rows, width)
    right = pltpu.VMEM((2, width, params), jnp.float32)
    cost = pl.CostEstimate(
        flops=6 * rows * count * width * params,
        bytes_accessed=4 * count * width * (params + rows),
        transcendentals=0,
    )
    near_value = pl.pallas_call(
        near_kernel,
        in_specs=[whole] * 4,
        out_specs=whole,
        out_shape=jax.ShapeDtypeStruct(value, jnp.float32),
        scratch_shapes=[right],
        compiler_params=VMEM,
        cost_estimate=cost,
    )(*left, near, near_other)
    return pl.pallas_call(
        far_kernel,
        in_specs=[whole] * 5,
        out_specs=pl.BlockSpec(memory_space=pltpu.HBM),
        out_shape=pltpu.HBM((rows, 2 * count * width), jnp.float32),
        scratch_shapes=[pltpu.VMEM(value, jnp.float32), right, pltpu.SemaphoreType.DMA((2 * count,))],
        compiler_params=VMEM,
        cost_estimate=cost,
    )(near_value, *left, far, far_other)


def body(log_derivs, sample_vector):
    left = lax.all_gather(log_derivs, "zl")
    blocks = left.shape[0]

    far = swap(log_derivs, "zh", 1)
    near = jnp.stack([log_derivs] + [shift(log_derivs, "x", by) for by in HOPS[1:]])
    near_other = swap(near, "core", 1)
    far = jnp.stack([far] + [shift(far, "x", by) for by in HOPS[1:]])
    far, left = lax.optimization_barrier((far, left))
    far_other = swap(far, "core", 1)

    total = product(left_halves(left), near, near_other, far, far_other)
    total, log_derivs, sample_vector = lax.optimization_barrier((total, log_derivs, sample_vector))
    summed = lax.psum_scatter(total, "par", scatter_dimension=0, tiled=True)
    value = term(log_derivs, sample_vector)
    for axis, bit in BUTTERFLY:
        value = value + swap(value, axis, bit)
    return (summed.reshape(-1, blocks, summed.shape[1]), value[0])


def solution(mesh):
    split = Mesh(mesh.devices.reshape(SIZES), AXES)
    in_specs = (P(SAMPLES, "par"), P(SAMPLES))
    out_specs = (P(("zh", "x", "core", "par"), None, "zl"), P("par"))
    return jax.shard_map(body, mesh=split, in_specs=in_specs, out_specs=out_specs, check_vma=False)
```

time: 132 us -> 128 us (0.970)
  waiting for transfers between devices: 46.4 us -> 42.8 us
    reduce_scatter x1, waiting for transfers between devices: 27.6 us -> 22.6 us  [body(): summed = lax.psum_scatter(total, 'par', scatter_dimension=0, tiled=True)]
    ppermute x9, waiting for transfers between devices: 12.1 us -> 14.8 us  [swap(): lax.ppermute(value, axis, [(i, i ^ bit) for i in range(lax.axis_size(axis...]
    ppermute x6, waiting for transfers between devices: 3.87 us -> 1.99 us  [shift(): lax.ppermute(value, axis, [(i, (i + by) % count) for i in range(count)])]
    ppermute x9, starting transfers between devices: 38.8 us -> 37.2 us  [swap(): lax.ppermute(value, axis, [(i, i ^ bit) for i in range(lax.axis_size(axis...]
  transfers between devices with their start and end apart: 17 -> 17, of which waited for: 9 -> 9; matrix products, arithmetic and copies ran while one was open for 1% -> 1% of each run, Pallas kernels for 3% -> 2%
where the time goes in v7:
time: 128 us; the launch traced here: 126 us
  starting transfers between devices  57 us (45%)
  waiting for transfers between devices  42.8 us (33%)
  between operations  14.3 us (11%)
  Pallas kernels  6.16 us (5%)
  local copies, waits for them, and re-layouts  4.11 us (3%)
  other arithmetic  1.7 us (1%)
    ppermute x9, starting transfers between devices, swap(): lax.ppermute(value, axis, [(i, i ^ bit) for i in range(lax.axis_size(axis...  37.2 us
    reduce_scatter x1, waiting for transfers between devices, body(): summed = lax.psum_scatter(total, 'par', scatter_dimension=0, tiled=True)  22.6 us
    ppermute x6, starting transfers between devices, shift(): lax.ppermute(value, axis, [(i, (i + by) % count) for i in range(count)])  19.8 us
    ppermute x9, waiting for transfers between devices, swap(): lax.ppermute(value, axis, [(i, i ^ bit) for i in range(lax.axis_size(axis...  14.8 us
    pallas_call x1, Pallas kernels, product(): pl.pallas_call(far_kernel, in_specs=[whole] * 5, out_specs=pl.BlockSpec(m...  3.37 us
    all_gather x1, waiting for transfers between devices, body(): left = lax.all_gather(log_derivs, 'zl')  2.74 us
  transfers between devices with their start and end apart: 17, of which 9 were waited for; matrix products, arithmetic and copies ran while one was open for 1% of the time, Pallas kernels for 2%

profile of v7, /device:TPU:7, one launch (start us, length us, event | category | flops | bytes accessed | tf_op | source)
XLA Modules:
  0.0 126.1 jit_solution(4832146446887905895)
XLA Ops:
  7.2 0.7 all-gather.3.cloned.1.call-update
  7.9 10.6 %collective-permute-start = (f32[128,512]{1,0:T(8,128)}, f32[128,512]{1,0:T(8,128)S(1)}, u32[]{:S(2)}, u32[]{:S(2)}) collective-permute-start(f32[128,512]{1,0:T(8,128)} %data_ref), channel_id=1, source_target_pairs={{0,64},{64,0},{1,65},{65,1},{2,66},{66,2},{3,67},{67,3},{4,68},{68... | collective-permute-start | bytes 786440 | tf_op jit(solution)/shard_map/ppermute | solution.py:23
  18.6 2.5 %collective-permute-start.5 = (f32[128,512]{1,0:T(8,128)}, f32[128,512]{1,0:T(8,128)S(1)}, u32[]{:S(2)}, u32[]{:S(2)}) collective-permute-start(f32[128,512]{1,0:T(8,128)} %data_ref), channel_id=1, source_target_pairs={{0,48},{16,0},{32,16},{48,32},{1,49},{17,1},{33,17},{49,33},{2,50}... | collective-permute-start | bytes 786440 | tf_op jit(solution)/shard_map/ppermute | solution.py:19
  21.1 4.0 %collective-permute-start.4 = (f32[128,512]{1,0:T(8,128)}, f32[128,512]{1,0:T(8,128)S(1)}, u32[]{:S(2)}, u32[]{:S(2)}) collective-permute-start(f32[128,512]{1,0:T(8,128)} %data_ref), channel_id=1, source_target_pairs={{0,16},{16,32},{32,48},{48,0},{1,17},{17,33},{33,49},{49,1},{2,18}... | collective-permute-start | bytes 786440 | tf_op jit(solution)/shard_map/ppermute | solution.py:19
  25.1 1.9 %collective-permute-start.6 = (f32[128,512]{1,0:T(8,128)}, f32[128,512]{1,0:T(8,128)S(1)}, u32[]{:S(2)}, u32[]{:S(2)}) collective-permute-start(f32[128,512]{1,0:T(8,128)} %data_ref), channel_id=1, source_target_pairs={{0,32},{16,48},{32,0},{48,16},{1,33},{17,49},{33,1},{49,17},{2,34}... | collective-permute-start | bytes 786440 | tf_op jit(solution)/shard_map/ppermute | solution.py:19
  27.0 4.9 %collective-permute-start.3 = (f32[128,512]{1,0:T(8,128)S(1)}, f32[128,512]{1,0:T(8,128)S(1)}, u32[]{:S(2)}, u32[]{:S(2)}) collective-permute-start(f32[128,512]{1,0:T(8,128)S(1)} %collective-permute-done), channel_id=1, source_target_pairs={{0,32},{16,48},{32,0},{48,16},{1,33},{17,49},{33,1},{49,17},{2,34}... | collective-permute-start | bytes 786440 | tf_op jit(solution)/shard_map/ppermute | solution.py:19
  31.9 1.9 %collective-permute-start.2 = (f32[128,512]{1,0:T(8,128)S(1)}, f32[128,512]{1,0:T(8,128)S(1)}, u32[]{:S(2)}, u32[]{:S(2)}) collective-permute-start(f32[128,512]{1,0:T(8,128)S(1)} %collective-permute-done), channel_id=1, source_target_pairs={{0,48},{16,0},{32,16},{48,32},{1,49},{17,1},{33,17},{49,33},{2,50}... | collective-permute-start | bytes 786440 | tf_op jit(solution)/shard_map/ppermute | solution.py:19
  33.9 4.6 %collective-permute-start.1 = (f32[128,512]{1,0:T(8,128)S(1)}, f32[128,512]{1,0:T(8,128)S(1)}, u32[]{:S(2)}, u32[]{:S(2)}) collective-permute-start(f32[128,512]{1,0:T(8,128)S(1)} %collective-permute-done), channel_id=1, source_target_pairs={{0,16},{16,32},{32,48},{48,0},{1,17},{17,33},{33,49},{49,1},{2,18}... | collective-permute-start | bytes 786440 | tf_op jit(solution)/shard_map/ppermute | solution.py:19
  38.5 1.0 pad_maximum_fusion.1.mine_ref
  39.5 6.8 %collective-permute-start.7 = (f32[4,128,512]{2,1,0:T(8,128)S(1)}, f32[4,128,512]{2,1,0:T(8,128)S(1)}, u32[]{:S(2)}, u32[]{:S(2)}) collective-permute-start(f32[4,128,512]{2,1,0:T(8,128)S(1)} %pad_maximum_fusion.1.mine_ref), channel_id=1, source_target_pairs={{0,8},{8,0},{1,9},{9,1},{2,10},{10,2},{3,11},{11,3},{4,12},{12,4},... | collective-permute-start | bytes 3145736 | tf_op jit(solution)/shard_map/ppermute | solution.py:23
  46.3 2.0 %collective-permute-done.2 = f32[128,512]{1,0:T(8,128)S(1)} collective-permute-done((f32[128,512]{1,0:T(8,128)S(1)}, f32[128,512]{1,0:T(8,128)S(1)}, u32[]{:S(2)}, u32[]{:S(2)}) %collective-permute-start.2) | collective-permute-done | bytes 262176 | tf_op jit(solution)/shard_map/ppermute | solution.py:19
  48.4 2.7 %all-gather.3.cloned.1.call-done = f32[512,512]{1,0:T(8,128)} async-done(((f32[128,512]{1,0:T(8,128)}), f32[512,512]{1,0:T(8,128)}) %all-gather.3.cloned.1.call-update) | async-done | bytes 1048592 | tf_op jit(solution)/shard_map/all_gather | solution.py:152
  51.1 2.8 %collective-permute-start.8 = (f32[4,128,512]{2,1,0:T(8,128)S(1)}, f32[4,128,512]{2,1,0:T(8,128)S(1)}, u32[]{:S(2)}, u32[]{:S(2)}) collective-permute-start(f32[4,128,512]{2,1,0:T(8,128)S(1)} %pad_maximum_fusion.mine_ref), channel_id=1, source_target_pairs={{0,8},{8,0},{1,9},{9,1},{2,10},{10,2},{3,11},{11,3},{4,12},{12,4},... | collective-permute-start | bytes 3145736 | tf_op jit(solution)/shard_map/ppermute | solution.py:23
  53.9 1.2 copy-done.1
  55.6 2.1 %shard_map.42.near_value = f32[4,512,256]{2,1,0:T(8,128)S(1)} custom-call(bf16[512,512]{1,0:T(8,128)(2,1)S(1)} %get-tuple-element.10.high_ref, bf16[512,512]{1,0:T(8,128)(2,1)S(1)} %get-tuple-element.11.low_ref, f32[4,128,512]{2,1,0:T(8,128)S(1)} %pad_maximum_fusion.1.mine_ref, f32[4,128,512]{2,1,0:T(8,128)S(1)} %collective-permute-done.7.other_ref), custom_call_target="tpu_custom_call" | custom-call | flops 1610612736 | bytes 4194304 | tf_op jit(solution)/shard_map/pallas_call | solution.py:131
  57.7 3.4 %shard_map.43 = f32[512,2048]{1,0:T(8,128)} custom-call(f32[4,512,256]{2,1,0:T(8,128)S(1)} %shard_map.42.near_value, bf16[512,512]{1,0:T(8,128)(2,1)S(1)} %get-tuple-element.10.high_ref, bf16[512,512]{1,0:T(8,128)(2,1)S(1)} %get-tuple-element.11.low_ref, f32[4,128,512]{2,1,0:T(8,128)S(1)} %pad_maximum_fusion.mine_ref, ...), custom_call_target="tpu_custom_call" | custom-call | flops 1610612736 | bytes 4194304 | tf_op jit(solution)/shard_map/pallas_call | solution.py:140
  61.1 0.9 copy-done
  62.3 1.9 %collective-permute-start.9 = (f32[1,512]{1,0:T(1,128)S(1)}, f32[1,512]{1,0:T(1,128)S(1)}, u32[]{:S(2)}, u32[]{:S(2)}) collective-permute-start(f32[1,512]{1,0:T(1,128)S(1)} %shard_map.44), channel_id=1, source_target_pairs={{0,8},{8,0},{1,9},{9,1},{2,10},{10,2},{3,11},{11,3},{4,12},{12,4},... | collective-permute-start | bytes 6152 | tf_op jit(solution)/shard_map/ppermute | solution.py:23
  64.2 1.1 collective-permute-done.9
  65.3 2.4 %collective-permute-start.10 = (f32[1,512]{1,0:T(1,128)S(1)}, f32[1,512]{1,0:T(1,128)S(1)}, u32[]{:S(2)}, u32[]{:S(2)}) collective-permute-start(f32[1,512]{1,0:T(1,128)S(1)} %add.20), channel_id=1, source_target_pairs={{0,16},{16,0},{32,48},{48,32},{1,17},{17,1},{33,49},{49,33},{2,18}... | collective-permute-start | bytes 6152 | tf_op jit(solution)/shard_map/ppermute | solution.py:23
  67.7 1.9 %collective-permute-done.10 = f32[1,512]{1,0:T(1,128)S(1)} collective-permute-done((f32[1,512]{1,0:T(1,128)S(1)}, f32[1,512]{1,0:T(1,128)S(1)}, u32[]{:S(2)}, u32[]{:S(2)}) %collective-permute-start.10) | collective-permute-done | bytes 2080 | tf_op jit(solution)/shard_map/ppermute | solution.py:23
  69.7 3.0 %collective-permute-start.11 = (f32[1,512]{1,0:T(1,128)S(1)}, f32[1,512]{1,0:T(1,128)S(1)}, u32[]{:S(2)}, u32[]{:S(2)}) collective-permute-start(f32[1,512]{1,0:T(1,128)S(1)} %add.21), channel_id=1, source_target_pairs={{0,32},{16,48},{32,0},{48,16},{1,33},{17,49},{33,1},{49,17},{2,34}... | collective-permute-start | bytes 6152 | tf_op jit(solution)/shard_map/ppermute | solution.py:23
  72.6 2.9 %collective-permute-done.11 = f32[1,512]{1,0:T(1,128)S(1)} collective-permute-done((f32[1,512]{1,0:T(1,128)S(1)}, f32[1,512]{1,0:T(1,128)S(1)}, u32[]{:S(2)}, u32[]{:S(2)}) %collective-permute-start.11) | collective-permute-done | bytes 2080 | tf_op jit(solution)/shard_map/ppermute | solution.py:23
  75.5 5.1 %collective-permute-start.12 = (f32[1,512]{1,0:T(1,128)S(1)}, f32[1,512]{1,0:T(1,128)S(1)}, u32[]{:S(2)}, u32[]{:S(2)}) collective-permute-start(f32[1,512]{1,0:T(1,128)S(1)} %add.22), channel_id=1, source_target_pairs={{0,64},{64,0},{1,65},{65,1},{2,66},{66,2},{3,67},{67,3},{4,68},{68... | collective-permute-start | bytes 6152 | tf_op jit(solution)/shard_map/ppermute | solution.py:23
  80.6 3.1 %collective-permute-done.12 = f32[1,512]{1,0:T(1,128)S(1)} collective-permute-done((f32[1,512]{1,0:T(1,128)S(1)}, f32[1,512]{1,0:T(1,128)S(1)}, u32[]{:S(2)}, u32[]{:S(2)}) %collective-permute-start.12) | collective-permute-done | bytes 2080 | tf_op jit(solution)/shard_map/ppermute | solution.py:23
  83.7 1.9 %collective-permute-start.13 = (f32[1,512]{1,0:T(1,128)S(1)}, f32[1,512]{1,0:T(1,128)S(1)}, u32[]{:S(2)}, u32[]{:S(2)}) collective-permute-start(f32[1,512]{1,0:T(1,128)S(1)} %add.23), channel_id=1, source_target_pairs={{0,128},{128,0},{256,384},{384,256},{1,129},{129,1},{257,385},{385... | collective-permute-start | bytes 6152 | tf_op jit(solution)/shard_map/ppermute | solution.py:23
  85.6 2.8 %collective-permute-done.13 = f32[1,512]{1,0:T(1,128)S(1)} collective-permute-done((f32[1,512]{1,0:T(1,128)S(1)}, f32[1,512]{1,0:T(1,128)S(1)}, u32[]{:S(2)}, u32[]{:S(2)}) %collective-permute-start.13) | collective-permute-done | bytes 2080 | tf_op jit(solution)/shard_map/ppermute | solution.py:23
  88.4 2.6 %collective-permute-start.14 = (f32[1,512]{1,0:T(1,128)S(1)}, f32[1,512]{1,0:T(1,128)S(1)}, u32[]{:S(2)}, u32[]{:S(2)}) collective-permute-start(f32[1,512]{1,0:T(1,128)S(1)} %add.24), channel_id=1, source_target_pairs={{0,256},{128,384},{256,0},{384,128},{1,257},{129,385},{257,1},{385... | collective-permute-start | bytes 6152 | tf_op jit(solution)/shard_map/ppermute | solution.py:23
  91.1 3.0 %collective-permute-done.14 = f32[1,512]{1,0:T(1,128)S(1)} collective-permute-done((f32[1,512]{1,0:T(1,128)S(1)}, f32[1,512]{1,0:T(1,128)S(1)}, u32[]{:S(2)}, u32[]{:S(2)}) %collective-permute-start.14) | collective-permute-done | bytes 2080 | tf_op jit(solution)/shard_map/ppermute | solution.py:23
  94.0 0.6 add.25
  94.6 22.6 %reduce-scatter.2.cloned.1.call-done = f32[64,2048]{1,0:T(8,128)} async-done(((f32[512,2048]{1,0:T(8,128)}), f32[64,2048]{1,0:T(8,128)}) %reduce-scatter.2.cloned.1.call-update) | async-done | bytes 524304 | tf_op jit(solution)/shard_map/reduce_scatter | solution.py:164
  117.2 2.0 %reshape.10 = f32[16,4,2048]{2,1,0:T(4,128)} reshape(f32[64,2048]{1,0:T(8,128)} %reduce-scatter.2.cloned.1.call-done) | data formatting | bytes 1048576 | tf_op jit(solution)/shard_map/reshape | solution.py:168
  (23 shorter events, 0.9 us)
Async XLA Ops:
  7.2 43.9 %all-gather.3.cloned.1.call-start = ((), (), s32[]{:S(2)}) async-start(), calls=%async_computation.2 | async-start | bytes 1310720 | tf_op jit(solution)/shard_map/all_gather | solution.py:152
  7.9 109.3 %reduce-scatter.2.cloned.1.call-start = ((), (), s32[]{:S(2)}) async-start(), calls=%async_computation.1 | async-start | bytes 4718592 | tf_op jit(solution)/shard_map/reduce_scatter | solution.py:164
  7.9 19.1 %collective-permute-start = (f32[128,512]{1,0:T(8,128)}, f32[128,512]{1,0:T(8,128)S(1)}, u32[]{:S(2)}, u32[]{:S(2)}) collective-permute-start(f32[128,512]{1,0:T(8,128)} %data_ref), channel_id=1, source_target_pairs={{0,64},{64,0},{1,65},{65,1},{2,66},{66,2},{3,67},{67,3},{4,68},{68... | collective-permute-start | bytes 786440 | tf_op jit(solution)/shard_map/ppermute | solution.py:23
  18.6 15.3 %collective-permute-start.5 = (f32[128,512]{1,0:T(8,128)}, f32[128,512]{1,0:T(8,128)S(1)}, u32[]{:S(2)}, u32[]{:S(2)}) collective-permute-start(f32[128,512]{1,0:T(8,128)} %data_ref), channel_id=1, source_target_pairs={{0,48},{16,0},{32,16},{48,32},{1,49},{17,1},{33,17},{49,33},{2,50}... | collective-permute-start | bytes 786440 | tf_op jit(solution)/shard_map/ppermute | solution.py:19
  21.1 17.4 %collective-permute-start.4 = (f32[128,512]{1,0:T(8,128)}, f32[128,512]{1,0:T(8,128)S(1)}, u32[]{:S(2)}, u32[]{:S(2)}) collective-permute-start(f32[128,512]{1,0:T(8,128)} %data_ref), channel_id=1, source_target_pairs={{0,16},{16,32},{32,48},{48,0},{1,17},{17,33},{33,49},{49,1},{2,18}... | collective-permute-start | bytes 786440 | tf_op jit(solution)/shard_map/ppermute | solution.py:19
  25.1 13.3 %collective-permute-start.6 = (f32[128,512]{1,0:T(8,128)}, f32[128,512]{1,0:T(8,128)S(1)}, u32[]{:S(2)}, u32[]{:S(2)}) collective-permute-start(f32[128,512]{1,0:T(8,128)} %data_ref), channel_id=1, source_target_pairs={{0,32},{16,48},{32,0},{48,16},{1,33},{17,49},{33,1},{49,17},{2,34}... | collective-permute-start | bytes 786440 | tf_op jit(solution)/shard_map/ppermute | solution.py:19
  27.0 19.2 %collective-permute-start.3 = (f32[128,512]{1,0:T(8,128)S(1)}, f32[128,512]{1,0:T(8,128)S(1)}, u32[]{:S(2)}, u32[]{:S(2)}) collective-permute-start(f32[128,512]{1,0:T(8,128)S(1)} %collective-permute-done), channel_id=1, source_target_pairs={{0,32},{16,48},{32,0},{48,16},{1,33},{17,49},{33,1},{49,17},{2,34}... | collective-permute-start | bytes 786440 | tf_op jit(solution)/shard_map/ppermute | solution.py:19
  31.9 16.4 %collective-permute-start.2 = (f32[128,512]{1,0:T(8,128)S(1)}, f32[128,512]{1,0:T(8,128)S(1)}, u32[]{:S(2)}, u32[]{:S(2)}) collective-permute-start(f32[128,512]{1,0:T(8,128)S(1)} %collective-permute-done), channel_id=1, source_target_pairs={{0,48},{16,0},{32,16},{48,32},{1,49},{17,1},{33,17},{49,33},{2,50}... | collective-permute-start | bytes 786440 | tf_op jit(solution)/shard_map/ppermute | solution.py:19
  33.9 14.4 %collective-permute-start.1 = (f32[128,512]{1,0:T(8,128)S(1)}, f32[128,512]{1,0:T(8,128)S(1)}, u32[]{:S(2)}, u32[]{:S(2)}) collective-permute-start(f32[128,512]{1,0:T(8,128)S(1)} %collective-permute-done), channel_id=1, source_target_pairs={{0,16},{16,32},{32,48},{48,0},{1,17},{17,33},{33,49},{49,1},{2,18}... | collective-permute-start | bytes 786440 | tf_op jit(solution)/shard_map/ppermute | solution.py:19
  39.5 16.1 %collective-permute-start.7 = (f32[4,128,512]{2,1,0:T(8,128)S(1)}, f32[4,128,512]{2,1,0:T(8,128)S(1)}, u32[]{:S(2)}, u32[]{:S(2)}) collective-permute-start(f32[4,128,512]{2,1,0:T(8,128)S(1)} %pad_maximum_fusion.1.mine_ref), channel_id=1, source_target_pairs={{0,8},{8,0},{1,9},{9,1},{2,10},{10,2},{3,11},{11,3},{4,12},{12,4},... | collective-permute-start | bytes 3145736 | tf_op jit(solution)/shard_map/ppermute | solution.py:23
  51.1 6.6 %collective-permute-start.8 = (f32[4,128,512]{2,1,0:T(8,128)S(1)}, f32[4,128,512]{2,1,0:T(8,128)S(1)}, u32[]{:S(2)}, u32[]{:S(2)}) collective-permute-start(f32[4,128,512]{2,1,0:T(8,128)S(1)} %pad_maximum_fusion.mine_ref), channel_id=1, source_target_pairs={{0,8},{8,0},{1,9},{9,1},{2,10},{10,2},{3,11},{11,3},{4,12},{12,4},... | collective-permute-start | bytes 3145736 | tf_op jit(solution)/shard_map/ppermute | solution.py:23
  53.9 1.2 copy-start.1
  61.1 1.0 copy-start
  61.1 0.9 copy-start.2
  62.3 3.0 %collective-permute-start.9 = (f32[1,512]{1,0:T(1,128)S(1)}, f32[1,512]{1,0:T(1,128)S(1)}, u32[]{:S(2)}, u32[]{:S(2)}) collective-permute-start(f32[1,512]{1,0:T(1,128)S(1)} %shard_map.44), channel_id=1, source_target_pairs={{0,8},{8,0},{1,9},{9,1},{2,10},{10,2},{3,11},{11,3},{4,12},{12,4},... | collective-permute-start | bytes 6152 | tf_op jit(solution)/shard_map/ppermute | solution.py:23
  65.3 4.3 %collective-permute-start.10 = (f32[1,512]{1,0:T(1,128)S(1)}, f32[1,512]{1,0:T(1,128)S(1)}, u32[]{:S(2)}, u32[]{:S(2)}) collective-permute-start(f32[1,512]{1,0:T(1,128)S(1)} %add.20), channel_id=1, source_target_pairs={{0,16},{16,0},{32,48},{48,32},{1,17},{17,1},{33,49},{49,33},{2,18}... | collective-permute-start | bytes 6152 | tf_op jit(solution)/shard_map/ppermute | solution.py:23
  69.7 5.8 %collective-permute-start.11 = (f32[1,512]{1,0:T(1,128)S(1)}, f32[1,512]{1,0:T(1,128)S(1)}, u32[]{:S(2)}, u32[]{:S(2)}) collective-permute-start(f32[1,512]{1,0:T(1,128)S(1)} %add.21), channel_id=1, source_target_pairs={{0,32},{16,48},{32,0},{48,16},{1,33},{17,49},{33,1},{49,17},{2,34}... | collective-permute-start | bytes 6152 | tf_op jit(solution)/shard_map/ppermute | solution.py:23
  75.5 8.2 %collective-permute-start.12 = (f32[1,512]{1,0:T(1,128)S(1)}, f32[1,512]{1,0:T(1,128)S(1)}, u32[]{:S(2)}, u32[]{:S(2)}) collective-permute-start(f32[1,512]{1,0:T(1,128)S(1)} %add.22), channel_id=1, source_target_pairs={{0,64},{64,0},{1,65},{65,1},{2,66},{66,2},{3,67},{67,3},{4,68},{68... | collective-permute-start | bytes 6152 | tf_op jit(solution)/shard_map/ppermute | solution.py:23
  83.7 4.7 %collective-permute-start.13 = (f32[1,512]{1,0:T(1,128)S(1)}, f32[1,512]{1,0:T(1,128)S(1)}, u32[]{:S(2)}, u32[]{:S(2)}) collective-permute-start(f32[1,512]{1,0:T(1,128)S(1)} %add.23), channel_id=1, source_target_pairs={{0,128},{128,0},{256,384},{384,256},{1,129},{129,1},{257,385},{385... | collective-permute-start | bytes 6152 | tf_op jit(solution)/shard_map/ppermute | solution.py:23
  88.4 5.6 %collective-permute-start.14 = (f32[1,512]{1,0:T(1,128)S(1)}, f32[1,512]{1,0:T(1,128)S(1)}, u32[]{:S(2)}, u32[]{:S(2)}) collective-permute-start(f32[1,512]{1,0:T(1,128)S(1)} %add.24), channel_id=1, source_target_pairs={{0,256},{128,384},{256,0},{384,128},{1,257},{129,385},{257,1},{385... | collective-permute-start | bytes 6152 | tf_op jit(solution)/shard_map/ppermute | solution.py:23
Sparse Core Ops, SparseCore 0:
  10.1 40.9 all-gather.2
  61.2 55.9 reduce-scatter.1

commit v8 on v7

--- a/solution.py
+++ b/solution.py
@@ -9,6 +9,7 @@
 SIZES = (4, 2, 4, 2, 8)
 SAMPLES = AXES[:4]
 LANES = 128
+PARTS = 4
 HOPS = (0, 1, 3, 2)
 BUTTERFLY = (("core", 1), ("x", 1), ("x", 2), ("zh", 1), ("zl", 1), ("zl", 2))
 VMEM = pltpu.CompilerParams(vmem_limit_bytes=24 * 1024 * 1024)
@@ -95,23 +96,29 @@
 
 
 def far_kernel(near_value, high_ref, low_ref, mine_ref, other_ref, total_hbm, far_value, right, sent):
-    count, _, width = far_value.shape
+    count, rows, width = far_value.shape
     x, zh = lax.axis_index("x"), lax.axis_index("zh")
 
     def send(value, half, n):
         source = lax.rem(x + (count - HOPS[n % count]), count)
         first = pl.multiple_of((half * count + source) * width, width)
-        return pltpu.make_async_copy(
-            value.at[n % count], total_hbm.at[:, pl.ds(first, width)], sent.at[n]
-        )
-
-    copies = [send(near_value, zh, n) for n in range(count)]
-    for copy in copies:
-        copy.start()
+        for part in range(PARTS):
+            some = pl.ds(part * (rows // PARTS), rows // PARTS)
+            copies.append(
+                pltpu.make_async_copy(
+                    value.at[n % count, some, :],
+                    total_hbm.at[some, pl.ds(first, width)],
+                    sent.at[n, part],
+                )
+            )
+            copies[-1].start()
+
+    copies = []
+    for n in range(count):
+        send(near_value, zh, n)
     for n in range(count):
         far_value[n] = multiply(high_ref, low_ref, mine_ref, other_ref, n, right.at[n % 2])
-        copies.append(send(far_value, 1 - zh, count + n))
-        copies[-1].start()
+        send(far_value, 1 - zh, count + n)
     for copy in copies:
         copy.wait()
 
@@ -142,10 +149,50 @@
         in_specs=[whole] * 5,
         out_specs=pl.BlockSpec(memory_space=pltpu.HBM),
         out_shape=pltpu.HBM((rows, 2 * count * width), jnp.float32),
-        scratch_shapes=[pltpu.VMEM(value, jnp.float32), right, pltpu.SemaphoreType.DMA((2 * count,))],
+        scratch_shapes=[pltpu.VMEM(value, jnp.float32), right, pltpu.SemaphoreType.DMA((2 * count, PARTS))],
         compiler_params=VMEM,
         cost_estimate=cost,
     )(near_value, *left, far, far_other)
+
+
+def write_kernel(sum_hbm, out_hbm, summed, value, arrived, sent):
+    parts, rows, _ = summed.shape
+    lines = value.shape[1]
+    copies = [
+        pltpu.make_async_copy(sum_hbm.at[pl.ds(n * rows, rows), :], summed.at[n], arrived.at[n])
+        for n in range(parts)
+    ]
+    for copy in copies:
+        copy.start()
+    leaving = []
+    for n in range(parts):
+        copies[n].wait()
+        value[n] = summed[n].reshape(value.shape[1:])
+        leaving.append(
+            pltpu.make_async_copy(value.at[n], out_hbm.at[pl.ds(n * lines, lines)], sent.at[n])
+        )
+        leaving[-1].start()
+    for copy in leaving:
+        copy.wait()
+
+
+def write(summed, blocks):
+    rows, columns = summed.shape
+    hbm = pl.BlockSpec(memory_space=pltpu.HBM)
+    return pl.pallas_call(
+        write_kernel,
+        in_specs=[hbm],
+        out_specs=hbm,
+        out_shape=pltpu.HBM((rows // blocks, blocks, columns), jnp.float32),
+        scratch_shapes=[
+            pltpu.VMEM((PARTS, rows // PARTS, columns), jnp.float32),
+            pltpu.VMEM((PARTS, rows // PARTS // blocks, blocks, columns), jnp.float32),
+            pltpu.SemaphoreType.DMA((PARTS,)),
+            pltpu.SemaphoreType.DMA((PARTS,)),
+        ],
+        compiler_params=pltpu.CompilerParams(vmem_limit_bytes=60 * 1024 * 1024),
+        cost_estimate=pl.CostEstimate(flops=0, bytes_accessed=8 * summed.size, transcendentals=0),
+    )(summed)
 
 
 def body(log_derivs, sample_vector):
@@ -165,7 +212,7 @@
     value = term(log_derivs, sample_vector)
     for axis, bit in BUTTERFLY:
         value = value + swap(value, axis, bit)
-    return (summed.reshape(-1, blocks, summed.shape[1]), value[0])
+    return (write(summed, blocks), value[0])
 
 
 def solution(mesh):

time: 128 us -> 128 us (level)
  Pallas kernels: 6.16 us -> 8.25 us
  local copies, waits for them, and re-layouts: 4.11 us -> 2.13 us
    reshape x1 -> x0, local copies, waits for them, and re-layouts: 1.98 us -> none  [body(): return (summed.reshape(-1, blocks, summed.shape[1]), value[0])]
    pallas_call x0 -> x1, Pallas kernels: none -> 1.82 us  [write(): pl.pallas_call(write_kernel, in_specs=[hbm], out_specs=hbm, out_shape=plt...]
where the time goes in v8:
time: 128 us; the launch traced here: 126 us
  starting transfers between devices  57 us (45%)
  waiting for transfers between devices  42.8 us (33%)
  between operations  14.3 us (11%)
  Pallas kernels  8.25 us (6%)
  local copies, waits for them, and re-layouts  2.13 us (2%)
  other arithmetic  1.7 us (1%)
    ppermute x9, starting transfers between devices, swap(): lax.ppermute(value, axis, [(i, i ^ bit) for i in range(lax.axis_size(axis...  37.2 us
    reduce_scatter x1, waiting for transfers between devices, body(): summed = lax.psum_scatter(total, 'par', scatter_dimension=0, tiled=True)  22.6 us
    ppermute x6, starting transfers between devices, shift(): lax.ppermute(value, axis, [(i, (i + by) % count) for i in range(count)])  19.8 us
    ppermute x9, waiting for transfers between devices, swap(): lax.ppermute(value, axis, [(i, i ^ bit) for i in range(lax.axis_size(axis...  14.8 us
    pallas_call x1, Pallas kernels, product(): pl.pallas_call(far_kernel, in_specs=[whole] * 5, out_specs=pl.BlockSpec(m...  3.64 us
    all_gather x1, waiting for transfers between devices, body(): left = lax.all_gather(log_derivs, 'zl')  2.74 us
  transfers between devices with their start and end apart: 17, of which 9 were waited for; matrix products, arithmetic and copies ran while one was open for 1% of the time, Pallas kernels for 2%

profile of v8, /device:TPU:7, one launch (start us, length us, event | category | flops | bytes accessed | tf_op | source)
XLA Modules:
  0.0 126.2 jit_solution(14994912645919119636)
XLA Ops:
  7.2 0.7 all-gather.3.cloned.1.call-update
  7.9 10.6 %collective-permute-start = (f32[128,512]{1,0:T(8,128)}, f32[128,512]{1,0:T(8,128)S(1)}, u32[]{:S(2)}, u32[]{:S(2)}) collective-permute-start(f32[128,512]{1,0:T(8,128)} %data_ref), channel_id=1, source_target_pairs={{0,64},{64,0},{1,65},{65,1},{2,66},{66,2},{3,67},{67,3},{4,68},{68... | collective-permute-start | bytes 786440 | tf_op jit(solution)/shard_map/ppermute | solution.py:24
  18.6 2.5 %collective-permute-start.5 = (f32[128,512]{1,0:T(8,128)}, f32[128,512]{1,0:T(8,128)S(1)}, u32[]{:S(2)}, u32[]{:S(2)}) collective-permute-start(f32[128,512]{1,0:T(8,128)} %data_ref), channel_id=1, source_target_pairs={{0,48},{16,0},{32,16},{48,32},{1,49},{17,1},{33,17},{49,33},{2,50}... | collective-permute-start | bytes 786440 | tf_op jit(solution)/shard_map/ppermute | solution.py:20
  21.1 4.0 %collective-permute-start.4 = (f32[128,512]{1,0:T(8,128)}, f32[128,512]{1,0:T(8,128)S(1)}, u32[]{:S(2)}, u32[]{:S(2)}) collective-permute-start(f32[128,512]{1,0:T(8,128)} %data_ref), channel_id=1, source_target_pairs={{0,16},{16,32},{32,48},{48,0},{1,17},{17,33},{33,49},{49,1},{2,18}... | collective-permute-start | bytes 786440 | tf_op jit(solution)/shard_map/ppermute | solution.py:20
  25.1 1.9 %collective-permute-start.6 = (f32[128,512]{1,0:T(8,128)}, f32[128,512]{1,0:T(8,128)S(1)}, u32[]{:S(2)}, u32[]{:S(2)}) collective-permute-start(f32[128,512]{1,0:T(8,128)} %data_ref), channel_id=1, source_target_pairs={{0,32},{16,48},{32,0},{48,16},{1,33},{17,49},{33,1},{49,17},{2,34}... | collective-permute-start | bytes 786440 | tf_op jit(solution)/shard_map/ppermute | solution.py:20
  27.0 4.9 %collective-permute-start.3 = (f32[128,512]{1,0:T(8,128)S(1)}, f32[128,512]{1,0:T(8,128)S(1)}, u32[]{:S(2)}, u32[]{:S(2)}) collective-permute-start(f32[128,512]{1,0:T(8,128)S(1)} %collective-permute-done), channel_id=1, source_target_pairs={{0,32},{16,48},{32,0},{48,16},{1,33},{17,49},{33,1},{49,17},{2,34}... | collective-permute-start | bytes 786440 | tf_op jit(solution)/shard_map/ppermute | solution.py:20
  31.9 1.9 %collective-permute-start.2 = (f32[128,512]{1,0:T(8,128)S(1)}, f32[128,512]{1,0:T(8,128)S(1)}, u32[]{:S(2)}, u32[]{:S(2)}) collective-permute-start(f32[128,512]{1,0:T(8,128)S(1)} %collective-permute-done), channel_id=1, source_target_pairs={{0,48},{16,0},{32,16},{48,32},{1,49},{17,1},{33,17},{49,33},{2,50}... | collective-permute-start | bytes 786440 | tf_op jit(solution)/shard_map/ppermute | solution.py:20
  33.9 4.6 %collective-permute-start.1 = (f32[128,512]{1,0:T(8,128)S(1)}, f32[128,512]{1,0:T(8,128)S(1)}, u32[]{:S(2)}, u32[]{:S(2)}) collective-permute-start(f32[128,512]{1,0:T(8,128)S(1)} %collective-permute-done), channel_id=1, source_target_pairs={{0,16},{16,32},{32,48},{48,0},{1,17},{17,33},{33,49},{49,1},{2,18}... | collective-permute-start | bytes 786440 | tf_op jit(solution)/shard_map/ppermute | solution.py:20
  38.5 1.0 pad_maximum_fusion.1.mine_ref
  39.5 6.8 %collective-permute-start.7 = (f32[4,128,512]{2,1,0:T(8,128)S(1)}, f32[4,128,512]{2,1,0:T(8,128)S(1)}, u32[]{:S(2)}, u32[]{:S(2)}) collective-permute-start(f32[4,128,512]{2,1,0:T(8,128)S(1)} %pad_maximum_fusion.1.mine_ref), channel_id=1, source_target_pairs={{0,8},{8,0},{1,9},{9,1},{2,10},{10,2},{3,11},{11,3},{4,12},{12,4},... | collective-permute-start | bytes 3145736 | tf_op jit(solution)/shard_map/ppermute | solution.py:24
  46.3 2.0 %collective-permute-done.2 = f32[128,512]{1,0:T(8,128)S(1)} collective-permute-done((f32[128,512]{1,0:T(8,128)S(1)}, f32[128,512]{1,0:T(8,128)S(1)}, u32[]{:S(2)}, u32[]{:S(2)}) %collective-permute-start.2) | collective-permute-done | bytes 262176 | tf_op jit(solution)/shard_map/ppermute | solution.py:20
  48.4 2.7 %all-gather.3.cloned.1.call-done = f32[512,512]{1,0:T(8,128)} async-done(((f32[128,512]{1,0:T(8,128)}), f32[512,512]{1,0:T(8,128)}) %all-gather.3.cloned.1.call-update) | async-done | bytes 1048592 | tf_op jit(solution)/shard_map/all_gather | solution.py:199
  51.1 2.8 %collective-permute-start.8 = (f32[4,128,512]{2,1,0:T(8,128)S(1)}, f32[4,128,512]{2,1,0:T(8,128)S(1)}, u32[]{:S(2)}, u32[]{:S(2)}) collective-permute-start(f32[4,128,512]{2,1,0:T(8,128)S(1)} %pad_maximum_fusion.mine_ref), channel_id=1, source_target_pairs={{0,8},{8,0},{1,9},{9,1},{2,10},{10,2},{3,11},{11,3},{4,12},{12,4},... | collective-permute-start | bytes 3145736 | tf_op jit(solution)/shard_map/ppermute | solution.py:24
  53.9 1.2 copy-done.1
  55.6 2.1 %shard_map.42.near_value = f32[4,512,256]{2,1,0:T(8,128)S(1)} custom-call(bf16[512,512]{1,0:T(8,128)(2,1)S(1)} %get-tuple-element.10.high_ref, bf16[512,512]{1,0:T(8,128)(2,1)S(1)} %get-tuple-element.11.low_ref, f32[4,128,512]{2,1,0:T(8,128)S(1)} %pad_maximum_fusion.1.mine_ref, f32[4,128,512]{2,1,0:T(8,128)S(1)} %collective-permute-done.7.other_ref), custom_call_target="tpu_custom_call" | custom-call | flops 1610612736 | bytes 4194304 | tf_op jit(solution)/shard_map/pallas_call | solution.py:138
  57.7 3.6 %shard_map.43 = f32[512,2048]{1,0:T(8,128)} custom-call(f32[4,512,256]{2,1,0:T(8,128)S(1)} %shard_map.42.near_value, bf16[512,512]{1,0:T(8,128)(2,1)S(1)} %get-tuple-element.10.high_ref, bf16[512,512]{1,0:T(8,128)(2,1)S(1)} %get-tuple-element.11.low_ref, f32[4,128,512]{2,1,0:T(8,128)S(1)} %pad_maximum_fusion.mine_ref, ...), custom_call_target="tpu_custom_call" | custom-call | flops 1610612736 | bytes 4194304 | tf_op jit(solution)/shard_map/pallas_call | solution.py:147
  61.4 0.9 copy-done
  62.5 1.9 %collective-permute-start.9 = (f32[1,512]{1,0:T(1,128)S(1)}, f32[1,512]{1,0:T(1,128)S(1)}, u32[]{:S(2)}, u32[]{:S(2)}) collective-permute-start(f32[1,512]{1,0:T(1,128)S(1)} %shard_map.45), channel_id=1, source_target_pairs={{0,8},{8,0},{1,9},{9,1},{2,10},{10,2},{3,11},{11,3},{4,12},{12,4},... | collective-permute-start | bytes 6152 | tf_op jit(solution)/shard_map/ppermute | solution.py:24
  64.5 1.1 collective-permute-done.9
  65.6 2.4 %collective-permute-start.10 = (f32[1,512]{1,0:T(1,128)S(1)}, f32[1,512]{1,0:T(1,128)S(1)}, u32[]{:S(2)}, u32[]{:S(2)}) collective-permute-start(f32[1,512]{1,0:T(1,128)S(1)} %add.20), channel_id=1, source_target_pairs={{0,16},{16,0},{32,48},{48,32},{1,17},{17,1},{33,49},{49,33},{2,18}... | collective-permute-start | bytes 6152 | tf_op jit(solution)/shard_map/ppermute | solution.py:24
  68.0 1.9 %collective-permute-done.10 = f32[1,512]{1,0:T(1,128)S(1)} collective-permute-done((f32[1,512]{1,0:T(1,128)S(1)}, f32[1,512]{1,0:T(1,128)S(1)}, u32[]{:S(2)}, u32[]{:S(2)}) %collective-permute-start.10) | collective-permute-done | bytes 2080 | tf_op jit(solution)/shard_map/ppermute | solution.py:24
  69.9 3.0 %collective-permute-start.11 = (f32[1,512]{1,0:T(1,128)S(1)}, f32[1,512]{1,0:T(1,128)S(1)}, u32[]{:S(2)}, u32[]{:S(2)}) collective-permute-start(f32[1,512]{1,0:T(1,128)S(1)} %add.21), channel_id=1, source_target_pairs={{0,32},{16,48},{32,0},{48,16},{1,33},{17,49},{33,1},{49,17},{2,34}... | collective-permute-start | bytes 6152 | tf_op jit(solution)/shard_map/ppermute | solution.py:24
  72.9 2.9 %collective-permute-done.11 = f32[1,512]{1,0:T(1,128)S(1)} collective-permute-done((f32[1,512]{1,0:T(1,128)S(1)}, f32[1,512]{1,0:T(1,128)S(1)}, u32[]{:S(2)}, u32[]{:S(2)}) %collective-permute-start.11) | collective-permute-done | bytes 2080 | tf_op jit(solution)/shard_map/ppermute | solution.py:24
  75.7 5.1 %collective-permute-start.12 = (f32[1,512]{1,0:T(1,128)S(1)}, f32[1,512]{1,0:T(1,128)S(1)}, u32[]{:S(2)}, u32[]{:S(2)}) collective-permute-start(f32[1,512]{1,0:T(1,128)S(1)} %add.22), channel_id=1, source_target_pairs={{0,64},{64,0},{1,65},{65,1},{2,66},{66,2},{3,67},{67,3},{4,68},{68... | collective-permute-start | bytes 6152 | tf_op jit(solution)/shard_map/ppermute | solution.py:24
  80.9 3.1 %collective-permute-done.12 = f32[1,512]{1,0:T(1,128)S(1)} collective-permute-done((f32[1,512]{1,0:T(1,128)S(1)}, f32[1,512]{1,0:T(1,128)S(1)}, u32[]{:S(2)}, u32[]{:S(2)}) %collective-permute-start.12) | collective-permute-done | bytes 2080 | tf_op jit(solution)/shard_map/ppermute | solution.py:24
  84.0 1.9 %collective-permute-start.13 = (f32[1,512]{1,0:T(1,128)S(1)}, f32[1,512]{1,0:T(1,128)S(1)}, u32[]{:S(2)}, u32[]{:S(2)}) collective-permute-start(f32[1,512]{1,0:T(1,128)S(1)} %add.23), channel_id=1, source_target_pairs={{0,128},{128,0},{256,384},{384,256},{1,129},{129,1},{257,385},{385... | collective-permute-start | bytes 6152 | tf_op jit(solution)/shard_map/ppermute | solution.py:24
  85.9 2.8 %collective-permute-done.13 = f32[1,512]{1,0:T(1,128)S(1)} collective-permute-done((f32[1,512]{1,0:T(1,128)S(1)}, f32[1,512]{1,0:T(1,128)S(1)}, u32[]{:S(2)}, u32[]{:S(2)}) %collective-permute-start.13) | collective-permute-done | bytes 2080 | tf_op jit(solution)/shard_map/ppermute | solution.py:24
  88.7 2.6 %collective-permute-start.14 = (f32[1,512]{1,0:T(1,128)S(1)}, f32[1,512]{1,0:T(1,128)S(1)}, u32[]{:S(2)}, u32[]{:S(2)}) collective-permute-start(f32[1,512]{1,0:T(1,128)S(1)} %add.24), channel_id=1, source_target_pairs={{0,256},{128,384},{256,0},{384,128},{1,257},{129,385},{257,1},{385... | collective-permute-start | bytes 6152 | tf_op jit(solution)/shard_map/ppermute | solution.py:24
  91.3 3.0 %collective-permute-done.14 = f32[1,512]{1,0:T(1,128)S(1)} collective-permute-done((f32[1,512]{1,0:T(1,128)S(1)}, f32[1,512]{1,0:T(1,128)S(1)}, u32[]{:S(2)}, u32[]{:S(2)}) %collective-permute-start.14) | collective-permute-done | bytes 2080 | tf_op jit(solution)/shard_map/ppermute | solution.py:24
  94.3 0.6 add.25
  94.9 22.6 %reduce-scatter.2.cloned.1.call-done.sum_hbm = f32[64,2048]{1,0:T(8,128)} async-done(((f32[512,2048]{1,0:T(8,128)}), f32[64,2048]{1,0:T(8,128)}) %reduce-scatter.2.cloned.1.call-update) | async-done | bytes 524304 | tf_op jit(solution)/shard_map/reduce_scatter | solution.py:211
  117.5 1.8 %shard_map.44 = f32[16,4,2048]{2,1,0:T(4,128)} custom-call(f32[64,2048]{1,0:T(8,128)} %reduce-scatter.2.cloned.1.call-done.sum_hbm), custom_call_target="tpu_custom_call" | custom-call | bytes 1048576 | tf_op jit(solution)/shard_map/pallas_call | solution.py:182
  (23 shorter events, 0.9 us)
Async XLA Ops:
  7.2 43.9 %all-gather.3.cloned.1.call-start = ((), (), s32[]{:S(2)}) async-start(), calls=%async_computation.2 | async-start | bytes 1310720 | tf_op jit(solution)/shard_map/all_gather | solution.py:199
  7.9 109.6 %reduce-scatter.2.cloned.1.call-start = ((), (), s32[]{:S(2)}) async-start(), calls=%async_computation.1 | async-start | bytes 4718592 | tf_op jit(solution)/shard_map/reduce_scatter | solution.py:211
  7.9 19.1 %collective-permute-start = (f32[128,512]{1,0:T(8,128)}, f32[128,512]{1,0:T(8,128)S(1)}, u32[]{:S(2)}, u32[]{:S(2)}) collective-permute-start(f32[128,512]{1,0:T(8,128)} %data_ref), channel_id=1, source_target_pairs={{0,64},{64,0},{1,65},{65,1},{2,66},{66,2},{3,67},{67,3},{4,68},{68... | collective-permute-start | bytes 786440 | tf_op jit(solution)/shard_map/ppermute | solution.py:24
  18.6 15.3 %collective-permute-start.5 = (f32[128,512]{1,0:T(8,128)}, f32[128,512]{1,0:T(8,128)S(1)}, u32[]{:S(2)}, u32[]{:S(2)}) collective-permute-start(f32[128,512]{1,0:T(8,128)} %data_ref), channel_id=1, source_target_pairs={{0,48},{16,0},{32,16},{48,32},{1,49},{17,1},{33,17},{49,33},{2,50}... | collective-permute-start | bytes 786440 | tf_op jit(solution)/shard_map/ppermute | solution.py:20
  21.1 17.4 %collective-permute-start.4 = (f32[128,512]{1,0:T(8,128)}, f32[128,512]{1,0:T(8,128)S(1)}, u32[]{:S(2)}, u32[]{:S(2)}) collective-permute-start(f32[128,512]{1,0:T(8,128)} %data_ref), channel_id=1, source_target_pairs={{0,16},{16,32},{32,48},{48,0},{1,17},{17,33},{33,49},{49,1},{2,18}... | collective-permute-start | bytes 786440 | tf_op jit(solution)/shard_map/ppermute | solution.py:20
  25.1 13.3 %collective-permute-start.6 = (f32[128,512]{1,0:T(8,128)}, f32[128,512]{1,0:T(8,128)S(1)}, u32[]{:S(2)}, u32[]{:S(2)}) collective-permute-start(f32[128,512]{1,0:T(8,128)} %data_ref), channel_id=1, source_target_pairs={{0,32},{16,48},{32,0},{48,16},{1,33},{17,49},{33,1},{49,17},{2,34}... | collective-permute-start | bytes 786440 | tf_op jit(solution)/shard_map/ppermute | solution.py:20
  27.0 19.2 %collective-permute-start.3 = (f32[128,512]{1,0:T(8,128)S(1)}, f32[128,512]{1,0:T(8,128)S(1)}, u32[]{:S(2)}, u32[]{:S(2)}) collective-permute-start(f32[128,512]{1,0:T(8,128)S(1)} %collective-permute-done), channel_id=1, source_target_pairs={{0,32},{16,48},{32,0},{48,16},{1,33},{17,49},{33,1},{49,17},{2,34}... | collective-permute-start | bytes 786440 | tf_op jit(solution)/shard_map/ppermute | solution.py:20
  31.9 16.4 %collective-permute-start.2 = (f32[128,512]{1,0:T(8,128)S(1)}, f32[128,512]{1,0:T(8,128)S(1)}, u32[]{:S(2)}, u32[]{:S(2)}) collective-permute-start(f32[128,512]{1,0:T(8,128)S(1)} %collective-permute-done), channel_id=1, source_target_pairs={{0,48},{16,0},{32,16},{48,32},{1,49},{17,1},{33,17},{49,33},{2,50}... | collective-permute-start | bytes 786440 | tf_op jit(solution)/shard_map/ppermute | solution.py:20
  33.9 14.4 %collective-permute-start.1 = (f32[128,512]{1,0:T(8,128)S(1)}, f32[128,512]{1,0:T(8,128)S(1)}, u32[]{:S(2)}, u32[]{:S(2)}) collective-permute-start(f32[128,512]{1,0:T(8,128)S(1)} %collective-permute-done), channel_id=1, source_target_pairs={{0,16},{16,32},{32,48},{48,0},{1,17},{17,33},{33,49},{49,1},{2,18}... | collective-permute-start | bytes 786440 | tf_op jit(solution)/shard_map/ppermute | solution.py:20
  39.5 16.1 %collective-permute-start.7 = (f32[4,128,512]{2,1,0:T(8,128)S(1)}, f32[4,128,512]{2,1,0:T(8,128)S(1)}, u32[]{:S(2)}, u32[]{:S(2)}) collective-permute-start(f32[4,128,512]{2,1,0:T(8,128)S(1)} %pad_maximum_fusion.1.mine_ref), channel_id=1, source_target_pairs={{0,8},{8,0},{1,9},{9,1},{2,10},{10,2},{3,11},{11,3},{4,12},{12,4},... | collective-permute-start | bytes 3145736 | tf_op jit(solution)/shard_map/ppermute | solution.py:24
  51.1 6.6 %collective-permute-start.8 = (f32[4,128,512]{2,1,0:T(8,128)S(1)}, f32[4,128,512]{2,1,0:T(8,128)S(1)}, u32[]{:S(2)}, u32[]{:S(2)}) collective-permute-start(f32[4,128,512]{2,1,0:T(8,128)S(1)} %pad_maximum_fusion.mine_ref), channel_id=1, source_target_pairs={{0,8},{8,0},{1,9},{9,1},{2,10},{10,2},{3,11},{11,3},{4,12},{12,4},... | collective-permute-start | bytes 3145736 | tf_op jit(solution)/shard_map/ppermute | solution.py:24
  53.9 1.2 copy-start.1
  61.3 1.0 copy-start
  61.4 0.9 copy-start.2
  62.5 3.0 %collective-permute-start.9 = (f32[1,512]{1,0:T(1,128)S(1)}, f32[1,512]{1,0:T(1,128)S(1)}, u32[]{:S(2)}, u32[]{:S(2)}) collective-permute-start(f32[1,512]{1,0:T(1,128)S(1)} %shard_map.45), channel_id=1, source_target_pairs={{0,8},{8,0},{1,9},{9,1},{2,10},{10,2},{3,11},{11,3},{4,12},{12,4},... | collective-permute-start | bytes 6152 | tf_op jit(solution)/shard_map/ppermute | solution.py:24
  65.6 4.3 %collective-permute-start.10 = (f32[1,512]{1,0:T(1,128)S(1)}, f32[1,512]{1,0:T(1,128)S(1)}, u32[]{:S(2)}, u32[]{:S(2)}) collective-permute-start(f32[1,512]{1,0:T(1,128)S(1)} %add.20), channel_id=1, source_target_pairs={{0,16},{16,0},{32,48},{48,32},{1,17},{17,1},{33,49},{49,33},{2,18}... | collective-permute-start | bytes 6152 | tf_op jit(solution)/shard_map/ppermute | solution.py:24
  69.9 5.8 %collective-permute-start.11 = (f32[1,512]{1,0:T(1,128)S(1)}, f32[1,512]{1,0:T(1,128)S(1)}, u32[]{:S(2)}, u32[]{:S(2)}) collective-permute-start(f32[1,512]{1,0:T(1,128)S(1)} %add.21), channel_id=1, source_target_pairs={{0,32},{16,48},{32,0},{48,16},{1,33},{17,49},{33,1},{49,17},{2,34}... | collective-permute-start | bytes 6152 | tf_op jit(solution)/shard_map/ppermute | solution.py:24
  75.7 8.2 %collective-permute-start.12 = (f32[1,512]{1,0:T(1,128)S(1)}, f32[1,512]{1,0:T(1,128)S(1)}, u32[]{:S(2)}, u32[]{:S(2)}) collective-permute-start(f32[1,512]{1,0:T(1,128)S(1)} %add.22), channel_id=1, source_target_pairs={{0,64},{64,0},{1,65},{65,1},{2,66},{66,2},{3,67},{67,3},{4,68},{68... | collective-permute-start | bytes 6152 | tf_op jit(solution)/shard_map/ppermute | solution.py:24
  84.0 4.7 %collective-permute-start.13 = (f32[1,512]{1,0:T(1,128)S(1)}, f32[1,512]{1,0:T(1,128)S(1)}, u32[]{:S(2)}, u32[]{:S(2)}) collective-permute-start(f32[1,512]{1,0:T(1,128)S(1)} %add.23), channel_id=1, source_target_pairs={{0,128},{128,0},{256,384},{384,256},{1,129},{129,1},{257,385},{385... | collective-permute-start | bytes 6152 | tf_op jit(solution)/shard_map/ppermute | solution.py:24
  88.7 5.6 %collective-permute-start.14 = (f32[1,512]{1,0:T(1,128)S(1)}, f32[1,512]{1,0:T(1,128)S(1)}, u32[]{:S(2)}, u32[]{:S(2)}) collective-permute-start(f32[1,512]{1,0:T(1,128)S(1)} %add.24), channel_id=1, source_target_pairs={{0,256},{128,384},{256,0},{384,128},{1,257},{129,385},{257,1},{385... | collective-permute-start | bytes 6152 | tf_op jit(solution)/shard_map/ppermute | solution.py:24
Sparse Core Ops, SparseCore 0:
  10.1 40.9 all-gather.2
  61.5 55.9 reduce-scatter.1

commit v9 on v7

--- a/solution.py
+++ b/solution.py
@@ -9,6 +9,7 @@
 SIZES = (4, 2, 4, 2, 8)
 SAMPLES = AXES[:4]
 LANES = 128
+ORDER = (0, 1, 3, 2)
 HOPS = (0, 1, 3, 2)
 BUTTERFLY = (("core", 1), ("x", 1), ("x", 2), ("zh", 1), ("zl", 1), ("zl", 2))
 VMEM = pltpu.CompilerParams(vmem_limit_bytes=24 * 1024 * 1024)
@@ -56,7 +57,7 @@
     for g in range(params // LANES):
         lanes = pl.ds(g * LANES, LANES)
         for a in range(blocks):
-            rows[g, pl.ds(a, local, stride=blocks), :] = left_ref[a, :, lanes]
+            rows[g, pl.ds(ORDER[a], local, stride=blocks), :] = left_ref[a, :, lanes]
         high_ref[:, lanes], low_ref[:, lanes] = halves(rows[g])
 
 
@@ -149,7 +150,7 @@
 
 
 def body(log_derivs, sample_vector):
-    left = lax.all_gather(log_derivs, "zl")
+    left = lax.all_gather(log_derivs, "zl", axis_index_groups=[list(ORDER)])
     blocks = left.shape[0]
 
     far = swap(log_derivs, "zh", 1)

time: 128 us -> 128 us (level)
  starting transfers between devices: 57 us -> 61.3 us
  waiting for transfers between devices: 42.8 us -> 38.5 us
    ppermute x9, starting transfers between devices: 37.2 us -> 41.5 us  [swap(): lax.ppermute(value, axis, [(i, i ^ bit) for i in range(lax.axis_size(axis...]
    ppermute x9, waiting for transfers between devices: 14.8 us -> 11.1 us  [swap(): lax.ppermute(value, axis, [(i, i ^ bit) for i in range(lax.axis_size(axis...]
    all_gather x1, waiting for transfers between devices: 2.74 us -> 1.46 us  [body(): left = lax.all_gather(log_derivs, 'zl', axis_index_groups=[list(ORDER)])]
where the time goes in v9:
time: 128 us; the launch traced here: 126 us
  starting transfers between devices  61.3 us (48%)
  waiting for transfers between devices  38.5 us (30%)
  between operations  14.3 us (11%)
  Pallas kernels  6.15 us (5%)
  local copies, waits for them, and re-layouts  4.11 us (3%)
  other arithmetic  1.69 us (1%)
    ppermute x9, starting transfers between devices, swap(): lax.ppermute(value, axis, [(i, i ^ bit) for i in range(lax.axis_size(axis...  41.5 us
    reduce_scatter x1, waiting for transfers between devices, body(): summed = lax.psum_scatter(total, 'par', scatter_dimension=0, tiled=True)  23.3 us
    ppermute x6, starting transfers between devices, shift(): lax.ppermute(value, axis, [(i, (i + by) % count) for i in range(count)])  19.8 us
    ppermute x9, waiting for transfers between devices, swap(): lax.ppermute(value, axis, [(i, i ^ bit) for i in range(lax.axis_size(axis...  11.1 us
    pallas_call x1, Pallas kernels, product(): pl.pallas_call(far_kernel, in_specs=[whole] * 5, out_specs=pl.BlockSpec(m...  3.37 us
  transfers between devices with their start and end apart: 17, of which 9 were waited for; matrix products, arithmetic and copies ran while one was open for 1% of the time, Pallas kernels for 2%

profile of v9, /device:TPU:7, one launch (start us, length us, event | category | flops | bytes accessed | tf_op | source)
XLA Modules:
  0.0 126.1 jit_solution(6039387549857247645)
XLA Ops:
  7.2 0.7 all-gather.3.cloned.1.call-update
  7.9 10.6 %collective-permute-start = (f32[128,512]{1,0:T(8,128)}, f32[128,512]{1,0:T(8,128)S(1)}, u32[]{:S(2)}, u32[]{:S(2)}) collective-permute-start(f32[128,512]{1,0:T(8,128)} %data_ref), channel_id=1, source_target_pairs={{0,64},{64,0},{1,65},{65,1},{2,66},{66,2},{3,67},{67,3},{4,68},{68... | collective-permute-start | bytes 786440 | tf_op jit(solution)/shard_map/ppermute | solution.py:24
  18.6 2.5 %collective-permute-start.5 = (f32[128,512]{1,0:T(8,128)}, f32[128,512]{1,0:T(8,128)S(1)}, u32[]{:S(2)}, u32[]{:S(2)}) collective-permute-start(f32[128,512]{1,0:T(8,128)} %data_ref), channel_id=1, source_target_pairs={{0,48},{16,0},{32,16},{48,32},{1,49},{17,1},{33,17},{49,33},{2,50}... | collective-permute-start | bytes 786440 | tf_op jit(solution)/shard_map/ppermute | solution.py:20
  21.1 4.0 %collective-permute-start.4 = (f32[128,512]{1,0:T(8,128)}, f32[128,512]{1,0:T(8,128)S(1)}, u32[]{:S(2)}, u32[]{:S(2)}) collective-permute-start(f32[128,512]{1,0:T(8,128)} %data_ref), channel_id=1, source_target_pairs={{0,16},{16,32},{32,48},{48,0},{1,17},{17,33},{33,49},{49,1},{2,18}... | collective-permute-start | bytes 786440 | tf_op jit(solution)/shard_map/ppermute | solution.py:20
  25.1 1.9 %collective-permute-start.6 = (f32[128,512]{1,0:T(8,128)}, f32[128,512]{1,0:T(8,128)S(1)}, u32[]{:S(2)}, u32[]{:S(2)}) collective-permute-start(f32[128,512]{1,0:T(8,128)} %data_ref), channel_id=1, source_target_pairs={{0,32},{16,48},{32,0},{48,16},{1,33},{17,49},{33,1},{49,17},{2,34}... | collective-permute-start | bytes 786440 | tf_op jit(solution)/shard_map/ppermute | solution.py:20
  27.0 4.9 %collective-permute-start.3 = (f32[128,512]{1,0:T(8,128)S(1)}, f32[128,512]{1,0:T(8,128)S(1)}, u32[]{:S(2)}, u32[]{:S(2)}) collective-permute-start(f32[128,512]{1,0:T(8,128)S(1)} %collective-permute-done), channel_id=1, source_target_pairs={{0,32},{16,48},{32,0},{48,16},{1,33},{17,49},{33,1},{49,17},{2,34}... | collective-permute-start | bytes 786440 | tf_op jit(solution)/shard_map/ppermute | solution.py:20
  31.9 1.9 %collective-permute-start.2 = (f32[128,512]{1,0:T(8,128)S(1)}, f32[128,512]{1,0:T(8,128)S(1)}, u32[]{:S(2)}, u32[]{:S(2)}) collective-permute-start(f32[128,512]{1,0:T(8,128)S(1)} %collective-permute-done), channel_id=1, source_target_pairs={{0,48},{16,0},{32,16},{48,32},{1,49},{17,1},{33,17},{49,33},{2,50}... | collective-permute-start | bytes 786440 | tf_op jit(solution)/shard_map/ppermute | solution.py:20
  33.9 4.6 %collective-permute-start.1 = (f32[128,512]{1,0:T(8,128)S(1)}, f32[128,512]{1,0:T(8,128)S(1)}, u32[]{:S(2)}, u32[]{:S(2)}) collective-permute-start(f32[128,512]{1,0:T(8,128)S(1)} %collective-permute-done), channel_id=1, source_target_pairs={{0,16},{16,32},{32,48},{48,0},{1,17},{17,33},{33,49},{49,1},{2,18}... | collective-permute-start | bytes 786440 | tf_op jit(solution)/shard_map/ppermute | solution.py:20
  38.5 1.0 pad_maximum_fusion.1.mine_ref
  39.5 6.8 %collective-permute-start.7 = (f32[4,128,512]{2,1,0:T(8,128)S(1)}, f32[4,128,512]{2,1,0:T(8,128)S(1)}, u32[]{:S(2)}, u32[]{:S(2)}) collective-permute-start(f32[4,128,512]{2,1,0:T(8,128)S(1)} %pad_maximum_fusion.1.mine_ref), channel_id=1, source_target_pairs={{0,8},{8,0},{1,9},{9,1},{2,10},{10,2},{3,11},{11,3},{4,12},{12,4},... | collective-permute-start | bytes 3145736 | tf_op jit(solution)/shard_map/ppermute | solution.py:24
  46.3 1.9 %collective-permute-done.2 = f32[128,512]{1,0:T(8,128)S(1)} collective-permute-done((f32[128,512]{1,0:T(8,128)S(1)}, f32[128,512]{1,0:T(8,128)S(1)}, u32[]{:S(2)}, u32[]{:S(2)}) %collective-permute-start.2) | collective-permute-done | bytes 262176 | tf_op jit(solution)/shard_map/ppermute | solution.py:20
  48.3 1.5 %all-gather.3.cloned.1.call-done = f32[512,512]{1,0:T(8,128)} async-done(((f32[128,512]{1,0:T(8,128)}), f32[512,512]{1,0:T(8,128)}) %all-gather.3.cloned.1.call-update) | async-done | bytes 1048592 | tf_op jit(solution)/shard_map/all_gather | solution.py:153
  49.8 2.6 %collective-permute-start.8 = (f32[4,128,512]{2,1,0:T(8,128)S(1)}, f32[4,128,512]{2,1,0:T(8,128)S(1)}, u32[]{:S(2)}, u32[]{:S(2)}) collective-permute-start(f32[4,128,512]{2,1,0:T(8,128)S(1)} %pad_maximum_fusion.mine_ref), channel_id=1, source_target_pairs={{0,8},{8,0},{1,9},{9,1},{2,10},{10,2},{3,11},{11,3},{4,12},{12,4},... | collective-permute-start | bytes 3145736 | tf_op jit(solution)/shard_map/ppermute | solution.py:24
  52.3 1.2 copy-done.1
  54.0 2.1 %shard_map.42.near_value = f32[4,512,256]{2,1,0:T(8,128)S(1)} custom-call(bf16[512,512]{1,0:T(8,128)(2,1)S(1)} %get-tuple-element.10.high_ref, bf16[512,512]{1,0:T(8,128)(2,1)S(1)} %get-tuple-element.11.low_ref, f32[4,128,512]{2,1,0:T(8,128)S(1)} %pad_maximum_fusion.1.mine_ref, f32[4,128,512]{2,1,0:T(8,128)S(1)} %collective-permute-done.7.other_ref), custom_call_target="tpu_custom_call" | custom-call | flops 1610612736 | bytes 4194304 | tf_op jit(solution)/shard_map/pallas_call | solution.py:132
  56.1 3.4 %shard_map.43 = f32[512,2048]{1,0:T(8,128)} custom-call(f32[4,512,256]{2,1,0:T(8,128)S(1)} %shard_map.42.near_value, bf16[512,512]{1,0:T(8,128)(2,1)S(1)} %get-tuple-element.10.high_ref, bf16[512,512]{1,0:T(8,128)(2,1)S(1)} %get-tuple-element.11.low_ref, f32[4,128,512]{2,1,0:T(8,128)S(1)} %pad_maximum_fusion.mine_ref, ...), custom_call_target="tpu_custom_call" | custom-call | flops 1610612736 | bytes 4194304 | tf_op jit(solution)/shard_map/pallas_call | solution.py:141
  59.6 0.9 copy-done
  60.7 1.9 %collective-permute-start.9 = (f32[1,512]{1,0:T(1,128)S(1)}, f32[1,512]{1,0:T(1,128)S(1)}, u32[]{:S(2)}, u32[]{:S(2)}) collective-permute-start(f32[1,512]{1,0:T(1,128)S(1)} %shard_map.44), channel_id=1, source_target_pairs={{0,8},{8,0},{1,9},{9,1},{2,10},{10,2},{3,11},{11,3},{4,12},{12,4},... | collective-permute-start | bytes 6152 | tf_op jit(solution)/shard_map/ppermute | solution.py:24
  62.6 1.1 collective-permute-done.9
  63.8 2.4 %collective-permute-start.10 = (f32[1,512]{1,0:T(1,128)S(1)}, f32[1,512]{1,0:T(1,128)S(1)}, u32[]{:S(2)}, u32[]{:S(2)}) collective-permute-start(f32[1,512]{1,0:T(1,128)S(1)} %add.20), channel_id=1, source_target_pairs={{0,16},{16,0},{32,48},{48,32},{1,17},{17,1},{33,49},{49,33},{2,18}... | collective-permute-start | bytes 6152 | tf_op jit(solution)/shard_map/ppermute | solution.py:24
  66.2 1.9 %collective-permute-done.10 = f32[1,512]{1,0:T(1,128)S(1)} collective-permute-done((f32[1,512]{1,0:T(1,128)S(1)}, f32[1,512]{1,0:T(1,128)S(1)}, u32[]{:S(2)}, u32[]{:S(2)}) %collective-permute-start.10) | collective-permute-done | bytes 2080 | tf_op jit(solution)/shard_map/ppermute | solution.py:24
  68.1 3.3 %collective-permute-start.11 = (f32[1,512]{1,0:T(1,128)S(1)}, f32[1,512]{1,0:T(1,128)S(1)}, u32[]{:S(2)}, u32[]{:S(2)}) collective-permute-start(f32[1,512]{1,0:T(1,128)S(1)} %add.21), channel_id=1, source_target_pairs={{0,32},{16,48},{32,0},{48,16},{1,33},{17,49},{33,1},{49,17},{2,34}... | collective-permute-start | bytes 6152 | tf_op jit(solution)/shard_map/ppermute | solution.py:24
  71.4 2.5 %collective-permute-done.11 = f32[1,512]{1,0:T(1,128)S(1)} collective-permute-done((f32[1,512]{1,0:T(1,128)S(1)}, f32[1,512]{1,0:T(1,128)S(1)}, u32[]{:S(2)}, u32[]{:S(2)}) %collective-permute-start.11) | collective-permute-done | bytes 2080 | tf_op jit(solution)/shard_map/ppermute | solution.py:24
  73.9 6.7 %collective-permute-start.12 = (f32[1,512]{1,0:T(1,128)S(1)}, f32[1,512]{1,0:T(1,128)S(1)}, u32[]{:S(2)}, u32[]{:S(2)}) collective-permute-start(f32[1,512]{1,0:T(1,128)S(1)} %add.22), channel_id=1, source_target_pairs={{0,64},{64,0},{1,65},{65,1},{2,66},{66,2},{3,67},{67,3},{4,68},{68... | collective-permute-start | bytes 6152 | tf_op jit(solution)/shard_map/ppermute | solution.py:24
  80.6 1.5 %collective-permute-done.12 = f32[1,512]{1,0:T(1,128)S(1)} collective-permute-done((f32[1,512]{1,0:T(1,128)S(1)}, f32[1,512]{1,0:T(1,128)S(1)}, u32[]{:S(2)}, u32[]{:S(2)}) %collective-permute-start.12) | collective-permute-done | bytes 2080 | tf_op jit(solution)/shard_map/ppermute | solution.py:24
  82.1 4.2 %collective-permute-start.13 = (f32[1,512]{1,0:T(1,128)S(1)}, f32[1,512]{1,0:T(1,128)S(1)}, u32[]{:S(2)}, u32[]{:S(2)}) collective-permute-start(f32[1,512]{1,0:T(1,128)S(1)} %add.23), channel_id=1, source_target_pairs={{0,128},{128,0},{256,384},{384,256},{1,129},{129,1},{257,385},{385... | collective-permute-start | bytes 6152 | tf_op jit(solution)/shard_map/ppermute | solution.py:24
  86.4 1.4 %collective-permute-done.13 = f32[1,512]{1,0:T(1,128)S(1)} collective-permute-done((f32[1,512]{1,0:T(1,128)S(1)}, f32[1,512]{1,0:T(1,128)S(1)}, u32[]{:S(2)}, u32[]{:S(2)}) %collective-permute-start.13) | collective-permute-done | bytes 2080 | tf_op jit(solution)/shard_map/ppermute | solution.py:24
  87.7 2.9 %collective-permute-start.14 = (f32[1,512]{1,0:T(1,128)S(1)}, f32[1,512]{1,0:T(1,128)S(1)}, u32[]{:S(2)}, u32[]{:S(2)}) collective-permute-start(f32[1,512]{1,0:T(1,128)S(1)} %add.24), channel_id=1, source_target_pairs={{0,256},{128,384},{256,0},{384,128},{1,257},{129,385},{257,1},{385... | collective-permute-start | bytes 6152 | tf_op jit(solution)/shard_map/ppermute | solution.py:24
  90.6 2.7 %collective-permute-done.14 = f32[1,512]{1,0:T(1,128)S(1)} collective-permute-done((f32[1,512]{1,0:T(1,128)S(1)}, f32[1,512]{1,0:T(1,128)S(1)}, u32[]{:S(2)}, u32[]{:S(2)}) %collective-permute-start.14) | collective-permute-done | bytes 2080 | tf_op jit(solution)/shard_map/ppermute | solution.py:24
  93.4 0.6 add.25
  93.9 23.3 %reduce-scatter.2.cloned.1.call-done = f32[64,2048]{1,0:T(8,128)} async-done(((f32[512,2048]{1,0:T(8,128)}), f32[64,2048]{1,0:T(8,128)}) %reduce-scatter.2.cloned.1.call-update) | async-done | bytes 524304 | tf_op jit(solution)/shard_map/reduce_scatter | solution.py:165
  117.2 2.0 %reshape.10 = f32[16,4,2048]{2,1,0:T(4,128)} reshape(f32[64,2048]{1,0:T(8,128)} %reduce-scatter.2.cloned.1.call-done) | data formatting | bytes 1048576 | tf_op jit(solution)/shard_map/reshape | solution.py:169
  (23 shorter events, 0.9 us)
Async XLA Ops:
  7.2 42.6 %all-gather.3.cloned.1.call-start = ((), (), s32[]{:S(2)}) async-start(), calls=%async_computation.2 | async-start | bytes 1310720 | tf_op jit(solution)/shard_map/all_gather | solution.py:153
  7.9 109.3 %reduce-scatter.2.cloned.1.call-start = ((), (), s32[]{:S(2)}) async-start(), calls=%async_computation.1 | async-start | bytes 4718592 | tf_op jit(solution)/shard_map/reduce_scatter | solution.py:165
  7.9 19.1 %collective-permute-start = (f32[128,512]{1,0:T(8,128)}, f32[128,512]{1,0:T(8,128)S(1)}, u32[]{:S(2)}, u32[]{:S(2)}) collective-permute-start(f32[128,512]{1,0:T(8,128)} %data_ref), channel_id=1, source_target_pairs={{0,64},{64,0},{1,65},{65,1},{2,66},{66,2},{3,67},{67,3},{4,68},{68... | collective-permute-start | bytes 786440 | tf_op jit(solution)/shard_map/ppermute | solution.py:24
  18.6 15.3 %collective-permute-start.5 = (f32[128,512]{1,0:T(8,128)}, f32[128,512]{1,0:T(8,128)S(1)}, u32[]{:S(2)}, u32[]{:S(2)}) collective-permute-start(f32[128,512]{1,0:T(8,128)} %data_ref), channel_id=1, source_target_pairs={{0,48},{16,0},{32,16},{48,32},{1,49},{17,1},{33,17},{49,33},{2,50}... | collective-permute-start | bytes 786440 | tf_op jit(solution)/shard_map/ppermute | solution.py:20
  21.1 17.4 %collective-permute-start.4 = (f32[128,512]{1,0:T(8,128)}, f32[128,512]{1,0:T(8,128)S(1)}, u32[]{:S(2)}, u32[]{:S(2)}) collective-permute-start(f32[128,512]{1,0:T(8,128)} %data_ref), channel_id=1, source_target_pairs={{0,16},{16,32},{32,48},{48,0},{1,17},{17,33},{33,49},{49,1},{2,18}... | collective-permute-start | bytes 786440 | tf_op jit(solution)/shard_map/ppermute | solution.py:20
  25.1 13.3 %collective-permute-start.6 = (f32[128,512]{1,0:T(8,128)}, f32[128,512]{1,0:T(8,128)S(1)}, u32[]{:S(2)}, u32[]{:S(2)}) collective-permute-start(f32[128,512]{1,0:T(8,128)} %data_ref), channel_id=1, source_target_pairs={{0,32},{16,48},{32,0},{48,16},{1,33},{17,49},{33,1},{49,17},{2,34}... | collective-permute-start | bytes 786440 | tf_op jit(solution)/shard_map/ppermute | solution.py:20
  27.0 19.3 %collective-permute-start.3 = (f32[128,512]{1,0:T(8,128)S(1)}, f32[128,512]{1,0:T(8,128)S(1)}, u32[]{:S(2)}, u32[]{:S(2)}) collective-permute-start(f32[128,512]{1,0:T(8,128)S(1)} %collective-permute-done), channel_id=1, source_target_pairs={{0,32},{16,48},{32,0},{48,16},{1,33},{17,49},{33,1},{49,17},{2,34}... | collective-permute-start | bytes 786440 | tf_op jit(solution)/shard_map/ppermute | solution.py:20
  31.9 16.3 %collective-permute-start.2 = (f32[128,512]{1,0:T(8,128)S(1)}, f32[128,512]{1,0:T(8,128)S(1)}, u32[]{:S(2)}, u32[]{:S(2)}) collective-permute-start(f32[128,512]{1,0:T(8,128)S(1)} %collective-permute-done), channel_id=1, source_target_pairs={{0,48},{16,0},{32,16},{48,32},{1,49},{17,1},{33,17},{49,33},{2,50}... | collective-permute-start | bytes 786440 | tf_op jit(solution)/shard_map/ppermute | solution.py:20
  33.9 14.4 %collective-permute-start.1 = (f32[128,512]{1,0:T(8,128)S(1)}, f32[128,512]{1,0:T(8,128)S(1)}, u32[]{:S(2)}, u32[]{:S(2)}) collective-permute-start(f32[128,512]{1,0:T(8,128)S(1)} %collective-permute-done), channel_id=1, source_target_pairs={{0,16},{16,32},{32,48},{48,0},{1,17},{17,33},{33,49},{49,1},{2,18}... | collective-permute-start | bytes 786440 | tf_op jit(solution)/shard_map/ppermute | solution.py:20
  39.5 14.5 %collective-permute-start.7 = (f32[4,128,512]{2,1,0:T(8,128)S(1)}, f32[4,128,512]{2,1,0:T(8,128)S(1)}, u32[]{:S(2)}, u32[]{:S(2)}) collective-permute-start(f32[4,128,512]{2,1,0:T(8,128)S(1)} %pad_maximum_fusion.1.mine_ref), channel_id=1, source_target_pairs={{0,8},{8,0},{1,9},{9,1},{2,10},{10,2},{3,11},{11,3},{4,12},{12,4},... | collective-permute-start | bytes 3145736 | tf_op jit(solution)/shard_map/ppermute | solution.py:24
  49.8 6.4 %collective-permute-start.8 = (f32[4,128,512]{2,1,0:T(8,128)S(1)}, f32[4,128,512]{2,1,0:T(8,128)S(1)}, u32[]{:S(2)}, u32[]{:S(2)}) collective-permute-start(f32[4,128,512]{2,1,0:T(8,128)S(1)} %pad_maximum_fusion.mine_ref), channel_id=1, source_target_pairs={{0,8},{8,0},{1,9},{9,1},{2,10},{10,2},{3,11},{11,3},{4,12},{12,4},... | collective-permute-start | bytes 3145736 | tf_op jit(solution)/shard_map/ppermute | solution.py:24
  52.3 1.2 copy-start.1
  59.5 1.0 copy-start
  59.5 0.9 copy-start.2
  60.7 3.0 %collective-permute-start.9 = (f32[1,512]{1,0:T(1,128)S(1)}, f32[1,512]{1,0:T(1,128)S(1)}, u32[]{:S(2)}, u32[]{:S(2)}) collective-permute-start(f32[1,512]{1,0:T(1,128)S(1)} %shard_map.44), channel_id=1, source_target_pairs={{0,8},{8,0},{1,9},{9,1},{2,10},{10,2},{3,11},{11,3},{4,12},{12,4},... | collective-permute-start | bytes 6152 | tf_op jit(solution)/shard_map/ppermute | solution.py:24
  63.8 4.3 %collective-permute-start.10 = (f32[1,512]{1,0:T(1,128)S(1)}, f32[1,512]{1,0:T(1,128)S(1)}, u32[]{:S(2)}, u32[]{:S(2)}) collective-permute-start(f32[1,512]{1,0:T(1,128)S(1)} %add.20), channel_id=1, source_target_pairs={{0,16},{16,0},{32,48},{48,32},{1,17},{17,1},{33,49},{49,33},{2,18}... | collective-permute-start | bytes 6152 | tf_op jit(solution)/shard_map/ppermute | solution.py:24
  68.1 5.8 %collective-permute-start.11 = (f32[1,512]{1,0:T(1,128)S(1)}, f32[1,512]{1,0:T(1,128)S(1)}, u32[]{:S(2)}, u32[]{:S(2)}) collective-permute-start(f32[1,512]{1,0:T(1,128)S(1)} %add.21), channel_id=1, source_target_pairs={{0,32},{16,48},{32,0},{48,16},{1,33},{17,49},{33,1},{49,17},{2,34}... | collective-permute-start | bytes 6152 | tf_op jit(solution)/shard_map/ppermute | solution.py:24
  73.9 8.2 %collective-permute-start.12 = (f32[1,512]{1,0:T(1,128)S(1)}, f32[1,512]{1,0:T(1,128)S(1)}, u32[]{:S(2)}, u32[]{:S(2)}) collective-permute-start(f32[1,512]{1,0:T(1,128)S(1)} %add.22), channel_id=1, source_target_pairs={{0,64},{64,0},{1,65},{65,1},{2,66},{66,2},{3,67},{67,3},{4,68},{68... | collective-permute-start | bytes 6152 | tf_op jit(solution)/shard_map/ppermute | solution.py:24
  82.1 5.6 %collective-permute-start.13 = (f32[1,512]{1,0:T(1,128)S(1)}, f32[1,512]{1,0:T(1,128)S(1)}, u32[]{:S(2)}, u32[]{:S(2)}) collective-permute-start(f32[1,512]{1,0:T(1,128)S(1)} %add.23), channel_id=1, source_target_pairs={{0,128},{128,0},{256,384},{384,256},{1,129},{129,1},{257,385},{385... | collective-permute-start | bytes 6152 | tf_op jit(solution)/shard_map/ppermute | solution.py:24
  87.7 5.6 %collective-permute-start.14 = (f32[1,512]{1,0:T(1,128)S(1)}, f32[1,512]{1,0:T(1,128)S(1)}, u32[]{:S(2)}, u32[]{:S(2)}) collective-permute-start(f32[1,512]{1,0:T(1,128)S(1)} %add.24), channel_id=1, source_target_pairs={{0,256},{128,384},{256,0},{384,128},{1,257},{129,385},{257,1},{385... | collective-permute-start | bytes 6152 | tf_op jit(solution)/shard_map/ppermute | solution.py:24
Sparse Core Ops, SparseCore 0:
  10.1 39.6 all-gather.2
  59.7 57.5 reduce-scatter.1

commit v10 on v9

--- a/solution.py
+++ b/solution.py
@@ -10,7 +10,7 @@
 SAMPLES = AXES[:4]
 LANES = 128
 ORDER = (0, 1, 3, 2)
-HOPS = (0, 1, 3, 2)
+HOPS = (0, 2, 3, 1)
 BUTTERFLY = (("core", 1), ("x", 1), ("x", 2), ("zh", 1), ("zl", 1), ("zl", 2))
 VMEM = pltpu.CompilerParams(vmem_limit_bytes=24 * 1024 * 1024)
 

time: 128 us -> 128 us (level)
  waiting for transfers between devices: 38.5 us -> 41.5 us
  starting transfers between devices: 61.3 us -> 59 us
    all_gather x1, waiting for transfers between devices: 1.46 us -> 5.75 us  [body(): left = lax.all_gather(log_derivs, 'zl', axis_index_groups=[list(ORDER)])]
    ppermute x6, starting transfers between devices: 19.8 us -> 18 us  [shift(): lax.ppermute(value, axis, [(i, (i + by) % count) for i in range(count)])]
  transfers between devices with their start and end apart: 17 -> 17, of which waited for: 9 -> 10; matrix products, arithmetic and copies ran while one was open for 1% -> 1% of each run, Pallas kernels for 2% -> 2%
where the time goes in v10:
time: 128 us; the launch traced here: 127 us
  starting transfers between devices  59 us (46%)
  waiting for transfers between devices  41.5 us (32%)
  between operations  14.3 us (11%)
  Pallas kernels  6.11 us (5%)
  local copies, waits for them, and re-layouts  4.11 us (3%)
  other arithmetic  1.69 us (1%)
    ppermute x9, starting transfers between devices, swap(): lax.ppermute(value, axis, [(i, i ^ bit) for i in range(lax.axis_size(axis...  41 us
    reduce_scatter x1, waiting for transfers between devices, body(): summed = lax.psum_scatter(total, 'par', scatter_dimension=0, tiled=True)  24 us
    ppermute x6, starting transfers between devices, shift(): lax.ppermute(value, axis, [(i, (i + by) % count) for i in range(count)])  18 us
    ppermute x9, waiting for transfers between devices, swap(): lax.ppermute(value, axis, [(i, i ^ bit) for i in range(lax.axis_size(axis...  9.95 us
    all_gather x1, waiting for transfers between devices, body(): left = lax.all_gather(log_derivs, 'zl', axis_index_groups=[list(ORDER)])  5.75 us
    pallas_call x1, Pallas kernels, product(): pl.pallas_call(far_kernel, in_specs=[whole] * 5, out_specs=pl.BlockSpec(m...  3.33 us
  transfers between devices with their start and end apart: 17, of which 10 were waited for; matrix products, arithmetic and copies ran while one was open for 1% of the time, Pallas kernels for 2%

profile of v10, /device:TPU:7, one launch (start us, length us, event | category | flops | bytes accessed | tf_op | source)
XLA Modules:
  0.0 126.7 jit_solution(12448374038668743692)
XLA Ops:
  7.2 0.7 all-gather.3.cloned.1.call-update
  7.9 10.6 %collective-permute-start = (f32[128,512]{1,0:T(8,128)}, f32[128,512]{1,0:T(8,128)S(1)}, u32[]{:S(2)}, u32[]{:S(2)}) collective-permute-start(f32[128,512]{1,0:T(8,128)} %data_ref), channel_id=1, source_target_pairs={{0,64},{64,0},{1,65},{65,1},{2,66},{66,2},{3,67},{67,3},{4,68},{68... | collective-permute-start | bytes 786440 | tf_op jit(solution)/shard_map/ppermute | solution.py:24
  18.6 2.5 %collective-permute-start.5 = (f32[128,512]{1,0:T(8,128)}, f32[128,512]{1,0:T(8,128)S(1)}, u32[]{:S(2)}, u32[]{:S(2)}) collective-permute-start(f32[128,512]{1,0:T(8,128)} %data_ref), channel_id=1, source_target_pairs={{0,48},{16,0},{32,16},{48,32},{1,49},{17,1},{33,17},{49,33},{2,50}... | collective-permute-start | bytes 786440 | tf_op jit(solution)/shard_map/ppermute | solution.py:20
  21.1 2.7 %collective-permute-start.4 = (f32[128,512]{1,0:T(8,128)}, f32[128,512]{1,0:T(8,128)S(1)}, u32[]{:S(2)}, u32[]{:S(2)}) collective-permute-start(f32[128,512]{1,0:T(8,128)} %data_ref), channel_id=1, source_target_pairs={{0,32},{16,48},{32,0},{48,16},{1,33},{17,49},{33,1},{49,17},{2,34}... | collective-permute-start | bytes 786440 | tf_op jit(solution)/shard_map/ppermute | solution.py:20
  23.8 3.7 %collective-permute-start.6 = (f32[128,512]{1,0:T(8,128)}, f32[128,512]{1,0:T(8,128)S(1)}, u32[]{:S(2)}, u32[]{:S(2)}) collective-permute-start(f32[128,512]{1,0:T(8,128)} %data_ref), channel_id=1, source_target_pairs={{0,16},{16,32},{32,48},{48,0},{1,17},{17,33},{33,49},{49,1},{2,18}... | collective-permute-start | bytes 786440 | tf_op jit(solution)/shard_map/ppermute | solution.py:20
  27.6 2.5 %collective-permute-start.3 = (f32[128,512]{1,0:T(8,128)S(1)}, f32[128,512]{1,0:T(8,128)S(1)}, u32[]{:S(2)}, u32[]{:S(2)}) collective-permute-start(f32[128,512]{1,0:T(8,128)S(1)} %collective-permute-done), channel_id=1, source_target_pairs={{0,16},{16,32},{32,48},{48,0},{1,17},{17,33},{33,49},{49,1},{2,18}... | collective-permute-start | bytes 786440 | tf_op jit(solution)/shard_map/ppermute | solution.py:20
  30.1 2.8 %collective-permute-start.2 = (f32[128,512]{1,0:T(8,128)S(1)}, f32[128,512]{1,0:T(8,128)S(1)}, u32[]{:S(2)}, u32[]{:S(2)}) collective-permute-start(f32[128,512]{1,0:T(8,128)S(1)} %collective-permute-done), channel_id=1, source_target_pairs={{0,48},{16,0},{32,16},{48,32},{1,49},{17,1},{33,17},{49,33},{2,50}... | collective-permute-start | bytes 786440 | tf_op jit(solution)/shard_map/ppermute | solution.py:20
  32.9 3.8 %collective-permute-start.1 = (f32[128,512]{1,0:T(8,128)S(1)}, f32[128,512]{1,0:T(8,128)S(1)}, u32[]{:S(2)}, u32[]{:S(2)}) collective-permute-start(f32[128,512]{1,0:T(8,128)S(1)} %collective-permute-done), channel_id=1, source_target_pairs={{0,32},{16,48},{32,0},{48,16},{1,33},{17,49},{33,1},{49,17},{2,34}... | collective-permute-start | bytes 786440 | tf_op jit(solution)/shard_map/ppermute | solution.py:20
  36.6 0.7 collective-permute-done.6
  37.3 1.0 pad_maximum_fusion.1.mine_ref
  38.3 5.2 %collective-permute-start.7 = (f32[4,128,512]{2,1,0:T(8,128)S(1)}, f32[4,128,512]{2,1,0:T(8,128)S(1)}, u32[]{:S(2)}, u32[]{:S(2)}) collective-permute-start(f32[4,128,512]{2,1,0:T(8,128)S(1)} %pad_maximum_fusion.1.mine_ref), channel_id=1, source_target_pairs={{0,8},{8,0},{1,9},{9,1},{2,10},{10,2},{3,11},{11,3},{4,12},{12,4},... | collective-permute-start | bytes 3145736 | tf_op jit(solution)/shard_map/ppermute | solution.py:24
  44.0 5.7 %all-gather.3.cloned.1.call-done = f32[512,512]{1,0:T(8,128)} async-done(((f32[128,512]{1,0:T(8,128)}), f32[512,512]{1,0:T(8,128)}) %all-gather.3.cloned.1.call-update) | async-done | bytes 1048592 | tf_op jit(solution)/shard_map/all_gather | solution.py:153
  49.8 2.6 %collective-permute-start.8 = (f32[4,128,512]{2,1,0:T(8,128)S(1)}, f32[4,128,512]{2,1,0:T(8,128)S(1)}, u32[]{:S(2)}, u32[]{:S(2)}) collective-permute-start(f32[4,128,512]{2,1,0:T(8,128)S(1)} %pad_maximum_fusion.mine_ref), channel_id=1, source_target_pairs={{0,8},{8,0},{1,9},{9,1},{2,10},{10,2},{3,11},{11,3},{4,12},{12,4},... | collective-permute-start | bytes 3145736 | tf_op jit(solution)/shard_map/ppermute | solution.py:24
  52.3 1.2 copy-done.1
  54.0 2.1 %shard_map.42.near_value = f32[4,512,256]{2,1,0:T(8,128)S(1)} custom-call(bf16[512,512]{1,0:T(8,128)(2,1)S(1)} %get-tuple-element.10.high_ref, bf16[512,512]{1,0:T(8,128)(2,1)S(1)} %get-tuple-element.11.low_ref, f32[4,128,512]{2,1,0:T(8,128)S(1)} %pad_maximum_fusion.1.mine_ref, f32[4,128,512]{2,1,0:T(8,128)S(1)} %collective-permute-done.7.other_ref), custom_call_target="tpu_custom_call" | custom-call | flops 1610612736 | bytes 4194304 | tf_op jit(solution)/shard_map/pallas_call | solution.py:132
  56.1 3.3 %shard_map.43 = f32[512,2048]{1,0:T(8,128)} custom-call(f32[4,512,256]{2,1,0:T(8,128)S(1)} %shard_map.42.near_value, bf16[512,512]{1,0:T(8,128)(2,1)S(1)} %get-tuple-element.10.high_ref, bf16[512,512]{1,0:T(8,128)(2,1)S(1)} %get-tuple-element.11.low_ref, f32[4,128,512]{2,1,0:T(8,128)S(1)} %pad_maximum_fusion.mine_ref, ...), custom_call_target="tpu_custom_call" | custom-call | flops 1610612736 | bytes 4194304 | tf_op jit(solution)/shard_map/pallas_call | solution.py:141
  59.5 0.9 copy-done
  60.7 1.9 %collective-permute-start.9 = (f32[1,512]{1,0:T(1,128)S(1)}, f32[1,512]{1,0:T(1,128)S(1)}, u32[]{:S(2)}, u32[]{:S(2)}) collective-permute-start(f32[1,512]{1,0:T(1,128)S(1)} %shard_map.44), channel_id=1, source_target_pairs={{0,8},{8,0},{1,9},{9,1},{2,10},{10,2},{3,11},{11,3},{4,12},{12,4},... | collective-permute-start | bytes 6152 | tf_op jit(solution)/shard_map/ppermute | solution.py:24
  62.6 1.1 collective-permute-done.9
  63.7 2.5 %collective-permute-start.10 = (f32[1,512]{1,0:T(1,128)S(1)}, f32[1,512]{1,0:T(1,128)S(1)}, u32[]{:S(2)}, u32[]{:S(2)}) collective-permute-start(f32[1,512]{1,0:T(1,128)S(1)} %add.20), channel_id=1, source_target_pairs={{0,16},{16,0},{32,48},{48,32},{1,17},{17,1},{33,49},{49,33},{2,18}... | collective-permute-start | bytes 6152 | tf_op jit(solution)/shard_map/ppermute | solution.py:24
  66.2 1.8 %collective-permute-done.10 = f32[1,512]{1,0:T(1,128)S(1)} collective-permute-done((f32[1,512]{1,0:T(1,128)S(1)}, f32[1,512]{1,0:T(1,128)S(1)}, u32[]{:S(2)}, u32[]{:S(2)}) %collective-permute-start.10) | collective-permute-done | bytes 2080 | tf_op jit(solution)/shard_map/ppermute | solution.py:24
  68.0 3.7 %collective-permute-start.11 = (f32[1,512]{1,0:T(1,128)S(1)}, f32[1,512]{1,0:T(1,128)S(1)}, u32[]{:S(2)}, u32[]{:S(2)}) collective-permute-start(f32[1,512]{1,0:T(1,128)S(1)} %add.21), channel_id=1, source_target_pairs={{0,32},{16,48},{32,0},{48,16},{1,33},{17,49},{33,1},{49,17},{2,34}... | collective-permute-start | bytes 6152 | tf_op jit(solution)/shard_map/ppermute | solution.py:24
  71.7 2.1 %collective-permute-done.11 = f32[1,512]{1,0:T(1,128)S(1)} collective-permute-done((f32[1,512]{1,0:T(1,128)S(1)}, f32[1,512]{1,0:T(1,128)S(1)}, u32[]{:S(2)}, u32[]{:S(2)}) %collective-permute-start.11) | collective-permute-done | bytes 2080 | tf_op jit(solution)/shard_map/ppermute | solution.py:24
  73.9 6.8 %collective-permute-start.12 = (f32[1,512]{1,0:T(1,128)S(1)}, f32[1,512]{1,0:T(1,128)S(1)}, u32[]{:S(2)}, u32[]{:S(2)}) collective-permute-start(f32[1,512]{1,0:T(1,128)S(1)} %add.22), channel_id=1, source_target_pairs={{0,64},{64,0},{1,65},{65,1},{2,66},{66,2},{3,67},{67,3},{4,68},{68... | collective-permute-start | bytes 6152 | tf_op jit(solution)/shard_map/ppermute | solution.py:24
  80.7 1.4 %collective-permute-done.12 = f32[1,512]{1,0:T(1,128)S(1)} collective-permute-done((f32[1,512]{1,0:T(1,128)S(1)}, f32[1,512]{1,0:T(1,128)S(1)}, u32[]{:S(2)}, u32[]{:S(2)}) %collective-permute-start.12) | collective-permute-done | bytes 2080 | tf_op jit(solution)/shard_map/ppermute | solution.py:24
  82.1 4.2 %collective-permute-start.13 = (f32[1,512]{1,0:T(1,128)S(1)}, f32[1,512]{1,0:T(1,128)S(1)}, u32[]{:S(2)}, u32[]{:S(2)}) collective-permute-start(f32[1,512]{1,0:T(1,128)S(1)} %add.23), channel_id=1, source_target_pairs={{0,128},{128,0},{256,384},{384,256},{1,129},{129,1},{257,385},{385... | collective-permute-start | bytes 6152 | tf_op jit(solution)/shard_map/ppermute | solution.py:24
  86.3 1.4 %collective-permute-done.13 = f32[1,512]{1,0:T(1,128)S(1)} collective-permute-done((f32[1,512]{1,0:T(1,128)S(1)}, f32[1,512]{1,0:T(1,128)S(1)}, u32[]{:S(2)}, u32[]{:S(2)}) %collective-permute-start.13) | collective-permute-done | bytes 2080 | tf_op jit(solution)/shard_map/ppermute | solution.py:24
  87.7 3.5 %collective-permute-start.14 = (f32[1,512]{1,0:T(1,128)S(1)}, f32[1,512]{1,0:T(1,128)S(1)}, u32[]{:S(2)}, u32[]{:S(2)}) collective-permute-start(f32[1,512]{1,0:T(1,128)S(1)} %add.24), channel_id=1, source_target_pairs={{0,256},{128,384},{256,0},{384,128},{1,257},{129,385},{257,1},{385... | collective-permute-start | bytes 6152 | tf_op jit(solution)/shard_map/ppermute | solution.py:24
  91.2 2.1 %collective-permute-done.14 = f32[1,512]{1,0:T(1,128)S(1)} collective-permute-done((f32[1,512]{1,0:T(1,128)S(1)}, f32[1,512]{1,0:T(1,128)S(1)}, u32[]{:S(2)}, u32[]{:S(2)}) %collective-permute-start.14) | collective-permute-done | bytes 2080 | tf_op jit(solution)/shard_map/ppermute | solution.py:24
  93.3 0.6 add.25
  93.9 24.0 %reduce-scatter.2.cloned.1.call-done = f32[64,2048]{1,0:T(8,128)} async-done(((f32[512,2048]{1,0:T(8,128)}), f32[64,2048]{1,0:T(8,128)}) %reduce-scatter.2.cloned.1.call-update) | async-done | bytes 524304 | tf_op jit(solution)/shard_map/reduce_scatter | solution.py:165
  117.9 2.0 %reshape.10 = f32[16,4,2048]{2,1,0:T(4,128)} reshape(f32[64,2048]{1,0:T(8,128)} %reduce-scatter.2.cloned.1.call-done) | data formatting | bytes 1048576 | tf_op jit(solution)/shard_map/reshape | solution.py:169
  (23 shorter events, 1.3 us)
Async XLA Ops:
  7.2 42.6 %all-gather.3.cloned.1.call-start = ((), (), s32[]{:S(2)}) async-start(), calls=%async_computation.2 | async-start | bytes 1310720 | tf_op jit(solution)/shard_map/all_gather | solution.py:153
  7.9 110.0 %reduce-scatter.2.cloned.1.call-start = ((), (), s32[]{:S(2)}) async-start(), calls=%async_computation.1 | async-start | bytes 4718592 | tf_op jit(solution)/shard_map/reduce_scatter | solution.py:165
  7.9 19.6 %collective-permute-start = (f32[128,512]{1,0:T(8,128)}, f32[128,512]{1,0:T(8,128)S(1)}, u32[]{:S(2)}, u32[]{:S(2)}) collective-permute-start(f32[128,512]{1,0:T(8,128)} %data_ref), channel_id=1, source_target_pairs={{0,64},{64,0},{1,65},{65,1},{2,66},{66,2},{3,67},{67,3},{4,68},{68... | collective-permute-start | bytes 786440 | tf_op jit(solution)/shard_map/ppermute | solution.py:24
  18.6 14.3 %collective-permute-start.5 = (f32[128,512]{1,0:T(8,128)}, f32[128,512]{1,0:T(8,128)S(1)}, u32[]{:S(2)}, u32[]{:S(2)}) collective-permute-start(f32[128,512]{1,0:T(8,128)} %data_ref), channel_id=1, source_target_pairs={{0,48},{16,0},{32,16},{48,32},{1,49},{17,1},{33,17},{49,33},{2,50}... | collective-permute-start | bytes 786440 | tf_op jit(solution)/shard_map/ppermute | solution.py:20
  21.1 15.6 %collective-permute-start.4 = (f32[128,512]{1,0:T(8,128)}, f32[128,512]{1,0:T(8,128)S(1)}, u32[]{:S(2)}, u32[]{:S(2)}) collective-permute-start(f32[128,512]{1,0:T(8,128)} %data_ref), channel_id=1, source_target_pairs={{0,32},{16,48},{32,0},{48,16},{1,33},{17,49},{33,1},{49,17},{2,34}... | collective-permute-start | bytes 786440 | tf_op jit(solution)/shard_map/ppermute | solution.py:20
  23.8 13.5 %collective-permute-start.6 = (f32[128,512]{1,0:T(8,128)}, f32[128,512]{1,0:T(8,128)S(1)}, u32[]{:S(2)}, u32[]{:S(2)}) collective-permute-start(f32[128,512]{1,0:T(8,128)} %data_ref), channel_id=1, source_target_pairs={{0,16},{16,32},{32,48},{48,0},{1,17},{17,33},{33,49},{49,1},{2,18}... | collective-permute-start | bytes 786440 | tf_op jit(solution)/shard_map/ppermute | solution.py:20
  27.6 16.3 %collective-permute-start.3 = (f32[128,512]{1,0:T(8,128)S(1)}, f32[128,512]{1,0:T(8,128)S(1)}, u32[]{:S(2)}, u32[]{:S(2)}) collective-permute-start(f32[128,512]{1,0:T(8,128)S(1)} %collective-permute-done), channel_id=1, source_target_pairs={{0,16},{16,32},{32,48},{48,0},{1,17},{17,33},{33,49},{49,1},{2,18}... | collective-permute-start | bytes 786440 | tf_op jit(solution)/shard_map/ppermute | solution.py:20
  30.1 13.8 %collective-permute-start.2 = (f32[128,512]{1,0:T(8,128)S(1)}, f32[128,512]{1,0:T(8,128)S(1)}, u32[]{:S(2)}, u32[]{:S(2)}) collective-permute-start(f32[128,512]{1,0:T(8,128)S(1)} %collective-permute-done), channel_id=1, source_target_pairs={{0,48},{16,0},{32,16},{48,32},{1,49},{17,1},{33,17},{49,33},{2,50}... | collective-permute-start | bytes 786440 | tf_op jit(solution)/shard_map/ppermute | solution.py:20
  32.9 11.1 %collective-permute-start.1 = (f32[128,512]{1,0:T(8,128)S(1)}, f32[128,512]{1,0:T(8,128)S(1)}, u32[]{:S(2)}, u32[]{:S(2)}) collective-permute-start(f32[128,512]{1,0:T(8,128)S(1)} %collective-permute-done), channel_id=1, source_target_pairs={{0,32},{16,48},{32,0},{48,16},{1,33},{17,49},{33,1},{49,17},{2,34}... | collective-permute-start | bytes 786440 | tf_op jit(solution)/shard_map/ppermute | solution.py:20
  38.3 15.7 %collective-permute-start.7 = (f32[4,128,512]{2,1,0:T(8,128)S(1)}, f32[4,128,512]{2,1,0:T(8,128)S(1)}, u32[]{:S(2)}, u32[]{:S(2)}) collective-permute-start(f32[4,128,512]{2,1,0:T(8,128)S(1)} %pad_maximum_fusion.1.mine_ref), channel_id=1, source_target_pairs={{0,8},{8,0},{1,9},{9,1},{2,10},{10,2},{3,11},{11,3},{4,12},{12,4},... | collective-permute-start | bytes 3145736 | tf_op jit(solution)/shard_map/ppermute | solution.py:24
  49.8 6.4 %collective-permute-start.8 = (f32[4,128,512]{2,1,0:T(8,128)S(1)}, f32[4,128,512]{2,1,0:T(8,128)S(1)}, u32[]{:S(2)}, u32[]{:S(2)}) collective-permute-start(f32[4,128,512]{2,1,0:T(8,128)S(1)} %pad_maximum_fusion.mine_ref), channel_id=1, source_target_pairs={{0,8},{8,0},{1,9},{9,1},{2,10},{10,2},{3,11},{11,3},{4,12},{12,4},... | collective-permute-start | bytes 3145736 | tf_op jit(solution)/shard_map/ppermute | solution.py:24
  52.3 1.2 copy-start.1
  59.5 1.0 copy-start
  59.5 0.9 copy-start.2
  60.7 3.0 %collective-permute-start.9 = (f32[1,512]{1,0:T(1,128)S(1)}, f32[1,512]{1,0:T(1,128)S(1)}, u32[]{:S(2)}, u32[]{:S(2)}) collective-permute-start(f32[1,512]{1,0:T(1,128)S(1)} %shard_map.44), channel_id=1, source_target_pairs={{0,8},{8,0},{1,9},{9,1},{2,10},{10,2},{3,11},{11,3},{4,12},{12,4},... | collective-permute-start | bytes 6152 | tf_op jit(solution)/shard_map/ppermute | solution.py:24
  63.7 4.3 %collective-permute-start.10 = (f32[1,512]{1,0:T(1,128)S(1)}, f32[1,512]{1,0:T(1,128)S(1)}, u32[]{:S(2)}, u32[]{:S(2)}) collective-permute-start(f32[1,512]{1,0:T(1,128)S(1)} %add.20), channel_id=1, source_target_pairs={{0,16},{16,0},{32,48},{48,32},{1,17},{17,1},{33,49},{49,33},{2,18}... | collective-permute-start | bytes 6152 | tf_op jit(solution)/shard_map/ppermute | solution.py:24
  68.0 5.8 %collective-permute-start.11 = (f32[1,512]{1,0:T(1,128)S(1)}, f32[1,512]{1,0:T(1,128)S(1)}, u32[]{:S(2)}, u32[]{:S(2)}) collective-permute-start(f32[1,512]{1,0:T(1,128)S(1)} %add.21), channel_id=1, source_target_pairs={{0,32},{16,48},{32,0},{48,16},{1,33},{17,49},{33,1},{49,17},{2,34}... | collective-permute-start | bytes 6152 | tf_op jit(solution)/shard_map/ppermute | solution.py:24
  73.9 8.2 %collective-permute-start.12 = (f32[1,512]{1,0:T(1,128)S(1)}, f32[1,512]{1,0:T(1,128)S(1)}, u32[]{:S(2)}, u32[]{:S(2)}) collective-permute-start(f32[1,512]{1,0:T(1,128)S(1)} %add.22), channel_id=1, source_target_pairs={{0,64},{64,0},{1,65},{65,1},{2,66},{66,2},{3,67},{67,3},{4,68},{68... | collective-permute-start | bytes 6152 | tf_op jit(solution)/shard_map/ppermute | solution.py:24
  82.1 5.6 %collective-permute-start.13 = (f32[1,512]{1,0:T(1,128)S(1)}, f32[1,512]{1,0:T(1,128)S(1)}, u32[]{:S(2)}, u32[]{:S(2)}) collective-permute-start(f32[1,512]{1,0:T(1,128)S(1)} %add.23), channel_id=1, source_target_pairs={{0,128},{128,0},{256,384},{384,256},{1,129},{129,1},{257,385},{385... | collective-permute-start | bytes 6152 | tf_op jit(solution)/shard_map/ppermute | solution.py:24
  87.7 5.6 %collective-permute-start.14 = (f32[1,512]{1,0:T(1,128)S(1)}, f32[1,512]{1,0:T(1,128)S(1)}, u32[]{:S(2)}, u32[]{:S(2)}) collective-permute-start(f32[1,512]{1,0:T(1,128)S(1)} %add.24), channel_id=1, source_target_pairs={{0,256},{128,384},{256,0},{384,128},{1,257},{129,385},{257,1},{385... | collective-permute-start | bytes 6152 | tf_op jit(solution)/shard_map/ppermute | solution.py:24
Sparse Core Ops, SparseCore 0:
  10.1 39.6 all-gather.2
  59.6 58.2 reduce-scatter.1

commit v11 on v9

--- a/solution.py
+++ b/solution.py
@@ -96,23 +96,33 @@
 
 
 def far_kernel(near_value, high_ref, low_ref, mine_ref, other_ref, total_hbm, far_value, right, sent):
-    count, _, width = far_value.shape
+    count, rows, width = far_value.shape
     x, zh = lax.axis_index("x"), lax.axis_index("zh")
 
-    def send(value, half, n):
+    def send(value, half, n, part, parts):
         source = lax.rem(x + (count - HOPS[n % count]), count)
         first = pl.multiple_of((half * count + source) * width, width)
-        return pltpu.make_async_copy(
-            value.at[n % count], total_hbm.at[:, pl.ds(first, width)], sent.at[n]
+        some = pl.ds(part * (rows // parts), rows // parts)
+        copies.append(
+            pltpu.make_async_copy(
+                value.at[n % count, some, :],
+                total_hbm.at[some, pl.ds(first, width)],
+                sent.at[len(copies)],
+            )
         )
+        copies[-1].start()
 
-    copies = [send(near_value, zh, n) for n in range(count)]
-    for copy in copies:
-        copy.start()
+    copies = []
     for n in range(count):
-        far_value[n] = multiply(high_ref, low_ref, mine_ref, other_ref, n, right.at[n % 2])
-        copies.append(send(far_value, 1 - zh, count + n))
-        copies[-1].start()
+        send(near_value, zh, n, 0, 1)
+    for n in range(count):
+        parts = 2 if n == count - 1 else 1
+        for part in range(parts):
+            some = pl.ds(part * (rows // parts), rows // parts)
+            far_value[n, some, :] = multiply(
+                high_ref.at[some], low_ref.at[some], mine_ref, other_ref, n, right.at[n % 2]
+            )
+            send(far_value, 1 - zh, count + n, part, parts)
     for copy in copies:
         copy.wait()
 
@@ -143,7 +153,7 @@
         in_specs=[whole] * 5,
         out_specs=pl.BlockSpec(memory_space=pltpu.HBM),
         out_shape=pltpu.HBM((rows, 2 * count * width), jnp.float32),
-        scratch_shapes=[pltpu.VMEM(value, jnp.float32), right, pltpu.SemaphoreType.DMA((2 * count,))],
+        scratch_shapes=[pltpu.VMEM(value, jnp.float32), right, pltpu.SemaphoreType.DMA((2 * count + 1,))],
         compiler_params=VMEM,
         cost_estimate=cost,
     )(near_value, *left, far, far_other)

time: 128 us -> 128 us (level)
  no operation moved by 1% of the time
where the time goes in v11:
time: 128 us; the launch traced here: 126 us
  starting transfers between devices  61.5 us (48%)
  waiting for transfers between devices  38.4 us (30%)
  between operations  14.3 us (11%)
  Pallas kernels  6.22 us (5%)
  local copies, waits for them, and re-layouts  4.11 us (3%)
  other arithmetic  1.69 us (1%)
    ppermute x9, starting transfers between devices, swap(): lax.ppermute(value, axis, [(i, i ^ bit) for i in range(lax.axis_size(axis...  41.6 us
    reduce_scatter x1, waiting for transfers between devices, body(): summed = lax.psum_scatter(total, 'par', scatter_dimension=0, tiled=True)  23.4 us
    ppermute x6, starting transfers between devices, shift(): lax.ppermute(value, axis, [(i, (i + by) % count) for i in range(count)])  19.8 us
    ppermute x9, waiting for transfers between devices, swap(): lax.ppermute(value, axis, [(i, i ^ bit) for i in range(lax.axis_size(axis...  11 us
    pallas_call x1, Pallas kernels, product(): pl.pallas_call(far_kernel, in_specs=[whole] * 5, out_specs=pl.BlockSpec(m...  3.44 us
  transfers between devices with their start and end apart: 17, of which 9 were waited for; matrix products, arithmetic and copies ran while one was open for 1% of the time, Pallas kernels for 2%

profile of v11, /device:TPU:7, one launch (start us, length us, event | category | flops | bytes accessed | tf_op | source)
XLA Modules:
  0.0 126.2 jit_solution(10657719168322640371)
XLA Ops:
  7.2 0.7 all-gather.3.cloned.1.call-update
  7.9 10.6 %collective-permute-start = (f32[128,512]{1,0:T(8,128)}, f32[128,512]{1,0:T(8,128)S(1)}, u32[]{:S(2)}, u32[]{:S(2)}) collective-permute-start(f32[128,512]{1,0:T(8,128)} %data_ref), channel_id=1, source_target_pairs={{0,64},{64,0},{1,65},{65,1},{2,66},{66,2},{3,67},{67,3},{4,68},{68... | collective-permute-start | bytes 786440 | tf_op jit(solution)/shard_map/ppermute | solution.py:24
  18.6 2.5 %collective-permute-start.5 = (f32[128,512]{1,0:T(8,128)}, f32[128,512]{1,0:T(8,128)S(1)}, u32[]{:S(2)}, u32[]{:S(2)}) collective-permute-start(f32[128,512]{1,0:T(8,128)} %data_ref), channel_id=1, source_target_pairs={{0,48},{16,0},{32,16},{48,32},{1,49},{17,1},{33,17},{49,33},{2,50}... | collective-permute-start | bytes 786440 | tf_op jit(solution)/shard_map/ppermute | solution.py:20
  21.1 4.0 %collective-permute-start.4 = (f32[128,512]{1,0:T(8,128)}, f32[128,512]{1,0:T(8,128)S(1)}, u32[]{:S(2)}, u32[]{:S(2)}) collective-permute-start(f32[128,512]{1,0:T(8,128)} %data_ref), channel_id=1, source_target_pairs={{0,16},{16,32},{32,48},{48,0},{1,17},{17,33},{33,49},{49,1},{2,18}... | collective-permute-start | bytes 786440 | tf_op jit(solution)/shard_map/ppermute | solution.py:20
  25.1 1.9 %collective-permute-start.6 = (f32[128,512]{1,0:T(8,128)}, f32[128,512]{1,0:T(8,128)S(1)}, u32[]{:S(2)}, u32[]{:S(2)}) collective-permute-start(f32[128,512]{1,0:T(8,128)} %data_ref), channel_id=1, source_target_pairs={{0,32},{16,48},{32,0},{48,16},{1,33},{17,49},{33,1},{49,17},{2,34}... | collective-permute-start | bytes 786440 | tf_op jit(solution)/shard_map/ppermute | solution.py:20
  27.0 4.9 %collective-permute-start.3 = (f32[128,512]{1,0:T(8,128)S(1)}, f32[128,512]{1,0:T(8,128)S(1)}, u32[]{:S(2)}, u32[]{:S(2)}) collective-permute-start(f32[128,512]{1,0:T(8,128)S(1)} %collective-permute-done), channel_id=1, source_target_pairs={{0,32},{16,48},{32,0},{48,16},{1,33},{17,49},{33,1},{49,17},{2,34}... | collective-permute-start | bytes 786440 | tf_op jit(solution)/shard_map/ppermute | solution.py:20
  31.9 1.9 %collective-permute-start.2 = (f32[128,512]{1,0:T(8,128)S(1)}, f32[128,512]{1,0:T(8,128)S(1)}, u32[]{:S(2)}, u32[]{:S(2)}) collective-permute-start(f32[128,512]{1,0:T(8,128)S(1)} %collective-permute-done), channel_id=1, source_target_pairs={{0,48},{16,0},{32,16},{48,32},{1,49},{17,1},{33,17},{49,33},{2,50}... | collective-permute-start | bytes 786440 | tf_op jit(solution)/shard_map/ppermute | solution.py:20
  33.9 4.6 %collective-permute-start.1 = (f32[128,512]{1,0:T(8,128)S(1)}, f32[128,512]{1,0:T(8,128)S(1)}, u32[]{:S(2)}, u32[]{:S(2)}) collective-permute-start(f32[128,512]{1,0:T(8,128)S(1)} %collective-permute-done), channel_id=1, source_target_pairs={{0,16},{16,32},{32,48},{48,0},{1,17},{17,33},{33,49},{49,1},{2,18}... | collective-permute-start | bytes 786440 | tf_op jit(solution)/shard_map/ppermute | solution.py:20
  38.5 1.0 pad_maximum_fusion.1.mine_ref
  39.5 6.8 %collective-permute-start.7 = (f32[4,128,512]{2,1,0:T(8,128)S(1)}, f32[4,128,512]{2,1,0:T(8,128)S(1)}, u32[]{:S(2)}, u32[]{:S(2)}) collective-permute-start(f32[4,128,512]{2,1,0:T(8,128)S(1)} %pad_maximum_fusion.1.mine_ref), channel_id=1, source_target_pairs={{0,8},{8,0},{1,9},{9,1},{2,10},{10,2},{3,11},{11,3},{4,12},{12,4},... | collective-permute-start | bytes 3145736 | tf_op jit(solution)/shard_map/ppermute | solution.py:24
  46.3 1.9 %collective-permute-done.2 = f32[128,512]{1,0:T(8,128)S(1)} collective-permute-done((f32[128,512]{1,0:T(8,128)S(1)}, f32[128,512]{1,0:T(8,128)S(1)}, u32[]{:S(2)}, u32[]{:S(2)}) %collective-permute-start.2) | collective-permute-done | bytes 262176 | tf_op jit(solution)/shard_map/ppermute | solution.py:20
  48.3 1.5 %all-gather.3.cloned.1.call-done = f32[512,512]{1,0:T(8,128)} async-done(((f32[128,512]{1,0:T(8,128)}), f32[512,512]{1,0:T(8,128)}) %all-gather.3.cloned.1.call-update) | async-done | bytes 1048592 | tf_op jit(solution)/shard_map/all_gather | solution.py:163
  49.8 2.6 %collective-permute-start.8 = (f32[4,128,512]{2,1,0:T(8,128)S(1)}, f32[4,128,512]{2,1,0:T(8,128)S(1)}, u32[]{:S(2)}, u32[]{:S(2)}) collective-permute-start(f32[4,128,512]{2,1,0:T(8,128)S(1)} %pad_maximum_fusion.mine_ref), channel_id=1, source_target_pairs={{0,8},{8,0},{1,9},{9,1},{2,10},{10,2},{3,11},{11,3},{4,12},{12,4},... | collective-permute-start | bytes 3145736 | tf_op jit(solution)/shard_map/ppermute | solution.py:24
  52.3 1.2 copy-done.1
  54.0 2.1 %shard_map.42.near_value = f32[4,512,256]{2,1,0:T(8,128)S(1)} custom-call(bf16[512,512]{1,0:T(8,128)(2,1)S(1)} %get-tuple-element.10.high_ref, bf16[512,512]{1,0:T(8,128)(2,1)S(1)} %get-tuple-element.11.low_ref, f32[4,128,512]{2,1,0:T(8,128)S(1)} %pad_maximum_fusion.1.mine_ref, f32[4,128,512]{2,1,0:T(8,128)S(1)} %collective-permute-done.7.other_ref), custom_call_target="tpu_custom_call" | custom-call | flops 1610612736 | bytes 4194304 | tf_op jit(solution)/shard_map/pallas_call | solution.py:142
  56.1 3.4 %shard_map.43 = f32[512,2048]{1,0:T(8,128)} custom-call(f32[4,512,256]{2,1,0:T(8,128)S(1)} %shard_map.42.near_value, bf16[512,512]{1,0:T(8,128)(2,1)S(1)} %get-tuple-element.10.high_ref, bf16[512,512]{1,0:T(8,128)(2,1)S(1)} %get-tuple-element.11.low_ref, f32[4,128,512]{2,1,0:T(8,128)S(1)} %pad_maximum_fusion.mine_ref, ...), custom_call_target="tpu_custom_call" | custom-call | flops 1610612736 | bytes 4194304 | tf_op jit(solution)/shard_map/pallas_call | solution.py:151
  59.6 0.9 copy-done
  60.8 1.9 %collective-permute-start.9 = (f32[1,512]{1,0:T(1,128)S(1)}, f32[1,512]{1,0:T(1,128)S(1)}, u32[]{:S(2)}, u32[]{:S(2)}) collective-permute-start(f32[1,512]{1,0:T(1,128)S(1)} %shard_map.44), channel_id=1, source_target_pairs={{0,8},{8,0},{1,9},{9,1},{2,10},{10,2},{3,11},{11,3},{4,12},{12,4},... | collective-permute-start | bytes 6152 | tf_op jit(solution)/shard_map/ppermute | solution.py:24
  62.7 1.1 collective-permute-done.9
  63.8 2.5 %collective-permute-start.10 = (f32[1,512]{1,0:T(1,128)S(1)}, f32[1,512]{1,0:T(1,128)S(1)}, u32[]{:S(2)}, u32[]{:S(2)}) collective-permute-start(f32[1,512]{1,0:T(1,128)S(1)} %add.20), channel_id=1, source_target_pairs={{0,16},{16,0},{32,48},{48,32},{1,17},{17,1},{33,49},{49,33},{2,18}... | collective-permute-start | bytes 6152 | tf_op jit(solution)/shard_map/ppermute | solution.py:24
  66.3 1.9 %collective-permute-done.10 = f32[1,512]{1,0:T(1,128)S(1)} collective-permute-done((f32[1,512]{1,0:T(1,128)S(1)}, f32[1,512]{1,0:T(1,128)S(1)}, u32[]{:S(2)}, u32[]{:S(2)}) %collective-permute-start.10) | collective-permute-done | bytes 2080 | tf_op jit(solution)/shard_map/ppermute | solution.py:24
  68.1 3.4 %collective-permute-start.11 = (f32[1,512]{1,0:T(1,128)S(1)}, f32[1,512]{1,0:T(1,128)S(1)}, u32[]{:S(2)}, u32[]{:S(2)}) collective-permute-start(f32[1,512]{1,0:T(1,128)S(1)} %add.21), channel_id=1, source_target_pairs={{0,32},{16,48},{32,0},{48,16},{1,33},{17,49},{33,1},{49,17},{2,34}... | collective-permute-start | bytes 6152 | tf_op jit(solution)/shard_map/ppermute | solution.py:24
  71.5 2.4 %collective-permute-done.11 = f32[1,512]{1,0:T(1,128)S(1)} collective-permute-done((f32[1,512]{1,0:T(1,128)S(1)}, f32[1,512]{1,0:T(1,128)S(1)}, u32[]{:S(2)}, u32[]{:S(2)}) %collective-permute-start.11) | collective-permute-done | bytes 2080 | tf_op jit(solution)/shard_map/ppermute | solution.py:24
  74.0 6.8 %collective-permute-start.12 = (f32[1,512]{1,0:T(1,128)S(1)}, f32[1,512]{1,0:T(1,128)S(1)}, u32[]{:S(2)}, u32[]{:S(2)}) collective-permute-start(f32[1,512]{1,0:T(1,128)S(1)} %add.22), channel_id=1, source_target_pairs={{0,64},{64,0},{1,65},{65,1},{2,66},{66,2},{3,67},{67,3},{4,68},{68... | collective-permute-start | bytes 6152 | tf_op jit(solution)/shard_map/ppermute | solution.py:24
  80.8 1.4 %collective-permute-done.12 = f32[1,512]{1,0:T(1,128)S(1)} collective-permute-done((f32[1,512]{1,0:T(1,128)S(1)}, f32[1,512]{1,0:T(1,128)S(1)}, u32[]{:S(2)}, u32[]{:S(2)}) %collective-permute-start.12) | collective-permute-done | bytes 2080 | tf_op jit(solution)/shard_map/ppermute | solution.py:24
  82.2 4.2 %collective-permute-start.13 = (f32[1,512]{1,0:T(1,128)S(1)}, f32[1,512]{1,0:T(1,128)S(1)}, u32[]{:S(2)}, u32[]{:S(2)}) collective-permute-start(f32[1,512]{1,0:T(1,128)S(1)} %add.23), channel_id=1, source_target_pairs={{0,128},{128,0},{256,384},{384,256},{1,129},{129,1},{257,385},{385... | collective-permute-start | bytes 6152 | tf_op jit(solution)/shard_map/ppermute | solution.py:24
  86.4 1.4 %collective-permute-done.13 = f32[1,512]{1,0:T(1,128)S(1)} collective-permute-done((f32[1,512]{1,0:T(1,128)S(1)}, f32[1,512]{1,0:T(1,128)S(1)}, u32[]{:S(2)}, u32[]{:S(2)}) %collective-permute-start.13) | collective-permute-done | bytes 2080 | tf_op jit(solution)/shard_map/ppermute | solution.py:24
  87.8 2.9 %collective-permute-start.14 = (f32[1,512]{1,0:T(1,128)S(1)}, f32[1,512]{1,0:T(1,128)S(1)}, u32[]{:S(2)}, u32[]{:S(2)}) collective-permute-start(f32[1,512]{1,0:T(1,128)S(1)} %add.24), channel_id=1, source_target_pairs={{0,256},{128,384},{256,0},{384,128},{1,257},{129,385},{257,1},{385... | collective-permute-start | bytes 6152 | tf_op jit(solution)/shard_map/ppermute | solution.py:24
  90.7 2.7 %collective-permute-done.14 = f32[1,512]{1,0:T(1,128)S(1)} collective-permute-done((f32[1,512]{1,0:T(1,128)S(1)}, f32[1,512]{1,0:T(1,128)S(1)}, u32[]{:S(2)}, u32[]{:S(2)}) %collective-permute-start.14) | collective-permute-done | bytes 2080 | tf_op jit(solution)/shard_map/ppermute | solution.py:24
  93.4 0.6 add.25
  94.0 23.4 %reduce-scatter.2.cloned.1.call-done = f32[64,2048]{1,0:T(8,128)} async-done(((f32[512,2048]{1,0:T(8,128)}), f32[64,2048]{1,0:T(8,128)}) %reduce-scatter.2.cloned.1.call-update) | async-done | bytes 524304 | tf_op jit(solution)/shard_map/reduce_scatter | solution.py:175
  117.4 2.0 %reshape.10 = f32[16,4,2048]{2,1,0:T(4,128)} reshape(f32[64,2048]{1,0:T(8,128)} %reduce-scatter.2.cloned.1.call-done) | data formatting | bytes 1048576 | tf_op jit(solution)/shard_map/reshape | solution.py:179
  (23 shorter events, 0.9 us)
Async XLA Ops:
  7.2 42.6 %all-gather.3.cloned.1.call-start = ((), (), s32[]{:S(2)}) async-start(), calls=%async_computation.2 | async-start | bytes 1310720 | tf_op jit(solution)/shard_map/all_gather | solution.py:163
  7.9 109.5 %reduce-scatter.2.cloned.1.call-start = ((), (), s32[]{:S(2)}) async-start(), calls=%async_computation.1 | async-start | bytes 4718592 | tf_op jit(solution)/shard_map/reduce_scatter | solution.py:175
  7.9 19.1 %collective-permute-start = (f32[128,512]{1,0:T(8,128)}, f32[128,512]{1,0:T(8,128)S(1)}, u32[]{:S(2)}, u32[]{:S(2)}) collective-permute-start(f32[128,512]{1,0:T(8,128)} %data_ref), channel_id=1, source_target_pairs={{0,64},{64,0},{1,65},{65,1},{2,66},{66,2},{3,67},{67,3},{4,68},{68... | collective-permute-start | bytes 786440 | tf_op jit(solution)/shard_map/ppermute | solution.py:24
  18.6 15.3 %collective-permute-start.5 = (f32[128,512]{1,0:T(8,128)}, f32[128,512]{1,0:T(8,128)S(1)}, u32[]{:S(2)}, u32[]{:S(2)}) collective-permute-start(f32[128,512]{1,0:T(8,128)} %data_ref), channel_id=1, source_target_pairs={{0,48},{16,0},{32,16},{48,32},{1,49},{17,1},{33,17},{49,33},{2,50}... | collective-permute-start | bytes 786440 | tf_op jit(solution)/shard_map/ppermute | solution.py:20
  21.1 17.4 %collective-permute-start.4 = (f32[128,512]{1,0:T(8,128)}, f32[128,512]{1,0:T(8,128)S(1)}, u32[]{:S(2)}, u32[]{:S(2)}) collective-permute-start(f32[128,512]{1,0:T(8,128)} %data_ref), channel_id=1, source_target_pairs={{0,16},{16,32},{32,48},{48,0},{1,17},{17,33},{33,49},{49,1},{2,18}... | collective-permute-start | bytes 786440 | tf_op jit(solution)/shard_map/ppermute | solution.py:20
  25.1 13.3 %collective-permute-start.6 = (f32[128,512]{1,0:T(8,128)}, f32[128,512]{1,0:T(8,128)S(1)}, u32[]{:S(2)}, u32[]{:S(2)}) collective-permute-start(f32[128,512]{1,0:T(8,128)} %data_ref), channel_id=1, source_target_pairs={{0,32},{16,48},{32,0},{48,16},{1,33},{17,49},{33,1},{49,17},{2,34}... | collective-permute-start | bytes 786440 | tf_op jit(solution)/shard_map/ppermute | solution.py:20
  27.0 19.3 %collective-permute-start.3 = (f32[128,512]{1,0:T(8,128)S(1)}, f32[128,512]{1,0:T(8,128)S(1)}, u32[]{:S(2)}, u32[]{:S(2)}) collective-permute-start(f32[128,512]{1,0:T(8,128)S(1)} %collective-permute-done), channel_id=1, source_target_pairs={{0,32},{16,48},{32,0},{48,16},{1,33},{17,49},{33,1},{49,17},{2,34}... | collective-permute-start | bytes 786440 | tf_op jit(solution)/shard_map/ppermute | solution.py:20
  31.9 16.3 %collective-permute-start.2 = (f32[128,512]{1,0:T(8,128)S(1)}, f32[128,512]{1,0:T(8,128)S(1)}, u32[]{:S(2)}, u32[]{:S(2)}) collective-permute-start(f32[128,512]{1,0:T(8,128)S(1)} %collective-permute-done), channel_id=1, source_target_pairs={{0,48},{16,0},{32,16},{48,32},{1,49},{17,1},{33,17},{49,33},{2,50}... | collective-permute-start | bytes 786440 | tf_op jit(solution)/shard_map/ppermute | solution.py:20
  33.9 14.4 %collective-permute-start.1 = (f32[128,512]{1,0:T(8,128)S(1)}, f32[128,512]{1,0:T(8,128)S(1)}, u32[]{:S(2)}, u32[]{:S(2)}) collective-permute-start(f32[128,512]{1,0:T(8,128)S(1)} %collective-permute-done), channel_id=1, source_target_pairs={{0,16},{16,32},{32,48},{48,0},{1,17},{17,33},{33,49},{49,1},{2,18}... | collective-permute-start | bytes 786440 | tf_op jit(solution)/shard_map/ppermute | solution.py:20
  39.5 14.5 %collective-permute-start.7 = (f32[4,128,512]{2,1,0:T(8,128)S(1)}, f32[4,128,512]{2,1,0:T(8,128)S(1)}, u32[]{:S(2)}, u32[]{:S(2)}) collective-permute-start(f32[4,128,512]{2,1,0:T(8,128)S(1)} %pad_maximum_fusion.1.mine_ref), channel_id=1, source_target_pairs={{0,8},{8,0},{1,9},{9,1},{2,10},{10,2},{3,11},{11,3},{4,12},{12,4},... | collective-permute-start | bytes 3145736 | tf_op jit(solution)/shard_map/ppermute | solution.py:24
  49.8 6.4 %collective-permute-start.8 = (f32[4,128,512]{2,1,0:T(8,128)S(1)}, f32[4,128,512]{2,1,0:T(8,128)S(1)}, u32[]{:S(2)}, u32[]{:S(2)}) collective-permute-start(f32[4,128,512]{2,1,0:T(8,128)S(1)} %pad_maximum_fusion.mine_ref), channel_id=1, source_target_pairs={{0,8},{8,0},{1,9},{9,1},{2,10},{10,2},{3,11},{11,3},{4,12},{12,4},... | collective-permute-start | bytes 3145736 | tf_op jit(solution)/shard_map/ppermute | solution.py:24
  52.3 1.2 copy-start.1
  59.6 1.0 copy-start
  59.6 0.9 copy-start.2
  60.8 3.0 %collective-permute-start.9 = (f32[1,512]{1,0:T(1,128)S(1)}, f32[1,512]{1,0:T(1,128)S(1)}, u32[]{:S(2)}, u32[]{:S(2)}) collective-permute-start(f32[1,512]{1,0:T(1,128)S(1)} %shard_map.44), channel_id=1, source_target_pairs={{0,8},{8,0},{1,9},{9,1},{2,10},{10,2},{3,11},{11,3},{4,12},{12,4},... | collective-permute-start | bytes 6152 | tf_op jit(solution)/shard_map/ppermute | solution.py:24
  63.8 4.3 %collective-permute-start.10 = (f32[1,512]{1,0:T(1,128)S(1)}, f32[1,512]{1,0:T(1,128)S(1)}, u32[]{:S(2)}, u32[]{:S(2)}) collective-permute-start(f32[1,512]{1,0:T(1,128)S(1)} %add.20), channel_id=1, source_target_pairs={{0,16},{16,0},{32,48},{48,32},{1,17},{17,1},{33,49},{49,33},{2,18}... | collective-permute-start | bytes 6152 | tf_op jit(solution)/shard_map/ppermute | solution.py:24
  68.1 5.8 %collective-permute-start.11 = (f32[1,512]{1,0:T(1,128)S(1)}, f32[1,512]{1,0:T(1,128)S(1)}, u32[]{:S(2)}, u32[]{:S(2)}) collective-permute-start(f32[1,512]{1,0:T(1,128)S(1)} %add.21), channel_id=1, source_target_pairs={{0,32},{16,48},{32,0},{48,16},{1,33},{17,49},{33,1},{49,17},{2,34}... | collective-permute-start | bytes 6152 | tf_op jit(solution)/shard_map/ppermute | solution.py:24
  74.0 8.2 %collective-permute-start.12 = (f32[1,512]{1,0:T(1,128)S(1)}, f32[1,512]{1,0:T(1,128)S(1)}, u32[]{:S(2)}, u32[]{:S(2)}) collective-permute-start(f32[1,512]{1,0:T(1,128)S(1)} %add.22), channel_id=1, source_target_pairs={{0,64},{64,0},{1,65},{65,1},{2,66},{66,2},{3,67},{67,3},{4,68},{68... | collective-permute-start | bytes 6152 | tf_op jit(solution)/shard_map/ppermute | solution.py:24
  82.2 5.6 %collective-permute-start.13 = (f32[1,512]{1,0:T(1,128)S(1)}, f32[1,512]{1,0:T(1,128)S(1)}, u32[]{:S(2)}, u32[]{:S(2)}) collective-permute-start(f32[1,512]{1,0:T(1,128)S(1)} %add.23), channel_id=1, source_target_pairs={{0,128},{128,0},{256,384},{384,256},{1,129},{129,1},{257,385},{385... | collective-permute-start | bytes 6152 | tf_op jit(solution)/shard_map/ppermute | solution.py:24
  87.8 5.6 %collective-permute-start.14 = (f32[1,512]{1,0:T(1,128)S(1)}, f32[1,512]{1,0:T(1,128)S(1)}, u32[]{:S(2)}, u32[]{:S(2)}) collective-permute-start(f32[1,512]{1,0:T(1,128)S(1)} %add.24), channel_id=1, source_target_pairs={{0,256},{128,384},{256,0},{384,128},{1,257},{129,385},{257,1},{385... | collective-permute-start | bytes 6152 | tf_op jit(solution)/shard_map/ppermute | solution.py:24
Sparse Core Ops, SparseCore 0:
  10.1 39.6 all-gather.2
  59.7 57.5 reduce-scatter.1

commit v12 on v9

--- a/solution.py
+++ b/solution.py
@@ -157,10 +157,11 @@
     near = jnp.stack([log_derivs] + [shift(log_derivs, "x", by) for by in HOPS[1:]])
     near_other = swap(near, "core", 1)
     far = jnp.stack([far] + [shift(far, "x", by) for by in HOPS[1:]])
+    left = left_halves(left)
     far, left = lax.optimization_barrier((far, left))
     far_other = swap(far, "core", 1)
 
-    total = product(left_halves(left), near, near_other, far, far_other)
+    total = product(left, near, near_other, far, far_other)
     total, log_derivs, sample_vector = lax.optimization_barrier((total, log_derivs, sample_vector))
     summed = lax.psum_scatter(total, "par", scatter_dimension=0, tiled=True)
     value = term(log_derivs, sample_vector)

time: 128 us -> 128 us (level)
  transfers between devices with their start and end apart: 17 -> 17, of which waited for: 9 -> 10; matrix products, arithmetic and copies ran while one was open for 1% -> 1% of each run, Pallas kernels for 2% -> 2%
where the time goes in v12:
time: 128 us; the launch traced here: 126 us
  starting transfers between devices  61.7 us (48%)
  waiting for transfers between devices  38.5 us (30%)
  between operations  14.3 us (11%)
  Pallas kernels  6.16 us (5%)
  local copies, waits for them, and re-layouts  4.12 us (3%)
  other arithmetic  1.69 us (1%)
    ppermute x9, starting transfers between devices, swap(): lax.ppermute(value, axis, [(i, i ^ bit) for i in range(lax.axis_size(axis...  41.8 us
    reduce_scatter x1, waiting for transfers between devices, body(): summed = lax.psum_scatter(total, 'par', scatter_dimension=0, tiled=True)  23.5 us
    ppermute x6, starting transfers between devices, shift(): lax.ppermute(value, axis, [(i, (i + by) % count) for i in range(count)])  19.8 us
    ppermute x9, waiting for transfers between devices, swap(): lax.ppermute(value, axis, [(i, i ^ bit) for i in range(lax.axis_size(axis...  10.9 us
    pallas_call x1, Pallas kernels, product(): pl.pallas_call(far_kernel, in_specs=[whole] * 5, out_specs=pl.BlockSpec(m...  3.37 us
  transfers between devices with their start and end apart: 17, of which 10 were waited for; matrix products, arithmetic and copies ran while one was open for 1% of the time, Pallas kernels for 2%

profile of v12, /device:TPU:7, one launch (start us, length us, event | category | flops | bytes accessed | tf_op | source)
XLA Modules:
  0.0 126.4 jit_solution(14621715450609772958)
XLA Ops:
  7.2 0.7 all-gather.3.cloned.1.call-update
  7.9 10.6 %collective-permute-start = (f32[128,512]{1,0:T(8,128)}, f32[128,512]{1,0:T(8,128)S(1)}, u32[]{:S(2)}, u32[]{:S(2)}) collective-permute-start(f32[128,512]{1,0:T(8,128)} %data_ref), channel_id=1, source_target_pairs={{0,64},{64,0},{1,65},{65,1},{2,66},{66,2},{3,67},{67,3},{4,68},{68... | collective-permute-start | bytes 786440 | tf_op jit(solution)/shard_map/ppermute | solution.py:24
  18.6 2.5 %collective-permute-start.5 = (f32[128,512]{1,0:T(8,128)}, f32[128,512]{1,0:T(8,128)S(1)}, u32[]{:S(2)}, u32[]{:S(2)}) collective-permute-start(f32[128,512]{1,0:T(8,128)} %data_ref), channel_id=1, source_target_pairs={{0,48},{16,0},{32,16},{48,32},{1,49},{17,1},{33,17},{49,33},{2,50}... | collective-permute-start | bytes 786440 | tf_op jit(solution)/shard_map/ppermute | solution.py:20
  21.1 4.0 %collective-permute-start.4 = (f32[128,512]{1,0:T(8,128)}, f32[128,512]{1,0:T(8,128)S(1)}, u32[]{:S(2)}, u32[]{:S(2)}) collective-permute-start(f32[128,512]{1,0:T(8,128)} %data_ref), channel_id=1, source_target_pairs={{0,16},{16,32},{32,48},{48,0},{1,17},{17,33},{33,49},{49,1},{2,18}... | collective-permute-start | bytes 786440 | tf_op jit(solution)/shard_map/ppermute | solution.py:20
  25.1 1.9 %collective-permute-start.6 = (f32[128,512]{1,0:T(8,128)}, f32[128,512]{1,0:T(8,128)S(1)}, u32[]{:S(2)}, u32[]{:S(2)}) collective-permute-start(f32[128,512]{1,0:T(8,128)} %data_ref), channel_id=1, source_target_pairs={{0,32},{16,48},{32,0},{48,16},{1,33},{17,49},{33,1},{49,17},{2,34}... | collective-permute-start | bytes 786440 | tf_op jit(solution)/shard_map/ppermute | solution.py:20
  27.0 4.9 %collective-permute-start.3 = (f32[128,512]{1,0:T(8,128)S(1)}, f32[128,512]{1,0:T(8,128)S(1)}, u32[]{:S(2)}, u32[]{:S(2)}) collective-permute-start(f32[128,512]{1,0:T(8,128)S(1)} %collective-permute-done), channel_id=1, source_target_pairs={{0,32},{16,48},{32,0},{48,16},{1,33},{17,49},{33,1},{49,17},{2,34}... | collective-permute-start | bytes 786440 | tf_op jit(solution)/shard_map/ppermute | solution.py:20
  31.9 1.9 %collective-permute-start.2 = (f32[128,512]{1,0:T(8,128)S(1)}, f32[128,512]{1,0:T(8,128)S(1)}, u32[]{:S(2)}, u32[]{:S(2)}) collective-permute-start(f32[128,512]{1,0:T(8,128)S(1)} %collective-permute-done), channel_id=1, source_target_pairs={{0,48},{16,0},{32,16},{48,32},{1,49},{17,1},{33,17},{49,33},{2,50}... | collective-permute-start | bytes 786440 | tf_op jit(solution)/shard_map/ppermute | solution.py:20
  33.9 4.6 %collective-permute-start.1 = (f32[128,512]{1,0:T(8,128)S(1)}, f32[128,512]{1,0:T(8,128)S(1)}, u32[]{:S(2)}, u32[]{:S(2)}) collective-permute-start(f32[128,512]{1,0:T(8,128)S(1)} %collective-permute-done), channel_id=1, source_target_pairs={{0,16},{16,32},{32,48},{48,0},{1,17},{17,33},{33,49},{49,1},{2,18}... | collective-permute-start | bytes 786440 | tf_op jit(solution)/shard_map/ppermute | solution.py:20
  38.5 1.0 pad_maximum_fusion.1.mine_ref
  39.5 6.8 %collective-permute-start.7 = (f32[4,128,512]{2,1,0:T(8,128)S(1)}, f32[4,128,512]{2,1,0:T(8,128)S(1)}, u32[]{:S(2)}, u32[]{:S(2)}) collective-permute-start(f32[4,128,512]{2,1,0:T(8,128)S(1)} %pad_maximum_fusion.1.mine_ref), channel_id=1, source_target_pairs={{0,8},{8,0},{1,9},{9,1},{2,10},{10,2},{3,11},{11,3},{4,12},{12,4},... | collective-permute-start | bytes 3145736 | tf_op jit(solution)/shard_map/ppermute | solution.py:24
  46.3 1.9 %collective-permute-done.2 = f32[128,512]{1,0:T(8,128)S(1)} collective-permute-done((f32[128,512]{1,0:T(8,128)S(1)}, f32[128,512]{1,0:T(8,128)S(1)}, u32[]{:S(2)}, u32[]{:S(2)}) %collective-permute-start.2) | collective-permute-done | bytes 262176 | tf_op jit(solution)/shard_map/ppermute | solution.py:20
  48.3 1.5 %all-gather.3.cloned.1.call-done = f32[512,512]{1,0:T(8,128)} async-done(((f32[128,512]{1,0:T(8,128)}), f32[512,512]{1,0:T(8,128)}) %all-gather.3.cloned.1.call-update) | async-done | bytes 1048592 | tf_op jit(solution)/shard_map/all_gather | solution.py:153
  49.8 1.2 copy-done.1
  51.4 2.6 %collective-permute-start.8 = (f32[4,128,512]{2,1,0:T(8,128)S(1)}, f32[4,128,512]{2,1,0:T(8,128)S(1)}, u32[]{:S(2)}, u32[]{:S(2)}) collective-permute-start(f32[4,128,512]{2,1,0:T(8,128)S(1)} %pad_maximum_fusion.mine_ref), channel_id=1, source_target_pairs={{0,8},{8,0},{1,9},{9,1},{2,10},{10,2},{3,11},{11,3},{4,12},{12,4},... | collective-permute-start | bytes 3145736 | tf_op jit(solution)/shard_map/ppermute | solution.py:24
  54.0 2.1 %shard_map.42.near_value = f32[4,512,256]{2,1,0:T(8,128)S(1)} custom-call(bf16[512,512]{1,0:T(8,128)(2,1)S(1)} %get-tuple-element.12.high_ref, bf16[512,512]{1,0:T(8,128)(2,1)S(1)} %get-tuple-element.13.low_ref, f32[4,128,512]{2,1,0:T(8,128)S(1)} %pad_maximum_fusion.1.mine_ref, f32[4,128,512]{2,1,0:T(8,128)S(1)} %collective-permute-done.7.other_ref), custom_call_target="tpu_custom_call" | custom-call | flops 1610612736 | bytes 4194304 | tf_op jit(solution)/shard_map/pallas_call | solution.py:132
  56.3 3.4 %shard_map.43 = f32[512,2048]{1,0:T(8,128)} custom-call(f32[4,512,256]{2,1,0:T(8,128)S(1)} %shard_map.42.near_value, bf16[512,512]{1,0:T(8,128)(2,1)S(1)} %get-tuple-element.12.high_ref, bf16[512,512]{1,0:T(8,128)(2,1)S(1)} %get-tuple-element.13.low_ref, f32[4,128,512]{2,1,0:T(8,128)S(1)} %pad_maximum_fusion.mine_ref, ...), custom_call_target="tpu_custom_call" | custom-call | flops 1610612736 | bytes 4194304 | tf_op jit(solution)/shard_map/pallas_call | solution.py:141
  59.7 0.9 copy-done
  60.8 2.3 %collective-permute-start.9 = (f32[1,512]{1,0:T(1,128)S(1)}, f32[1,512]{1,0:T(1,128)S(1)}, u32[]{:S(2)}, u32[]{:S(2)}) collective-permute-start(f32[1,512]{1,0:T(1,128)S(1)} %shard_map.44), channel_id=1, source_target_pairs={{0,8},{8,0},{1,9},{9,1},{2,10},{10,2},{3,11},{11,3},{4,12},{12,4},... | collective-permute-start | bytes 6152 | tf_op jit(solution)/shard_map/ppermute | solution.py:24
  63.1 0.8 collective-permute-done.9
  63.9 2.4 %collective-permute-start.10 = (f32[1,512]{1,0:T(1,128)S(1)}, f32[1,512]{1,0:T(1,128)S(1)}, u32[]{:S(2)}, u32[]{:S(2)}) collective-permute-start(f32[1,512]{1,0:T(1,128)S(1)} %add.20), channel_id=1, source_target_pairs={{0,16},{16,0},{32,48},{48,32},{1,17},{17,1},{33,49},{49,33},{2,18}... | collective-permute-start | bytes 6152 | tf_op jit(solution)/shard_map/ppermute | solution.py:24
  66.3 1.9 %collective-permute-done.10 = f32[1,512]{1,0:T(1,128)S(1)} collective-permute-done((f32[1,512]{1,0:T(1,128)S(1)}, f32[1,512]{1,0:T(1,128)S(1)}, u32[]{:S(2)}, u32[]{:S(2)}) %collective-permute-start.10) | collective-permute-done | bytes 2080 | tf_op jit(solution)/shard_map/ppermute | solution.py:24
  68.2 3.3 %collective-permute-start.11 = (f32[1,512]{1,0:T(1,128)S(1)}, f32[1,512]{1,0:T(1,128)S(1)}, u32[]{:S(2)}, u32[]{:S(2)}) collective-permute-start(f32[1,512]{1,0:T(1,128)S(1)} %add.21), channel_id=1, source_target_pairs={{0,32},{16,48},{32,0},{48,16},{1,33},{17,49},{33,1},{49,17},{2,34}... | collective-permute-start | bytes 6152 | tf_op jit(solution)/shard_map/ppermute | solution.py:24
  71.6 2.5 %collective-permute-done.11 = f32[1,512]{1,0:T(1,128)S(1)} collective-permute-done((f32[1,512]{1,0:T(1,128)S(1)}, f32[1,512]{1,0:T(1,128)S(1)}, u32[]{:S(2)}, u32[]{:S(2)}) %collective-permute-start.11) | collective-permute-done | bytes 2080 | tf_op jit(solution)/shard_map/ppermute | solution.py:24
  74.1 6.7 %collective-permute-start.12 = (f32[1,512]{1,0:T(1,128)S(1)}, f32[1,512]{1,0:T(1,128)S(1)}, u32[]{:S(2)}, u32[]{:S(2)}) collective-permute-start(f32[1,512]{1,0:T(1,128)S(1)} %add.22), channel_id=1, source_target_pairs={{0,64},{64,0},{1,65},{65,1},{2,66},{66,2},{3,67},{67,3},{4,68},{68... | collective-permute-start | bytes 6152 | tf_op jit(solution)/shard_map/ppermute | solution.py:24
  80.8 1.5 %collective-permute-done.12 = f32[1,512]{1,0:T(1,128)S(1)} collective-permute-done((f32[1,512]{1,0:T(1,128)S(1)}, f32[1,512]{1,0:T(1,128)S(1)}, u32[]{:S(2)}, u32[]{:S(2)}) %collective-permute-start.12) | collective-permute-done | bytes 2080 | tf_op jit(solution)/shard_map/ppermute | solution.py:24
  82.3 4.2 %collective-permute-start.13 = (f32[1,512]{1,0:T(1,128)S(1)}, f32[1,512]{1,0:T(1,128)S(1)}, u32[]{:S(2)}, u32[]{:S(2)}) collective-permute-start(f32[1,512]{1,0:T(1,128)S(1)} %add.23), channel_id=1, source_target_pairs={{0,128},{128,0},{256,384},{384,256},{1,129},{129,1},{257,385},{385... | collective-permute-start | bytes 6152 | tf_op jit(solution)/shard_map/ppermute | solution.py:24
  86.5 1.4 %collective-permute-done.13 = f32[1,512]{1,0:T(1,128)S(1)} collective-permute-done((f32[1,512]{1,0:T(1,128)S(1)}, f32[1,512]{1,0:T(1,128)S(1)}, u32[]{:S(2)}, u32[]{:S(2)}) %collective-permute-start.13) | collective-permute-done | bytes 2080 | tf_op jit(solution)/shard_map/ppermute | solution.py:24
  87.9 2.9 %collective-permute-start.14 = (f32[1,512]{1,0:T(1,128)S(1)}, f32[1,512]{1,0:T(1,128)S(1)}, u32[]{:S(2)}, u32[]{:S(2)}) collective-permute-start(f32[1,512]{1,0:T(1,128)S(1)} %add.24), channel_id=1, source_target_pairs={{0,256},{128,384},{256,0},{384,128},{1,257},{129,385},{257,1},{385... | collective-permute-start | bytes 6152 | tf_op jit(solution)/shard_map/ppermute | solution.py:24
  90.8 2.7 %collective-permute-done.14 = f32[1,512]{1,0:T(1,128)S(1)} collective-permute-done((f32[1,512]{1,0:T(1,128)S(1)}, f32[1,512]{1,0:T(1,128)S(1)}, u32[]{:S(2)}, u32[]{:S(2)}) %collective-permute-start.14) | collective-permute-done | bytes 2080 | tf_op jit(solution)/shard_map/ppermute | solution.py:24
  93.5 0.6 add.25
  94.1 23.5 %reduce-scatter.2.cloned.1.call-done = f32[64,2048]{1,0:T(8,128)} async-done(((f32[512,2048]{1,0:T(8,128)}), f32[64,2048]{1,0:T(8,128)}) %reduce-scatter.2.cloned.1.call-update) | async-done | bytes 524304 | tf_op jit(solution)/shard_map/reduce_scatter | solution.py:166
  117.6 2.0 %reshape.10 = f32[16,4,2048]{2,1,0:T(4,128)} reshape(f32[64,2048]{1,0:T(8,128)} %reduce-scatter.2.cloned.1.call-done) | data formatting | bytes 1048576 | tf_op jit(solution)/shard_map/reshape | solution.py:170
  (23 shorter events, 1.0 us)
Async XLA Ops:
  7.2 42.6 %all-gather.3.cloned.1.call-start = ((), (), s32[]{:S(2)}) async-start(), calls=%async_computation.2 | async-start | bytes 1310720 | tf_op jit(solution)/shard_map/all_gather | solution.py:153
  7.9 109.7 %reduce-scatter.2.cloned.1.call-start = ((), (), s32[]{:S(2)}) async-start(), calls=%async_computation.1 | async-start | bytes 4718592 | tf_op jit(solution)/shard_map/reduce_scatter | solution.py:166
  7.9 19.1 %collective-permute-start = (f32[128,512]{1,0:T(8,128)}, f32[128,512]{1,0:T(8,128)S(1)}, u32[]{:S(2)}, u32[]{:S(2)}) collective-permute-start(f32[128,512]{1,0:T(8,128)} %data_ref), channel_id=1, source_target_pairs={{0,64},{64,0},{1,65},{65,1},{2,66},{66,2},{3,67},{67,3},{4,68},{68... | collective-permute-start | bytes 786440 | tf_op jit(solution)/shard_map/ppermute | solution.py:24
  18.6 15.3 %collective-permute-start.5 = (f32[128,512]{1,0:T(8,128)}, f32[128,512]{1,0:T(8,128)S(1)}, u32[]{:S(2)}, u32[]{:S(2)}) collective-permute-start(f32[128,512]{1,0:T(8,128)} %data_ref), channel_id=1, source_target_pairs={{0,48},{16,0},{32,16},{48,32},{1,49},{17,1},{33,17},{49,33},{2,50}... | collective-permute-start | bytes 786440 | tf_op jit(solution)/shard_map/ppermute | solution.py:20
  21.1 17.4 %collective-permute-start.4 = (f32[128,512]{1,0:T(8,128)}, f32[128,512]{1,0:T(8,128)S(1)}, u32[]{:S(2)}, u32[]{:S(2)}) collective-permute-start(f32[128,512]{1,0:T(8,128)} %data_ref), channel_id=1, source_target_pairs={{0,16},{16,32},{32,48},{48,0},{1,17},{17,33},{33,49},{49,1},{2,18}... | collective-permute-start | bytes 786440 | tf_op jit(solution)/shard_map/ppermute | solution.py:20
  25.1 13.3 %collective-permute-start.6 = (f32[128,512]{1,0:T(8,128)}, f32[128,512]{1,0:T(8,128)S(1)}, u32[]{:S(2)}, u32[]{:S(2)}) collective-permute-start(f32[128,512]{1,0:T(8,128)} %data_ref), channel_id=1, source_target_pairs={{0,32},{16,48},{32,0},{48,16},{1,33},{17,49},{33,1},{49,17},{2,34}... | collective-permute-start | bytes 786440 | tf_op jit(solution)/shard_map/ppermute | solution.py:20
  27.0 19.3 %collective-permute-start.3 = (f32[128,512]{1,0:T(8,128)S(1)}, f32[128,512]{1,0:T(8,128)S(1)}, u32[]{:S(2)}, u32[]{:S(2)}) collective-permute-start(f32[128,512]{1,0:T(8,128)S(1)} %collective-permute-done), channel_id=1, source_target_pairs={{0,32},{16,48},{32,0},{48,16},{1,33},{17,49},{33,1},{49,17},{2,34}... | collective-permute-start | bytes 786440 | tf_op jit(solution)/shard_map/ppermute | solution.py:20
  31.9 16.3 %collective-permute-start.2 = (f32[128,512]{1,0:T(8,128)S(1)}, f32[128,512]{1,0:T(8,128)S(1)}, u32[]{:S(2)}, u32[]{:S(2)}) collective-permute-start(f32[128,512]{1,0:T(8,128)S(1)} %collective-permute-done), channel_id=1, source_target_pairs={{0,48},{16,0},{32,16},{48,32},{1,49},{17,1},{33,17},{49,33},{2,50}... | collective-permute-start | bytes 786440 | tf_op jit(solution)/shard_map/ppermute | solution.py:20
  33.9 14.4 %collective-permute-start.1 = (f32[128,512]{1,0:T(8,128)S(1)}, f32[128,512]{1,0:T(8,128)S(1)}, u32[]{:S(2)}, u32[]{:S(2)}) collective-permute-start(f32[128,512]{1,0:T(8,128)S(1)} %collective-permute-done), channel_id=1, source_target_pairs={{0,16},{16,32},{32,48},{48,0},{1,17},{17,33},{33,49},{49,1},{2,18}... | collective-permute-start | bytes 786440 | tf_op jit(solution)/shard_map/ppermute | solution.py:20
  39.5 14.5 %collective-permute-start.7 = (f32[4,128,512]{2,1,0:T(8,128)S(1)}, f32[4,128,512]{2,1,0:T(8,128)S(1)}, u32[]{:S(2)}, u32[]{:S(2)}) collective-permute-start(f32[4,128,512]{2,1,0:T(8,128)S(1)} %pad_maximum_fusion.1.mine_ref), channel_id=1, source_target_pairs={{0,8},{8,0},{1,9},{9,1},{2,10},{10,2},{3,11},{11,3},{4,12},{12,4},... | collective-permute-start | bytes 3145736 | tf_op jit(solution)/shard_map/ppermute | solution.py:24
  49.8 1.2 copy-start.1
  51.4 4.9 %collective-permute-start.8 = (f32[4,128,512]{2,1,0:T(8,128)S(1)}, f32[4,128,512]{2,1,0:T(8,128)S(1)}, u32[]{:S(2)}, u32[]{:S(2)}) collective-permute-start(f32[4,128,512]{2,1,0:T(8,128)S(1)} %pad_maximum_fusion.mine_ref), channel_id=1, source_target_pairs={{0,8},{8,0},{1,9},{9,1},{2,10},{10,2},{3,11},{11,3},{4,12},{12,4},... | collective-permute-start | bytes 3145736 | tf_op jit(solution)/shard_map/ppermute | solution.py:24
  59.6 1.0 copy-start
  59.7 0.9 copy-start.2
  60.8 3.1 %collective-permute-start.9 = (f32[1,512]{1,0:T(1,128)S(1)}, f32[1,512]{1,0:T(1,128)S(1)}, u32[]{:S(2)}, u32[]{:S(2)}) collective-permute-start(f32[1,512]{1,0:T(1,128)S(1)} %shard_map.44), channel_id=1, source_target_pairs={{0,8},{8,0},{1,9},{9,1},{2,10},{10,2},{3,11},{11,3},{4,12},{12,4},... | collective-permute-start | bytes 6152 | tf_op jit(solution)/shard_map/ppermute | solution.py:24
  63.9 4.3 %collective-permute-start.10 = (f32[1,512]{1,0:T(1,128)S(1)}, f32[1,512]{1,0:T(1,128)S(1)}, u32[]{:S(2)}, u32[]{:S(2)}) collective-permute-start(f32[1,512]{1,0:T(1,128)S(1)} %add.20), channel_id=1, source_target_pairs={{0,16},{16,0},{32,48},{48,32},{1,17},{17,1},{33,49},{49,33},{2,18}... | collective-permute-start | bytes 6152 | tf_op jit(solution)/shard_map/ppermute | solution.py:24
  68.2 5.8 %collective-permute-start.11 = (f32[1,512]{1,0:T(1,128)S(1)}, f32[1,512]{1,0:T(1,128)S(1)}, u32[]{:S(2)}, u32[]{:S(2)}) collective-permute-start(f32[1,512]{1,0:T(1,128)S(1)} %add.21), channel_id=1, source_target_pairs={{0,32},{16,48},{32,0},{48,16},{1,33},{17,49},{33,1},{49,17},{2,34}... | collective-permute-start | bytes 6152 | tf_op jit(solution)/shard_map/ppermute | solution.py:24
  74.1 8.2 %collective-permute-start.12 = (f32[1,512]{1,0:T(1,128)S(1)}, f32[1,512]{1,0:T(1,128)S(1)}, u32[]{:S(2)}, u32[]{:S(2)}) collective-permute-start(f32[1,512]{1,0:T(1,128)S(1)} %add.22), channel_id=1, source_target_pairs={{0,64},{64,0},{1,65},{65,1},{2,66},{66,2},{3,67},{67,3},{4,68},{68... | collective-permute-start | bytes 6152 | tf_op jit(solution)/shard_map/ppermute | solution.py:24
  82.3 5.6 %collective-permute-start.13 = (f32[1,512]{1,0:T(1,128)S(1)}, f32[1,512]{1,0:T(1,128)S(1)}, u32[]{:S(2)}, u32[]{:S(2)}) collective-permute-start(f32[1,512]{1,0:T(1,128)S(1)} %add.23), channel_id=1, source_target_pairs={{0,128},{128,0},{256,384},{384,256},{1,129},{129,1},{257,385},{385... | collective-permute-start | bytes 6152 | tf_op jit(solution)/shard_map/ppermute | solution.py:24
  87.9 5.6 %collective-permute-start.14 = (f32[1,512]{1,0:T(1,128)S(1)}, f32[1,512]{1,0:T(1,128)S(1)}, u32[]{:S(2)}, u32[]{:S(2)}) collective-permute-start(f32[1,512]{1,0:T(1,128)S(1)} %add.24), channel_id=1, source_target_pairs={{0,256},{128,384},{256,0},{384,128},{1,257},{129,385},{257,1},{385... | collective-permute-start | bytes 6152 | tf_op jit(solution)/shard_map/ppermute | solution.py:24
Sparse Core Ops, SparseCore 0:
  10.1 39.6 all-gather.2
  59.8 57.7 reduce-scatter.1
